TPU v7x, 256 devices: a whole 4x4x8 slice. The times are simulated.
256 devices in a mesh: view: 2 (over x_hi), frame: 32 (over z, x_lo, core), dp: 4 (over y).
Axes of the slice: x: 4 (x_hi: 2, x_lo: 2; x = x_hi * 2 + x_lo), y: 4, z: 8, core: 2. Of those that a mesh axis runs over, the one named last changes fastest.
Arguments:
- level_in: bfloat16 [8, 32, 128, 640], P('view', 'frame', 'dp'), may hold values from -6 to 6
- out_grad: bfloat16 [8, 32, 128, 640], P('view', 'frame', 'dp'), may hold values from -6 to 6
- view_qkv: bfloat16 [640, 1920], replicated, may hold values from -0.25 to 0.25
- view_out: bfloat16 [640, 640], replicated, may hold values from -0.25 to 0.25
- time_qkv: bfloat16 [640, 1920], replicated, may hold values from -0.25 to 0.25
- time_out: bfloat16 [640, 640], replicated, may hold values from -0.25 to 0.25
Outputs:
- level_out: bfloat16 [8, 32, 128, 640], P('view', 'frame', 'dp')
- level_in_grad: bfloat16 [8, 32, 128, 640], P('view', 'frame', 'dp')
- view_qkv_grad: bfloat16 [640, 1920], P(('frame', 'dp'))
- view_out_grad: bfloat16 [640, 640], P(('frame', 'dp'))
- time_qkv_grad: bfloat16 [640, 1920], P(('frame', 'dp'))
- time_out_grad: bfloat16 [640, 640], P(('frame', 'dp'))
- norm_back_sums: float32 [2, 2, 8, 32, 32], P(None, None, 'view', 'frame')
All inputs are finite; a program needn't handle non-finite values.
Results may differ from a plain program's by a relative error of at most 0.025.
Values may be sent and summed in bfloat16 or wider, within the bound.
No kernel may reach another device: no remote copies, remote signals or barrier semaphores. Data moves between devices by JAX's collectives and lax.ppermute only.
A program may use at most 128 MiB of HBM per device.

v0:
```python
import jax
import jax.numpy as jnp
from jax import lax
from jax.sharding import PartitionSpec as P

HEADS = 10
HD = 64
GROUPS = 32


EPS = 1e-05


def to_sequence(tensor, attend_dim):
    return jnp.moveaxis(tensor, attend_dim, 2).reshape(
        -1, tensor.shape[attend_dim], tensor.shape[-1]
    )


def from_sequence(flattened, attend_dim, target_shape):
    remaining = [target_shape[member] for member in range(3) if member != attend_dim]
    tensor = flattened.reshape(
        remaining[0], remaining[1], target_shape[attend_dim], flattened.shape[-1]
    )
    return jnp.moveaxis(tensor, 2, attend_dim)


def mixing(tensor, matrix):
    flattened = tensor.reshape(-1, tensor.shape[-1])
    product = jnp.dot(flattened, matrix, preferred_element_type=jnp.float32)
    return product.reshape(tensor.shape[:-1] + (matrix.shape[1],))


def project(tensor, matrix):
    return mixing(tensor, matrix).astype(jnp.bfloat16)


def project_back(tensor, matrix):
    flattened = tensor.reshape(-1, tensor.shape[-1])
    product = lax.dot_general(
        flattened, matrix, (((1,), (1,)), ((), ())), preferred_element_type=jnp.float32
    )
    return product.astype(jnp.bfloat16).reshape(tensor.shape[:-1] + (matrix.shape[0],))


def weight_grad(left_side, right_side):
    return lax.dot_general(
        left_side.reshape(-1, left_side.shape[-1]),
        right_side.reshape(-1, right_side.shape[-1]),
        (((0,), (0,)), ((), ())),
        preferred_element_type=jnp.float32,
    )


def split_heads(tensor):
    return tensor.reshape(tensor.shape[0], tensor.shape[1], HEADS, -1)


def attend(queries, key_rows, value_rows):
    scaling = HD ** (-0.5)
    scores = (
        jnp.einsum(
            "bqhe,bkhe->bhqk",
            split_heads(queries),
            split_heads(key_rows),
            preferred_element_type=jnp.float32,
        )
        * scaling
    )
    softmax_out = jax.nn.softmax(scores, axis=-1)
    combined = jnp.einsum(
        "bhqk,bkhe->bqhe",
        softmax_out.astype(jnp.bfloat16),
        split_heads(value_rows),
        preferred_element_type=jnp.float32,
    )
    return (combined.astype(jnp.bfloat16).reshape(queries.shape), softmax_out)


def attend_back(upstream, queries, key_rows, value_rows, softmax_out):
    scaling = HD ** (-0.5)
    upstream_heads = split_heads(upstream)
    dvalue = jnp.einsum(
        "bhqk,bqhe->bkhe",
        softmax_out.astype(jnp.bfloat16),
        upstream_heads,
        preferred_element_type=jnp.float32,
    )
    dprob = jnp.einsum(
        "bqhe,bkhe->bhqk",
        upstream_heads,
        split_heads(value_rows),
        preferred_element_type=jnp.float32,
    )
    dscore = softmax_out * (dprob - jnp.sum(dprob * softmax_out, axis=-1, keepdims=True))
    dscore_b = (dscore * scaling).astype(jnp.bfloat16)
    dquery = jnp.einsum(
        "bhqk,bkhe->bqhe", dscore_b, split_heads(key_rows), preferred_element_type=jnp.float32
    )
    dkey = jnp.einsum(
        "bhqk,bqhe->bkhe", dscore_b, split_heads(queries), preferred_element_type=jnp.float32
    )
    return (
        dquery.reshape(queries.shape),
        dkey.reshape(key_rows.shape),
        dvalue.reshape(value_rows.shape),
    )


def attention_pieces(packed, attend_dim, width):
    return (
        to_sequence(packed[..., :width], attend_dim),
        to_sequence(packed[..., width : 2 * width], attend_dim),
        to_sequence(packed[..., 2 * width :], attend_dim),
    )


def body(level_in, out_grad, view_qkv, view_out, time_qkv, time_out):
    width = level_in.shape[-1]
    entries = level_in.shape[2] * lax.axis_size("dp") * (width // GROUPS)

    def normalize(tensor):
        shaped = tensor.reshape(tensor.shape[:3] + (GROUPS, -1))
        totals = lax.psum(jnp.sum(shaped, axis=(2, 4), keepdims=True), "dp")
        centred = shaped - totals / entries
        spread = lax.psum(jnp.sum(centred * centred, axis=(2, 4), keepdims=True), "dp")
        variance = spread / entries
        inverse = lax.rsqrt(variance + EPS)
        return ((centred * inverse).reshape(tensor.shape), inverse)

    def normalize_back(upstream, normed, inverse):
        shaped = upstream.reshape(upstream.shape[:3] + (GROUPS, -1))
        normed_shaped = normed.reshape(shaped.shape)
        first_sum, second_sum = lax.psum(
            (
                jnp.sum(shaped, axis=(2, 4), keepdims=True),
                jnp.sum(shaped * normed_shaped, axis=(2, 4), keepdims=True),
            ),
            "dp",
        )
        result = inverse * (shaped - first_sum / entries - normed_shaped * (second_sum / entries))
        sums = jnp.stack(
            [
                first_sum.reshape(shaped.shape[:2] + (GROUPS,)),
                second_sum.reshape(shaped.shape[:2] + (GROUPS,)),
            ]
        )
        return (result.reshape(upstream.shape), sums)

    source = level_in.astype(jnp.float32)
    normed_one, inverse_one = normalize(source)
    hidden_one = normed_one.astype(jnp.bfloat16)
    packed_one = project(hidden_one, view_qkv)
    query_one = to_sequence(packed_one[..., :width], 0)
    gathered = lax.all_gather(packed_one[..., width:], "view", axis=0, tiled=True)
    key_one = to_sequence(gathered[..., :width], 0)
    value_one = to_sequence(gathered[..., width:], 0)
    attn_one, soft_one = attend(query_one, key_one, value_one)
    mixed_one = from_sequence(attn_one, 0, level_in.shape)
    stream = source + mixing(mixed_one, view_out)
    normed_two, inverse_two = normalize(stream)
    hidden_two = normed_two.astype(jnp.bfloat16)
    packed_two = lax.all_to_all(
        project(hidden_two, time_qkv), "frame", split_axis=2, concat_axis=1, tiled=True
    )
    moved_shape = packed_two.shape
    query_two, key_two, value_two = attention_pieces(packed_two, 1, width)
    attn_two, soft_two = attend(query_two, key_two, value_two)
    mixed_moved = from_sequence(attn_two, 1, moved_shape)
    mixed_two = lax.all_to_all(mixed_moved, "frame", split_axis=1, concat_axis=2, tiled=True)
    temporal = project(mixed_two, time_out)
    level_out = (stream + temporal.astype(jnp.float32)).astype(jnp.bfloat16)
    grad_mixed_two = project_back(out_grad, time_out)
    time_out_total = weight_grad(mixed_two, out_grad)
    grad_moved = lax.all_to_all(grad_mixed_two, "frame", split_axis=2, concat_axis=1, tiled=True)
    dquery_two, dkey_two, dvalue_two = attend_back(
        to_sequence(grad_moved, 1), query_two, key_two, value_two, soft_two
    )
    packed_grad_moved = jnp.concatenate(
        [from_sequence(member, 1, moved_shape) for member in (dquery_two, dkey_two, dvalue_two)],
        axis=-1,
    ).astype(jnp.bfloat16)
    packed_grad_two = lax.all_to_all(
        packed_grad_moved, "frame", split_axis=1, concat_axis=2, tiled=True
    )
    time_qkv_total = weight_grad(hidden_two, packed_grad_two)
    grad_hidden_two = project_back(packed_grad_two, time_qkv)
    back_two, sums_two = normalize_back(
        grad_hidden_two.astype(jnp.float32), normed_two, inverse_two
    )
    grad_stream = out_grad.astype(jnp.float32) + back_two
    grad_stream_b = grad_stream.astype(jnp.bfloat16)
    grad_mixed_one = project_back(grad_stream_b, view_out)
    view_out_total = weight_grad(mixed_one, grad_stream_b)
    dquery_one, dkey_one, dvalue_one = attend_back(
        to_sequence(grad_mixed_one, 0), query_one, key_one, value_one, soft_one
    )
    pair_grads = jnp.concatenate(
        [from_sequence(dkey_one, 0, gathered.shape), from_sequence(dvalue_one, 0, gathered.shape)],
        axis=-1,
    )
    pair_local = lax.psum_scatter(
        pair_grads.astype(jnp.bfloat16), "view", scatter_dimension=0, tiled=True
    ).astype(jnp.float32)
    packed_grad_one = jnp.concatenate(
        [from_sequence(dquery_one, 0, level_in.shape), pair_local], axis=-1
    ).astype(jnp.bfloat16)
    view_qkv_total = weight_grad(hidden_one, packed_grad_one)
    grad_hidden_one = project_back(packed_grad_one, view_qkv)
    back_one, sums_one = normalize_back(
        grad_hidden_one.astype(jnp.float32), normed_one, inverse_one
    )
    level_in_grad = (grad_stream + back_one).astype(jnp.bfloat16)
    norm_back_sums = jnp.stack([sums_one, sums_two])
    share_vq, share_vo, share_tq, share_to = (
        lax.psum_scatter(view_qkv_total, ("frame", "dp"), scatter_dimension=0, tiled=True),
        lax.psum_scatter(view_out_total, ("frame", "dp"), scatter_dimension=0, tiled=True),
        lax.psum_scatter(time_qkv_total, ("frame", "dp"), scatter_dimension=0, tiled=True),
        lax.psum_scatter(time_out_total, ("frame", "dp"), scatter_dimension=0, tiled=True),
    )
    total_vq, total_vo, total_tq, total_to = (
        lax.psum(share_vq.astype(jnp.bfloat16), "view").astype(jnp.float32),
        lax.psum(share_vo.astype(jnp.bfloat16), "view").astype(jnp.float32),
        lax.psum(share_tq.astype(jnp.bfloat16), "view").astype(jnp.float32),
        lax.psum(share_to.astype(jnp.bfloat16), "view").astype(jnp.float32),
    )
    return (
        level_out,
        level_in_grad,
        total_vq.astype(jnp.bfloat16),
        total_vo.astype(jnp.bfloat16),
        total_tq.astype(jnp.bfloat16),
        total_to.astype(jnp.bfloat16),
        norm_back_sums,
    )


def solution(mesh):
    return jax.shard_map(
        body,
        mesh=mesh,
        in_specs=(
            P("view", "frame", "dp", None),
            P("view", "frame", "dp", None),
            P(),
            P(),
            P(),
            P(),
        ),
        out_specs=(
            P("view", "frame", "dp", None),
            P("view", "frame", "dp", None),
            P(("frame", "dp"), None),
            P(("frame", "dp"), None),
            P(("frame", "dp"), None),
            P(("frame", "dp"), None),
            P(None, None, "view", "frame", None),
        ),
        check_vma=False,
    )
```

profile of v0, /device:TPU:1, one launch (start us, length us, event | category | flops | bytes accessed | tf_op | source)
XLA Modules:
  0.0 955.8 jit_solution(6951037837723114522)
XLA Ops:
  7.2 1.8 convolution_convert_fusion.11
  9.7 11.1 %all-to-all-start.2 = ((bf16[4,1,32,640]{3,0,1,2:T(4,128)(2,1)}), bf16[4,1,32,640]{3,0,1,2:T(4,128)(2,1)}, u32[]{:S(2)}, u32[]{:S(2)}) async-start(bf16[4,1,32,640]{3,0,1,2:T(4,128)(2,1)} %copy.159), calls=%async_computation.2 | async-start | bytes 327680 | tf_op jit(solution)/shard_map/all_to_all | solution.py:175
  21.1 9.5 psum.84
  31.1 6.0 psum.85
  37.3 2.3 fusion.17
  39.7 8.1 all_gather.3
  47.9 1.5 reshape.446
  49.4 1.5 reshape.447
  52.0 3.2 fusion.140
  56.0 2.1 fusion.38
  59.2 1.6 fusion.141
  61.0 7.4 psum.86
  68.9 6.0 psum.87
  77.5 16.7 %all-to-all-start = ((bf16[4,1,32,1920]{3,0,1,2:T(4,128)(2,1)}), bf16[4,1,32,1920]{3,0,1,2:T(4,128)(2,1)S(1)}, u32[]{:S(2)}, u32[]{:S(2)}) async-start(bf16[4,1,32,1920]{3,0,1,2:T(4,128)(2,1)} %copy.147), calls=%async_computation | async-start | bytes 983040 | tf_op jit(solution)/shard_map/all_to_all | solution.py:163
  94.2 2.0 reshape.451
  96.2 13.8 %all-to-all-done = bf16[4,1,32,1920]{3,0,1,2:T(4,128)(2,1)S(1)} async-done(((bf16[4,1,32,1920]{3,0,1,2:T(4,128)(2,1)}), bf16[4,1,32,1920]{3,0,1,2:T(4,128)(2,1)S(1)}, u32[]{:S(2)}, u32[]{:S(2)}) %all-to-all-start) | async-done | bytes 491552 | tf_op jit(solution)/shard_map/all_to_all | solution.py:163
  111.0 2.0 reshape.448
  113.0 1.2 reshape.450
  114.2 2.2 reshape.449
  116.4 3.1 fusion.142
  119.5 3.0 fusion.34
  122.5 2.8 fusion.37
  125.3 2.4 fusion.74
  127.8 1.1 copy.202
  129.8 5.8 all-to-all-start.1
  135.6 3.2 fusion.36
  138.8 3.0 fusion.35
  150.3 8.4 all-to-all-start.3
  158.8 1.5 copy.203
  162.5 2.5 copy.206
  166.2 1.6 copy.157
  167.8 6.8 all-to-all-done.3
  177.2 2.6 reshape.429
  179.8 2.7 fusion.138
  182.7 7.9 all-reduce.6
  195.0 2.2 convolution_convert_fusion.9
  197.1 2.0 reshape_reshape.33
  199.2 2.4 fusion.25
  201.6 1.5 fusion.66
  203.1 1.1 copy.205
  204.3 2.4 reshape.441
  206.7 17.4 %fusion.24 = bf16[32,8,10,64]{3,1,2,0:T(8,128)(2,1)} fusion(f32[32,10,4,8]{3,2,1,0:T(4,128)} %fusion.66, bf16[32,4,10,64]{3,2,0,1:T(8,128)(2,1)} %reshape_reshape.30, f32[32,10,4,8]{3,2,1,0:T(4,128)} %get-tuple-element.57, f32[32,10,4]{2,1,0:T(8,128)} %copy-done.22), kind=kOutput, calls=%fused_computation.24 | convolution fusion | flops 1547527 | bytes 578560 | tf_op jit(solution)/shard_map/bhqk,bqhe->bkhe/dot_general | solution.py:100
  224.1 2.2 copy.204
  226.3 2.7 reshape.440
  229.0 2.0 pad_maximum_fusion
  231.0 2.6 fusion.152
  233.6 1.9 fusion.47
  235.5 17.1 %fusion.39 = bf16[32,4,10,64]{3,1,2,0:T(4,128)(2,1)} fusion(f32[32,10,4,8]{3,2,1,0:T(4,128)} %fusion.66, bf16[32,8,10,64]{3,2,0,1:T(8,128)(2,1)} %reshape.447, f32[32,10,4,8]{3,2,1,0:T(4,128)} %get-tuple-element.57, f32[32,10,4]{2,1,0:T(8,128)} %copy-done.22), kind=kOutput, calls=%fused_computation.45 | convolution fusion | flops 1465607 | bytes 578560 | tf_op jit(solution)/shard_map/bhqk,bkhe->bqhe/dot_general | solution.py:97
  252.5 1.9 copy.181
  254.4 2.0 reshape.432
  256.4 2.6 convolution_bitcast_fusion.1
  259.1 3.0 fusion.151
  262.7 3.5 fusion.41
  266.2 1.9 copy.188
  268.1 2.6 reshape.431
  270.7 2.7 fusion.137
  273.5 6.6 all-reduce.5
  283.0 4.1 convolution_bitcast_fusion
  287.1 642.6 %all-reduce.9 = (bf16[640,1920]{1,0:T(8,128)(2,1)}, bf16[640,640]{1,0:T(8,128)(2,1)}, bf16[640,1920]{1,0:T(8,128)(2,1)}, bf16[640,640]{1,0:T(8,128)(2,1)}) all-reduce(f32[640,1920]{1,0:T(8,128)} %convolution_bitcast_fusion, ...), channel_id=3, replica_groups=mesh['view'=2,'frame'=32,'dp'=4] {'frame','dp'}, use_global_device_ids=true, to_apply=%region_27.0.clone | all-reduce | flops 3276800 | bytes 19660800
  930.5 1.3 dynamic-slice_convert_fusion.3
  932.7 1.3 dynamic-slice_convert_fusion.2
  934.7 1.3 pad_maximum_fusion.2
  936.0 1.9 fusion.83
  937.9 10.7 %all-reduce.7 = (bf16[5,1920]{1,0:T(8,128)(2,1)}, bf16[5,640]{1,0:T(8,128)(2,1)}, bf16[5,1920]{1,0:T(8,128)(2,1)}, bf16[5,640]{1,0:T(8,128)(2,1)}) all-reduce(bf16[5,1920]{1,0:T(8,128)(2,1)S(1)} %dynamic-slice_convert_fusion.1, bf16[5,640]{1,0:T(8,128)(2,1)} %dynamic-slice_convert_fusion.3, ...), channel_id=1, replica_groups=mesh['view'=2,'frame'=32,'dp'=4] {'view'}, use_global_device_ids=true, to_apply=%region_28.0 | all-reduce | flops 25600 | bytes 102400 | tf_op jit(solution)/shard_map/psum | solution.py:222
  (123 shorter events, 34.2 us)
Async XLA Ops:
  7.2 68.7 %copy-start = (bf16[640,1920]{1,0:T(8,128)(2,1)S(1)}, bf16[640,1920]{1,0:T(8,128)(2,1)}, u32[]{:S(2)}) copy-start(bf16[640,1920]{1,0:T(8,128)(2,1)} %param.10) | copy-start | bytes 7372804
  7.2 13.6 %copy-start.1 = (bf16[4,1,32,640]{3,2,1,0:T(8,128)(2,1)S(1)}, bf16[4,1,32,640]{3,2,1,0:T(8,128)(2,1)}, u32[]{:S(2)}) copy-start(bf16[4,1,32,640]{3,2,1,0:T(8,128)(2,1)} %param.6) | copy-start | bytes 491524
  9.7 67.8 %all-to-all-start.2 = ((bf16[4,1,32,640]{3,0,1,2:T(4,128)(2,1)}), bf16[4,1,32,640]{3,0,1,2:T(4,128)(2,1)}, u32[]{:S(2)}, u32[]{:S(2)}) async-start(bf16[4,1,32,640]{3,0,1,2:T(4,128)(2,1)} %copy.159), calls=%async_computation.2 | async-start | bytes 327680 | tf_op jit(solution)/shard_map/all_to_all | solution.py:175
  55.3 0.7 copy-start.22
  75.2 0.7 copy-start.7
  77.5 32.5 %all-to-all-start = ((bf16[4,1,32,1920]{3,0,1,2:T(4,128)(2,1)}), bf16[4,1,32,1920]{3,0,1,2:T(4,128)(2,1)S(1)}, u32[]{:S(2)}, u32[]{:S(2)}) async-start(bf16[4,1,32,1920]{3,0,1,2:T(4,128)(2,1)} %copy.147), calls=%async_computation | async-start | bytes 983040 | tf_op jit(solution)/shard_map/all_to_all | solution.py:163
  114.2 5.3 copy-start.12
  119.5 3.0 copy-start.9
  129.8 20.4 %all-to-all-start.1 = ((bf16[4,32,1,640]{3,0,2,1:T(4,128)(2,1)}), bf16[4,32,1,640]{3,0,2,1:T(4,128)(2,1)}, u32[]{:S(2)}, u32[]{:S(2)}) async-start(bf16[4,32,1,640]{3,0,2,1:T(4,128)(2,1)} %reshape.439), calls=%async_computation.1 | async-start | bytes 327680 | tf_op jit(solution)/shard_map/all_to_all | solution.py:170
  135.6 3.2 copy-start.13
  150.3 24.3 %all-to-all-start.3 = ((bf16[4,32,1,1920]{3,0,2,1:T(4,128)(2,1)}), bf16[4,32,1,1920]{3,0,2,1:T(4,128)(2,1)S(1)}, u32[]{:S(2)}, u32[]{:S(2)}) async-start(bf16[4,32,1,1920]{3,0,2,1:T(4,128)(2,1)} %copy.170), calls=%async_computation.3 | async-start | bytes 983040 | tf_op jit(solution)/shard_map/all_to_all | solution.py:183
  158.7 104.1 %reduce-scatter.2.cloned.1.call-start = ((), (), s32[]{:S(2)}) async-start(), calls=%async_computation.5 | async-start | bytes 983040 | tf_op jit(solution)/shard_map/reduce_scatter | solution.py:202
  158.8 6.2 copy-start.21
  174.7 0.8 copy-start.2
  179.8 13.7 %copy-start.6 = (bf16[4,1,32,640]{3,2,1,0:T(8,128)(2,1)S(1)}, bf16[4,1,32,640]{3,2,1,0:T(8,128)(2,1)}, u32[]{:S(2)}) copy-start(bf16[4,1,32,640]{3,2,1,0:T(8,128)(2,1)} %param.7) | copy-start | bytes 491524
  190.6 0.6 copy-start.17
  190.6 0.6 copy-start.19
  194.3 0.7 copy-start.11
  199.2 2.4 copy-start.5
  199.2 2.4 copy-start.10
  231.0 2.6 copy-start.4
  256.4 2.6 copy-start.3
  256.4 2.6 copy-start.8
  259.1 3.1 copy-start.18
  259.1 3.0 copy-start.20
  266.2 4.5 copy-start.14
  266.2 4.5 copy-start.15
  280.1 0.6 copy-start.16
Sparse Core Ops, SparseCore 0:
  231.1 19.7 reduce-scatter.1
where the time goes:
time: 970 us; the launch traced here: 956 us
  blocking collectives  705 us (73%)
  matrix products  88.1 us (9%)
  local copies, waits for them, and re-layouts  68.3 us (7%)
  starting transfers between devices  42 us (4%)
  waiting for transfers between devices  20.7 us (2%)
  other arithmetic  16.4 us (2%)
  between operations  15.5 us (2%)
    unnamed x1, blocking collectives  643 us
    dot_general x2, matrix products, attend_back(): jnp.einsum('bhqk,bqhe->bkhe', dscore_b, split_heads(queries), preferred_e...  20.5 us
    dot_general x2, matrix products, attend_back(): jnp.einsum('bhqk,bkhe->bqhe', dscore_b, split_heads(key_rows), preferred_...  20.1 us
  transfers between devices with their start and end apart: 5, of which 2 were waited for; matrix products, arithmetic and copies ran while one was open for 8% of the time, Pallas kernels for 0%

commit v1 on v0

v1 whole, which is shorter than its diff:
```python
import functools

import jax
import jax.numpy as jnp
from jax import lax
from jax.experimental import pallas as pl
from jax.experimental.pallas import tpu as pltpu
from jax.sharding import Mesh, PartitionSpec as P

HEADS = 10
HD = 64
GROUPS = 32
EPS = 1e-05
D = 640
CH = D // GROUPS
VIEWS = 8
PX = 16
T = VIEWS * PX
HALF = T // 2
SCALE = HD ** (-0.5)
F32 = jnp.float32
BF16 = jnp.bfloat16


def group_matrix():
    row = lax.broadcasted_iota(jnp.int32, (D, 128), 0)
    low = lax.broadcasted_iota(jnp.int32, (D, 128), 1) * CH
    return ((row >= low) & (row < low + CH)).astype(F32)


def to_groups(rows, member):
    return jnp.dot(rows, member, precision=lax.Precision.HIGHEST, preferred_element_type=F32)


def to_channels(groups, member):
    return lax.dot_general(
        groups, member, (((1,), (1,)), ((), ())), precision=lax.Precision.HIGHEST, preferred_element_type=F32
    )


def view_sum(tokens):
    return jnp.sum(tokens.reshape(tokens.shape[0] // PX, PX, D), axis=1)


def per_token(rows):
    return jnp.broadcast_to(rows[:, None, :], (rows.shape[0], PX, D)).reshape(rows.shape[0] * PX, D)


def partial_stats(tokens, member):
    mean = to_groups(view_sum(tokens), member) * (1.0 / (PX * CH))
    centred = tokens - per_token(to_channels(mean, member))
    return mean, to_groups(view_sum(centred * centred), member)


def merge_stats(means, spreads, entries):
    count = len(means)
    mean = sum(means) * (1.0 / count)
    spread = sum(spreads)
    for other in means:
        gap = other - mean
        spread = spread + gap * gap * float(PX * CH)
    return mean, lax.rsqrt(spread * (1.0 / entries) + EPS)


def spread_out(ref, top, bottom):
    both = jnp.concatenate([top, bottom], axis=0)
    ref[...] = jnp.broadcast_to(both[None], ref.shape)


def mm(left, right):
    return jnp.dot(left, right, preferred_element_type=F32)


def mm_t(left, right):
    return lax.dot_general(left, right, (((1,), (1,)), ((), ())), preferred_element_type=F32)


def t_mm(left, right):
    return lax.dot_general(left, right, (((0,), (0,)), ((), ())), preferred_element_type=F32)


def lane_low(rows):
    return lax.broadcasted_iota(jnp.int32, (rows, 128), 1) < HD


def both_heads(pair):
    low = lane_low(pair.shape[0])
    zero = jnp.zeros_like(pair)
    return jnp.concatenate([jnp.where(low, pair, zero), jnp.where(low, zero, pair)], axis=0)


def join_heads(stacked):
    return jnp.where(lane_low(T), stacked[:T], stacked[T:])


def same_sequence(period):
    row = lax.broadcasted_iota(jnp.int32, (2 * T, T), 0)
    col = lax.broadcasted_iota(jnp.int32, (2 * T, T), 1)
    return ((row ^ col) & (period - 1)) == 0


def softmax_pair(stacked_q, keys, allowed):
    scores = jnp.where(allowed, mm_t(stacked_q, keys) * SCALE, -1e30)
    top = jnp.max(scores, axis=-1, keepdims=True)
    weights = jnp.exp(scores - top)
    return weights / jnp.sum(weights, axis=-1, keepdims=True)


def pair_of(index):
    return slice(index * 128, (index + 1) * 128)


def attend(packed, allowed):
    outs = []
    for pair in range(HEADS // 2):
        q = both_heads(packed[:, pair_of(pair)])
        k = packed[:, pair_of(pair + 5)]
        v = packed[:, pair_of(pair + 10)]
        prob = softmax_pair(q, k, allowed).astype(BF16)
        outs.append(join_heads(mm(prob, v)).astype(BF16))
    return jnp.concatenate(outs, axis=1)


def attend_back(grad, packed, allowed):
    dqs, dks, dvs = [], [], []
    for pair in range(HEADS // 2):
        q = both_heads(packed[:, pair_of(pair)])
        k = packed[:, pair_of(pair + 5)]
        v = packed[:, pair_of(pair + 10)]
        g = both_heads(grad[:, pair_of(pair)])
        prob = softmax_pair(q, k, allowed)
        dvs.append(t_mm(prob.astype(BF16), g).astype(BF16))
        dprob = mm_t(g, v)
        dscore = prob * (dprob - jnp.sum(dprob * prob, axis=-1, keepdims=True))
        dscore = (dscore * SCALE).astype(BF16)
        dqs.append(join_heads(mm(dscore, k)).astype(BF16))
        dks.append(t_mm(dscore, q).astype(BF16))
    return jnp.concatenate(dqs + dks + dvs, axis=1)


def k_split(place, x_ref, og_ref, xkeep_ref, ogkeep_ref, send_ref, stats_ref):
    first = place[0] == 0
    member = group_matrix()

    def halves(ref):
        low = ref[:, 0:PX, :].reshape(HALF, D)
        high = ref[:, PX : 2 * PX, :].reshape(HALF, D)
        return jnp.where(first, low, high), jnp.where(first, high, low)

    xkeep, xsend = halves(x_ref)
    ogkeep, ogsend = halves(og_ref)
    xkeep_ref[...] = xkeep
    ogkeep_ref[...] = ogkeep
    send_ref[:, :D] = xsend
    send_ref[:, D:] = ogsend
    tokens = jnp.concatenate([xkeep, xsend], axis=0).astype(F32)
    spread_out(stats_ref, *partial_stats(tokens, member))


def k_view(entries, place, xkeep_ref, ogkeep_ref, recv_ref, g_ref, wqkv_ref, wout_ref,
           stream_ref, packed_ref, mixed_ref, normed_ref, og_ref, own_ref, stats_ref):
    first = place[0] == 0
    member = group_matrix()
    sources = g_ref.shape[0]
    half = VIEWS // 2

    def side(low):
        chosen = range(low, low + sources // 2)
        means = [g_ref[s, a * half : (a + 1) * half, :] for s in chosen for a in range(2)]
        spreads = [g_ref[s, VIEWS + a * half : VIEWS + (a + 1) * half, :] for s in chosen for a in range(2)]
        return merge_stats(means, spreads, entries)

    low, high = side(0), side(sources // 2)
    mean = jnp.concatenate([low[0], high[0]], axis=0)
    inverse = jnp.concatenate([low[1], high[1]], axis=0)
    own_ref[0:VIEWS, :] = mean
    own_ref[VIEWS:, :] = inverse

    def ordered(mine, theirs):
        return jnp.concatenate([jnp.where(first, mine, theirs), jnp.where(first, theirs, mine)], axis=0)

    og_ref[...] = ordered(ogkeep_ref[...], recv_ref[:, D:])
    x = ordered(xkeep_ref[...], recv_ref[:, :D]).astype(F32)
    normed = (x - per_token(to_channels(mean, member))) * per_token(to_channels(inverse, member))
    normed_ref[...] = normed
    packed = mm(normed.astype(BF16), wqkv_ref[...]).astype(BF16)
    packed_ref[...] = packed
    mixed = attend(packed, same_sequence(PX))
    mixed_ref[...] = mixed
    stream = x + mm(mixed, wout_ref[...])
    stream_ref[...] = stream
    spread_out(stats_ref, *partial_stats(stream, member))


def k_norm_two(entries, stream_ref, og_ref, g_ref, send_ref, normed_ref, inverse_ref):
    member = group_matrix()
    sources = range(g_ref.shape[0])
    mean, inverse = merge_stats(
        [g_ref[s, 0:VIEWS, :] for s in sources], [g_ref[s, VIEWS:, :] for s in sources], entries
    )
    inverse_ref[...] = inverse
    normed = (stream_ref[...] - per_token(to_channels(mean, member))) * per_token(to_channels(inverse, member))
    normed_ref[...] = normed
    shape = send_ref.shape[:2] + (D,)
    send_ref[:, :, :D] = normed.astype(BF16).reshape(shape)
    send_ref[:, :, D:] = og_ref[...].reshape(shape)


def weight_sides(core, hidden, mixed, packed_grad, grad, keep_ref, give_ref):
    first = core == 0
    quarter = packed_grad[:, :D], packed_grad[:, D : 2 * D], packed_grad[:, 2 * D :], grad
    keep_ref[:, :D] = hidden
    give_ref[:, :D] = hidden
    keep_ref[:, D : 2 * D] = jnp.where(first, hidden, mixed)
    give_ref[:, D : 2 * D] = jnp.where(first, mixed, hidden)
    for slot in range(2):
        cols = slice((2 + slot) * D, (3 + slot) * D)
        keep_ref[:, cols] = jnp.where(first, quarter[slot], quarter[2 + slot])
        give_ref[:, cols] = jnp.where(first, quarter[2 + slot], quarter[slot])


def k_time(place, recv_ref, wqkv_ref, wout_ref, back_ref, keep_ref, give_ref):
    hidden = recv_ref[:, :, :D].reshape(T, D)
    grad = recv_ref[:, :, D:].reshape(T, D)
    allowed = same_sequence(recv_ref.shape[1])
    packed = mm(hidden, wqkv_ref[...]).astype(BF16)
    mixed = attend(packed, allowed)
    shape = back_ref.shape[:2] + (D,)
    back_ref[:, :, :D] = mm(mixed, wout_ref[...]).astype(BF16).reshape(shape)
    packed_grad = attend_back(mm_t(grad, wout_ref[...]).astype(BF16), packed, allowed)
    back_ref[:, :, D:] = mm_t(packed_grad, wqkv_ref[...]).astype(BF16).reshape(shape)
    weight_sides(place[1], hidden, mixed, packed_grad, grad, keep_ref, give_ref)


def k_level_out(place, back_ref, stream_ref, normed_ref, keep_ref, send_ref, ghid_ref, stats_ref):
    first = place[0] == 0
    member = group_matrix()
    temporal = back_ref[:, :, :D].reshape(T, D)
    ghid = back_ref[:, :, D:].reshape(T, D)
    ghid_ref[...] = ghid
    out = (stream_ref[...] + temporal.astype(F32)).astype(BF16)
    keep_ref[...] = jnp.where(first, out[:HALF], out[HALF:])
    send_ref[...] = jnp.where(first, out[HALF:], out[:HALF])
    grad = ghid.astype(F32)
    spread_out(
        stats_ref,
        to_groups(view_sum(grad), member),
        to_groups(view_sum(grad * normed_ref[...]), member),
    )


def k_view_back(entries, place, ghid_ref, ntwo_ref, itwo_ref, g_ref, og_ref, packed_ref, mixed_ref,
                none_ref, own_ref, wqkv_ref, wout_ref,
                ukeep_ref, usend_ref, keep_ref, give_ref, sums_ref, stats_ref):
    first = place[0] == 0
    member = group_matrix()
    sums = g_ref[0]
    for s in range(1, g_ref.shape[0]):
        sums = sums + g_ref[s]
    sums_ref[...] = sums
    m1 = per_token(to_channels(sums[:VIEWS] * (1.0 / entries), member))
    m2 = per_token(to_channels(sums[VIEWS:] * (1.0 / entries), member))
    inverse = per_token(to_channels(itwo_ref[...], member))
    grad_stream = og_ref[...].astype(F32) + inverse * (ghid_ref[...].astype(F32) - m1 - ntwo_ref[...] * m2)
    grad_b = grad_stream.astype(BF16)
    packed = packed_ref[...]
    packed_grad = attend_back(mm_t(grad_b, wout_ref[...]).astype(BF16), packed, same_sequence(PX))
    normed = none_ref[...]
    weight_sides(place[1], normed.astype(BF16), mixed_ref[...], packed_grad, grad_b, keep_ref, give_ref)
    grad = mm_t(packed_grad, wqkv_ref[...]).astype(BF16).astype(F32)
    spread_out(stats_ref, to_groups(view_sum(grad), member), to_groups(view_sum(grad * normed), member))
    partly = grad_stream + per_token(to_channels(own_ref[VIEWS:, :], member)) * grad
    ukeep_ref[...] = jnp.where(first, partly[:HALF], partly[HALF:])
    usend_ref[...] = jnp.where(first, partly[HALF:], partly[:HALF]).astype(BF16)


def k_finish(entries, place, g_ref, sumstwo_ref, own_ref, xkeep_ref, send_ref, ukeep_ref, urecv_ref,
             okeep_ref, orecv_ref, out_ref, grad_ref, sums_ref):
    first = place[0] == 0
    member = group_matrix()
    half = VIEWS // 2
    sums = g_ref[0]
    for s in range(1, g_ref.shape[0]):
        sums = sums + g_ref[s]

    def mine(rows):
        return jnp.where(first, rows[:half], rows[half:])

    s1, s2 = mine(sums[:VIEWS]), mine(sums[VIEWS:])
    sums_ref[0] = s1
    sums_ref[1] = s2
    sums_ref[2] = mine(sumstwo_ref[0:VIEWS, :])
    sums_ref[3] = mine(sumstwo_ref[VIEWS:, :])
    inverse = mine(own_ref[VIEWS:, :])
    mean_c = per_token(to_channels(mine(own_ref[0:VIEWS, :]), member))
    inverse_c = per_token(to_channels(inverse, member))
    a = per_token(to_channels(inverse * s1 * (1.0 / entries), member))
    b = per_token(to_channels(inverse * s2 * (1.0 / entries), member))

    def finished(part, x):
        normed = (x.astype(F32) - mean_c) * inverse_c
        return (part.astype(F32) - a - normed * b).astype(BF16)

    keep = finished(ukeep_ref[...], xkeep_ref[...])
    other = finished(urecv_ref[...], send_ref[:, :D])
    shape = (half, PX, D)
    grad_ref[:, 0:PX, :] = jnp.where(first, keep, other).reshape(shape)
    grad_ref[:, PX:, :] = jnp.where(first, other, keep).reshape(shape)
    okeep, orecv = okeep_ref[...], orecv_ref[...]
    out_ref[:, 0:PX, :] = jnp.where(first, okeep, orecv).reshape(shape)
    out_ref[:, PX:, :] = jnp.where(first, orecv, okeep).reshape(shape)


def k_weights(order_ref, keep_ref, recv_ref, out_ref):
    for unit in range(2):
        left = jnp.concatenate([keep_ref[:, unit * D : (unit + 1) * D], recv_ref[:, unit * D : (unit + 1) * D]], axis=0)
        cols = slice((2 + unit) * D, (3 + unit) * D)
        right = jnp.concatenate([keep_ref[:, cols], recv_ref[:, cols]], axis=0)
        left = mm(left, order_ref[...]).astype(BF16)
        out_ref[:, unit * D : (unit + 1) * D] = t_mm(left, right).astype(BF16)


def k_sum(parts_ref, out_ref):
    total = parts_ref[0].astype(F32)
    for s in range(1, parts_ref.shape[0]):
        total = total + parts_ref[s].astype(F32)
    total = total.astype(BF16)
    if len(out_ref.shape) == 2:
        out_ref[...] = total
    else:
        rows = out_ref.shape[1]
        for s in range(out_ref.shape[0]):
            out_ref[s] = total[s * rows : (s + 1) * rows]


def call(kernel, outs, *args, place=None):
    vmem = pl.BlockSpec(memory_space=pltpu.VMEM)
    specs = [vmem] * len(args)
    if place is not None:
        specs = [pl.BlockSpec(memory_space=pltpu.SMEM)] + specs
        args = (place,) + args
    return pl.pallas_call(
        kernel,
        out_shape=[jax.ShapeDtypeStruct(shape, dtype) for shape, dtype in outs],
        in_specs=specs,
        out_specs=[vmem] * len(outs),
        compiler_params=pltpu.CompilerParams(vmem_limit_bytes=40 * 1024 * 1024),
    )(*args)


def row_order(z, xl, core, dp):
    rows = D // (z * xl * core * dp)
    place = jnp.arange(D).reshape(z, xl, core, dp, rows).transpose(3, 0, 1, 2, 4).reshape(-1)
    return (jnp.arange(D)[:, None] == place[None, :]).astype(BF16)


def body(sizes, level_in, out_grad, view_qkv, view_out, time_qkv, time_out):
    z, xl, core, dp = sizes
    frames = z * xl * core
    entries = float(dp * 2 * PX * CH)
    frame_axes = ("z", "xl", "core")
    mates = ("view", "dp")
    group = 2 * dp
    place = jnp.stack([lax.axis_index("view"), lax.axis_index("core")]).astype(jnp.int32)
    order = row_order(z, xl, core, dp)
    stats = ((group, 2 * VIEWS, 128), F32)
    tok32, tok16 = ((T, D), F32), ((T, D), BF16)
    half32, half16 = ((HALF, D), F32), ((HALF, D), BF16)
    wide = ((T, 4 * D), BF16)
    moved = ((frames, T // frames, 2 * D), BF16)

    def share(field):
        return lax.all_to_all(field, mates, 0, 0, tiled=True)

    def transpose(field):
        return lax.all_to_all(field, frame_axes, 0, 0, tiled=True)

    def swap(field, axis):
        return lax.ppermute(field, axis, [(0, 1), (1, 0)])

    def reduce_weights(keep, give):
        taken = swap(give, "core")
        (partial,) = call(k_weights, [((D, 2 * D), BF16)], order, keep, taken)
        parts = lax.all_to_all(partial.reshape(dp, D // dp, 2 * D), "dp", 0, 0, tiled=True)
        rows = D // dp // (z * xl)
        (summed,) = call(k_sum, [((z * xl, rows, 2 * D), BF16)], parts)
        parts = lax.all_to_all(summed, ("z", "xl"), 0, 0, tiled=True)
        (summed,) = call(k_sum, [((rows, 2 * D), BF16)], parts)
        total = (summed.astype(F32) + swap(summed, "view").astype(F32)).astype(BF16)
        rows = rows // 2
        first = place[1] == 0
        mine = jnp.where(first, total[:rows], total[rows:])
        other = swap(jnp.where(first, total[rows:], total[:rows]), "core")
        low, high = jnp.where(first, mine, other), jnp.where(first, other, mine)
        return jnp.concatenate([low, high[:, :D]], axis=1), high[:, D:]

    views = VIEWS // 2
    x_keep, og_keep, send, st1 = call(
        k_split, [half16, half16, ((HALF, 2 * D), BF16), stats],
        level_in.reshape(views, 2 * PX, D), out_grad.reshape(views, 2 * PX, D), place=place,
    )
    recv = swap(send, "view")
    stream, packed_one, mixed_one, normed_one, og, own, st2 = call(
        functools.partial(k_view, entries),
        [tok32, ((T, 3 * D), BF16), tok16, tok32, tok16, ((2 * VIEWS, 128), F32), stats],
        x_keep, og_keep, recv, share(st1), view_qkv, view_out, place=place,
    )
    out_field, normed_two, inverse_two = call(
        functools.partial(k_norm_two, entries), [moved, tok32, ((VIEWS, 128), F32)], stream, og, share(st2)
    )
    back, keep_two, give_two = call(
        k_time, [moved, wide, wide], transpose(out_field), time_qkv, time_out, place=place
    )
    o_keep, o_send, ghid, st3 = call(
        k_level_out, [half16, half16, tok16, stats], transpose(back), stream, normed_two, place=place
    )
    o_recv = swap(o_send, "view")
    u_keep, u_send, keep_one, give_one, sums_two, st4 = call(
        functools.partial(k_view_back, entries),
        [half32, half16, wide, wide, ((2 * VIEWS, 128), F32), stats],
        ghid, normed_two, inverse_two, share(st3), og, packed_one, mixed_one, normed_one, own,
        view_qkv, view_out, place=place,
    )
    u_recv = swap(u_send, "view")
    level_out, level_in_grad, sums = call(
        functools.partial(k_finish, entries),
        [((views, 2 * PX, D), BF16), ((views, 2 * PX, D), BF16), ((4, views, 128), F32)],
        share(st4), sums_two, own, x_keep, send, u_keep, u_recv, o_keep, o_recv, place=place,
    )
    time_qkv_grad, time_out_grad = reduce_weights(keep_two, give_two)
    view_qkv_grad, view_out_grad = reduce_weights(keep_one, give_one)
    return (
        level_out.reshape(level_in.shape),
        level_in_grad.reshape(level_in.shape),
        view_qkv_grad,
        view_out_grad,
        time_qkv_grad,
        time_out_grad,
        sums[:, :, :GROUPS].reshape(2, 2, views, 1, GROUPS),
    )


def solution(mesh):
    frames, dp = mesh.shape["frame"], mesh.shape["dp"]
    sizes = (frames // 4, 2, 2, dp)
    fine = Mesh(mesh.devices.reshape((2,) + sizes), ("view", "z", "xl", "core", "dp"))
    split = ("z", "xl", "core")
    tokens = P("view", split, "dp", None)
    rows = P(split + ("dp",), None)
    return jax.shard_map(
        functools.partial(body, sizes),
        mesh=fine,
        in_specs=(tokens, tokens, P(), P(), P(), P()),
        out_specs=(tokens, tokens, rows, rows, rows, rows, P(None, None, "view", split, None)),
        check_vma=False,
    )
```

time: 970 us -> 221 us (0.23); the launches traced: 956 us -> 220 us
  blocking collectives: 705 us -> 45.4 us
  matrix products: 88.1 us -> 0 us
  waiting for transfers between devices: 20.7 us -> 68.3 us
  local copies, waits for them, and re-layouts: 68.3 us -> 21.5 us
  Pallas kernels: 0 us -> 31.4 us
  other arithmetic: 16.4 us -> 1.66 us
  between operations: 15.5 us -> 0.91 us
    unnamed x1 -> x0, blocking collectives: 643 us -> none
    dot_general x22 -> x0, matrix products: 81.8 us -> none  [the longest x2 20.5 us: attend_back(): jnp.einsum('bhqk,bqhe->bkhe', dscore_b, split_heads(queries), preferred_e...]
    psum x7 -> x0, blocking collectives: 54.1 us -> none  [the longest x2 17 us: normalize(): totals = lax.psum(jnp.sum(shaped, axis=(2, 4), keepdims=True), 'dp')]
    all_to_all x0 -> x3, blocking collectives: none -> 45.4 us  [the longest x1 25.6 us: transpose(): return lax.all_to_all(field, frame_axes, 0, 0, tiled=True)]
    all_to_all x4 -> x7, waiting for transfers between devices: 20.6 us -> 63.6 us  [the longest x2 32.7 us: reduce_weights(): lax.all_to_all(partial.reshape(dp, D // dp, 2 * D), 'dp', 0, 0, tiled=True)]
    pallas_call x0 -> x13, Pallas kernels: none -> 31.4 us  [call(): pl.pallas_call(kernel, out_shape=[jax.ShapeDtypeStruct(shape, dtype) for...]
    another operation x17 -> x0, local copies, waits for them, and re-layouts: 29.1 us -> none  [the longest x8 13.7 us: split_heads(): return tensor.reshape(tensor.shape[0], tensor.shape[1], HEADS, -1)]
    ppermute x0 -> x9, starting transfers between devices: none -> 19.9 us  [swap(): return lax.ppermute(field, axis, [(0, 1), (1, 0)])]
  transfers between devices with their start and end apart: 5 -> 16, of which waited for: 2 -> 9; matrix products, arithmetic and copies ran while one was open for 8% -> 1% of each run, Pallas kernels for 0% -> 9%
where the time goes in v1:
time: 221 us; the launch traced here: 220 us
  waiting for transfers between devices  68.3 us (31%)
  starting transfers between devices  50.6 us (23%)
  blocking collectives  45.4 us (21%)
  Pallas kernels  31.4 us (14%)
  local copies, waits for them, and re-layouts  21.5 us (10%)
    all_to_all x2, waiting for transfers between devices, reduce_weights(): lax.all_to_all(partial.reshape(dp, D // dp, 2 * D), 'dp', 0, 0, tiled=True)  32.7 us
    pallas_call x13, Pallas kernels, call(): pl.pallas_call(kernel, out_shape=[jax.ShapeDtypeStruct(shape, dtype) for...  31.4 us
    all_to_all x1, blocking collectives, transpose(): return lax.all_to_all(field, frame_axes, 0, 0, tiled=True)  25.6 us
    unnamed x68, local copies, waits for them, and re-layouts  20.1 us
    ppermute x9, starting transfers between devices, swap(): return lax.ppermute(field, axis, [(0, 1), (1, 0)])  19.9 us
    all_to_all x2, blocking collectives, share(): return lax.all_to_all(field, mates, 0, 0, tiled=True)  19.8 us
    all_to_all x2, starting transfers between devices, reduce_weights(): parts = lax.all_to_all(summed, ('z', 'xl'), 0, 0, tiled=True)  12.2 us
    all_to_all x2, waiting for transfers between devices, reduce_weights(): parts = lax.all_to_all(summed, ('z', 'xl'), 0, 0, tiled=True)  11.9 us
  transfers between devices with their start and end apart: 16, of which 9 were waited for; matrix products, arithmetic and copies ran while one was open for 1% of the time, Pallas kernels for 9%

profile of v1, /device:TPU:1, one launch (start us, length us, event | category | flops | bytes accessed | tf_op | source)
XLA Modules:
  0.0 219.8 jit_solution(964275840532100584)
XLA Ops:
  0.7 0.9 copy-done.25
  1.6 0.9 copy-done.26
  2.5 1.9 shard_map.117
  4.5 3.6 %collective-permute-start = (bf16[64,1280]{1,0:T(8,128)(2,1)S(1)}, bf16[64,1280]{1,0:T(8,128)(2,1)S(1)}, u32[]{:S(2)}, u32[]{:S(2)}) collective-permute-start(bf16[64,1280]{1,0:T(8,128)(2,1)S(1)} %get-tuple-element.39.send_ref), channel_id=1, source_target_pairs={{0,128},{128,0},{1,129},{129,1},{2,130},{130,2},{3,131},{131,3},{4... | collective-permute-start | bytes 491528 | tf_op jit(solution)/shard_map/ppermute | solution.py:379
  8.1 0.7 copy-done.21
  8.7 10.7 %all_to_all.50.g_ref = f32[8,16,128]{2,1,0:T(8,128)S(1)} all-to-all(f32[8,16,128]{2,1,0:T(8,128)S(1)} %get-tuple-element.40), channel_id=1, replica_groups=mesh['view'=2,'z'=8,'xl'=2,'core'=2,'dp'=4] {'view','dp'}, dimensions={0} | all-to-all | bytes 131072 | tf_op jit(solution)/shard_map/all_to_all | solution.py:373
  19.4 1.7 copy-done
  21.1 1.1 copy-done.4
  22.3 4.1 %shard_map.118 = (f32[128,640]{1,0:T(8,128)S(1)}, bf16[128,1920]{1,0:T(8,128)(2,1)S(1)}, bf16[128,640]{1,0:T(8,128)(2,1)S(1)}, f32[128,640]{1,0:T(8,128)S(1)}, b...) custom-call(s32[2]{0:T(128)S(1)} %pad_add_fusion.place, ...), custom_call_target="tpu_custom_call" | custom-call | tf_op jit(solution)/shard_map/pallas_call | solution.py:342
  26.3 0.8 copy-done.15
  27.1 0.7 copy-done.17
  27.8 9.1 %all_to_all.51.g_ref = f32[8,16,128]{2,1,0:T(8,128)S(1)} all-to-all(f32[8,16,128]{2,1,0:T(8,128)S(1)} %get-tuple-element.43), channel_id=1, replica_groups=mesh['view'=2,'z'=8,'xl'=2,'core'=2,'dp'=4] {'view','dp'}, dimensions={0} | all-to-all | bytes 131072 | tf_op jit(solution)/shard_map/all_to_all | solution.py:373
  36.9 0.8 shard_map.119
  37.7 25.6 %all_to_all.52.recv_ref = bf16[32,4,1280]{2,1,0:T(4,128)(2,1)S(1)} all-to-all(bf16[32,4,1280]{2,1,0:T(4,128)(2,1)S(1)} %get-tuple-element.44), channel_id=1, replica_groups=mesh['view'=2,'z'=8,'xl'=2,'core'=2,'dp'=4] {'z','xl','core'}, dimensions={0} | all-to-all | bytes 655360 | tf_op jit(solution)/shard_map/all_to_all | solution.py:376
  63.3 5.7 %shard_map.120 = (bf16[32,4,1280]{2,1,0:T(4,128)(2,1)}, bf16[128,2560]{1,0:T(8,128)(2,1)S(1)}, bf16[128,2560]{1,0:T(8,128)(2,1)}) custom-call(s32[2]{0:T(128)S(1)} %pad_add_fusion.place, bf16[32,4,1280]{2,1,0:T(4,128)(2,1)S(1)} %all_to_all.52.recv_ref, bf16[640,1920]{1,0:T(8,128)(2,1)S(1)} %copy-done.7, bf16[640,640]{1,0:T(8,128)(2,1)S(1)} %copy-done.10), custom_call_target="tpu_custom_call" | custom-call | tf_op jit(solution)/shard_map/pallas_call | solution.py:342
  69.0 1.3 collective-permute-start.6
  70.3 3.7 %all-to-all-start.3 = ((bf16[32,4,1280]{2,1,0:T(4,128)(2,1)}), bf16[32,4,1280]{2,1,0:T(4,128)(2,1)S(1)}, u32[]{:S(2)}, u32[]{:S(2)}) async-start(bf16[32,4,1280]{2,1,0:T(4,128)(2,1)} %get-tuple-element.45), calls=%async_computation.3 | async-start | bytes 655360 | tf_op jit(solution)/shard_map/all_to_all | solution.py:376
  74.5 2.8 %shard_map.127 = bf16[640,1280]{1,0:T(8,128)(2,1)} custom-call(bf16[640,640]{1,0:T(8,128)(2,1)S(1)} %fusion.order_ref, bf16[128,2560]{1,0:T(8,128)(2,1)S(1)} %get-tuple-element.64.keep_ref, bf16[128,2560]{1,0:T(8,128)(2,1)S(1)} %collective-permute-done.6.recv_ref), custom_call_target="tpu_custom_call" | custom-call | tf_op jit(solution)/shard_map/pallas_call | solution.py:342
  77.3 9.3 %all-to-all-done.3.back_ref = bf16[32,4,1280]{2,1,0:T(4,128)(2,1)S(1)} async-done(((bf16[32,4,1280]{2,1,0:T(4,128)(2,1)}), bf16[32,4,1280]{2,1,0:T(4,128)(2,1)S(1)}, u32[]{:S(2)}, u32[]{:S(2)}) %all-to-all-start.3) | async-done | bytes 327712 | tf_op jit(solution)/shard_map/all_to_all | solution.py:376
  86.6 3.6 %all-to-all-start.8 = ((bf16[4,160,1280]{2,1,0:T(8,128)(2,1)}), bf16[4,160,1280]{2,1,0:T(8,128)(2,1)S(1)}, u32[]{:S(2)}, u32[]{:S(2)}) async-start(bf16[4,160,1280]{2,1,0:T(8,128)(2,1)} %bitcast.9), calls=%async_computation.8 | async-start | bytes 3276800 | tf_op jit(solution)/shard_map/all_to_all | solution.py:384
  90.2 1.2 shard_map.121
  91.4 0.7 copy-done.19
  92.1 0.7 copy-done.27
  92.7 0.6 copy-done.29
  93.4 0.6 copy-done.30
  94.0 16.2 %all-to-all-done.8.parts_ref = bf16[4,160,1280]{2,1,0:T(8,128)(2,1)S(1)} async-done(((bf16[4,160,1280]{2,1,0:T(8,128)(2,1)}), bf16[4,160,1280]{2,1,0:T(8,128)(2,1)S(1)}, u32[]{:S(2)}, u32[]{:S(2)}) %all-to-all-start.8) | async-done | bytes 1638432 | tf_op jit(solution)/shard_map/all_to_all | solution.py:384
  110.2 1.2 copy-done.2
  111.4 4.2 %all-to-all-start.4 = ((f32[8,16,128]{2,1,0:T(8,128)}), f32[8,16,128]{2,1,0:T(8,128)}, u32[]{:S(2)}, u32[]{:S(2)}) async-start(f32[8,16,128]{2,1,0:T(8,128)} %copy-done.29), calls=%async_computation.4 | async-start | bytes 131072 | tf_op jit(solution)/shard_map/all_to_all | solution.py:373
  115.6 1.4 copy-done.3
  117.3 0.8 copy-done.6
  118.2 4.2 %all-to-all-done.4.g_ref = f32[8,16,128]{2,1,0:T(8,128)} async-done(((f32[8,16,128]{2,1,0:T(8,128)}), f32[8,16,128]{2,1,0:T(8,128)}, u32[]{:S(2)}, u32[]{:S(2)}) %all-to-all-start.4) | async-done | bytes 65568 | tf_op jit(solution)/shard_map/all_to_all | solution.py:373
  122.3 4.5 %all-to-all-start.9 = ((bf16[16,10,1280]{2,1,0:T(8,128)(2,1)}), bf16[16,10,1280]{2,1,0:T(8,128)(2,1)}, u32[]{:S(2)}, u32[]{:S(2)}) async-start(bf16[16,10,1280]{2,1,0:T(8,128)(2,1)} %copy-done.6), calls=%async_computation.9 | async-start | bytes 1310720 | tf_op jit(solution)/shard_map/all_to_all | solution.py:387
  126.9 1.1 copy-done.5
  128.0 1.0 copy-done.9
  129.0 1.0 copy-done.14
  130.0 1.0 copy-done.16
  131.0 0.9 copy-done.18
  131.9 0.9 copy-done.20
  132.8 6.7 %shard_map.122 = (f32[64,640]{1,0:T(8,128)S(1)}, bf16[64,640]{1,0:T(8,128)(2,1)S(1)}, bf16[128,2560]{1,0:T(8,128)(2,1)S(1)}, bf16[128,2560]{1,0:T(8,128)(2,1)S(1...) custom-call(s32[2]{0:T(128)S(1)} %pad_add_fusion.place, bf16[128,640]{1,0:T(8,128)(2,1)S(1)} %copy-done.20, ...), custom_call_target="tpu_custom_call" | custom-call | tf_op jit(solution)/shard_map/pallas_call | solution.py:342
  139.5 0.7 copy-done.23
  140.2 0.6 copy-done.32
  140.8 3.2 %collective-permute-start.3 = (bf16[128,2560]{1,0:T(8,128)(2,1)S(1)}, bf16[128,2560]{1,0:T(8,128)(2,1)S(1)}, u32[]{:S(2)}, u32[]{:S(2)}) collective-permute-start(bf16[128,2560]{1,0:T(8,128)(2,1)S(1)} %get-tuple-element.63), channel_id=1, source_target_pairs={{0,4},{4,0},{1,5},{5,1},{2,6},{6,2},{3,7},{7,3},{8,12},{12,8},{9,1... | collective-permute-start | bytes 1966088 | tf_op jit(solution)/shard_map/ppermute | solution.py:379
  144.0 1.7 collective-permute-done.3.recv_ref
  145.8 2.8 %shard_map.124 = bf16[640,1280]{1,0:T(8,128)(2,1)} custom-call(bf16[640,640]{1,0:T(8,128)(2,1)S(1)} %fusion.order_ref, bf16[128,2560]{1,0:T(8,128)(2,1)S(1)} %get-tuple-element.62.keep_ref, bf16[128,2560]{1,0:T(8,128)(2,1)S(1)} %collective-permute-done.3.recv_ref), custom_call_target="tpu_custom_call" | custom-call | tf_op jit(solution)/shard_map/pallas_call | solution.py:342
  148.6 3.7 %all-to-all-start.6 = ((bf16[4,160,1280]{2,1,0:T(8,128)(2,1)}), bf16[4,160,1280]{2,1,0:T(8,128)(2,1)S(1)}, u32[]{:S(2)}, u32[]{:S(2)}) async-start(bf16[4,160,1280]{2,1,0:T(8,128)(2,1)} %bitcast.8), calls=%async_computation.6 | async-start | bytes 3276800 | tf_op jit(solution)/shard_map/all_to_all | solution.py:384
  152.3 1.2 shard_map.129
  153.4 0.5 collective-permute-start.7
  153.9 2.6 %collective-permute-start.2 = (bf16[64,640]{1,0:T(8,128)(2,1)S(1)}, bf16[64,640]{1,0:T(8,128)(2,1)S(1)}, u32[]{:S(2)}, u32[]{:S(2)}) collective-permute-start(bf16[64,640]{1,0:T(8,128)(2,1)S(1)} %copy-done.31), channel_id=1, source_target_pairs={{0,128},{128,0},{1,129},{129,1},{2,130},{130,2},{3,131},{131,3},{4... | collective-permute-start | bytes 245768 | tf_op jit(solution)/shard_map/ppermute | solution.py:379
  156.5 0.4 collective-permute-start.1
  156.9 16.5 %all-to-all-done.6.parts_ref = bf16[4,160,1280]{2,1,0:T(8,128)(2,1)S(1)} async-done(((bf16[4,160,1280]{2,1,0:T(8,128)(2,1)}), bf16[4,160,1280]{2,1,0:T(8,128)(2,1)S(1)}, u32[]{:S(2)}, u32[]{:S(2)}) %all-to-all-start.6) | async-done | bytes 1638432 | tf_op jit(solution)/shard_map/all_to_all | solution.py:384
  173.4 3.3 %all-to-all-start.5 = ((f32[8,16,128]{2,1,0:T(8,128)}), f32[8,16,128]{2,1,0:T(8,128)S(1)}, u32[]{:S(2)}, u32[]{:S(2)}) async-start(f32[8,16,128]{2,1,0:T(8,128)} %get-tuple-element.54), calls=%async_computation.5 | async-start | bytes 131072 | tf_op jit(solution)/shard_map/all_to_all | solution.py:373
  176.8 1.1 shard_map.125
  177.9 5.5 %all-to-all-done.5.g_ref = f32[8,16,128]{2,1,0:T(8,128)S(1)} async-done(((f32[8,16,128]{2,1,0:T(8,128)}), f32[8,16,128]{2,1,0:T(8,128)S(1)}, u32[]{:S(2)}, u32[]{:S(2)}) %all-to-all-start.5) | async-done | bytes 65568 | tf_op jit(solution)/shard_map/all_to_all | solution.py:373
  183.4 7.7 %all-to-all-start.7 = ((bf16[16,10,1280]{2,1,0:T(8,128)(2,1)}), bf16[16,10,1280]{2,1,0:T(8,128)(2,1)S(1)}, u32[]{:S(2)}, u32[]{:S(2)}) async-start(bf16[16,10,1280]{2,1,0:T(8,128)(2,1)} %shard_map.125), calls=%async_computation.7 | async-start | bytes 1310720 | tf_op jit(solution)/shard_map/all_to_all | solution.py:387
  191.1 2.7 %collective-permute-start.8 = (bf16[5,1280]{1,0:T(8,128)(2,1)S(1)}, bf16[5,1280]{1,0:T(8,128)(2,1)S(1)}, u32[]{:S(2)}, u32[]{:S(2)}) collective-permute-start(bf16[5,1280]{1,0:T(8,128)(2,1)S(1)} %broadcast_select_fusion.2), channel_id=1, source_target_pairs={{0,4},{4,0},{1,5},{5,1},{2,6},{6,2},{3,7},{7,3},{8,12},{12,8},{9,1... | collective-permute-start | bytes 38408 | tf_op jit(solution)/shard_map/ppermute | solution.py:379
  193.9 2.7 %shard_map.123 = (bf16[4,32,640]{2,1,0:T(8,128)(2,1)}, bf16[4,32,640]{2,1,0:T(8,128)(2,1)}, f32[4,4,128]{2,1,0:T(4,128)}) custom-call(s32[2]{0:T(128)S(1)} %pad_add_fusion.place, f32[8,16,128]{2,1,0:T(8,128)S(1)} %all-to-all-done.5.g_ref, f32[16,128]{1,0:T(8,128)S(1)} %get-tuple-element.55.sumstwo_ref, f32[16,128]{1,0:T(8,128)S(1)} %get-tuple-element.53.own_ref, ...), custom_call_target="tpu_custom_call" | custom-call | tf_op jit(solution)/shard_map/pallas_call | solution.py:342
  196.6 11.9 %all-to-all-done.7.parts_ref = bf16[16,10,1280]{2,1,0:T(8,128)(2,1)S(1)} async-done(((bf16[16,10,1280]{2,1,0:T(8,128)(2,1)}), bf16[16,10,1280]{2,1,0:T(8,128)(2,1)S(1)}, u32[]{:S(2)}, u32[]{:S(2)}) %all-to-all-start.7) | async-done | bytes 409632 | tf_op jit(solution)/shard_map/all_to_all | solution.py:387
  208.5 1.0 collective-permute-start.4
  209.6 0.6 fusion.1
  210.2 2.8 %collective-permute-done.4 = bf16[10,1280]{1,0:T(8,128)(2,1)S(1)} collective-permute-done((bf16[10,1280]{1,0:T(8,128)(2,1)S(1)}, bf16[10,1280]{1,0:T(8,128)(2,1)S(1)}, u32[]{:S(2)}, u32[]{:S(2)}) %collective-permute-start.4) | collective-permute-done | bytes 25632 | tf_op jit(solution)/shard_map/ppermute | solution.py:379
  213.0 4.7 %collective-permute-start.5 = (bf16[5,1280]{1,0:T(8,128)(2,1)S(1)}, bf16[5,1280]{1,0:T(8,128)(2,1)S(1)}, u32[]{:S(2)}, u32[]{:S(2)}) collective-permute-start(bf16[5,1280]{1,0:T(8,128)(2,1)S(1)} %broadcast_select_fusion.6), channel_id=1, source_target_pairs={{0,4},{4,0},{1,5},{5,1},{2,6},{6,2},{3,7},{7,3},{8,12},{12,8},{9,1... | collective-permute-start | bytes 38408 | tf_op jit(solution)/shard_map/ppermute | solution.py:379
  217.7 0.6 pad_maximum_fusion.1
  218.6 0.6 fusion.2
  219.2 0.6 pad_maximum_fusion
  (66 shorter events, 1.3 us)
Async XLA Ops:
  0.7 0.9 copy-start.25
  1.6 0.9 copy-start.26
  4.5 14.9 %collective-permute-start = (bf16[64,1280]{1,0:T(8,128)(2,1)S(1)}, bf16[64,1280]{1,0:T(8,128)(2,1)S(1)}, u32[]{:S(2)}, u32[]{:S(2)}) collective-permute-start(bf16[64,1280]{1,0:T(8,128)(2,1)S(1)} %get-tuple-element.39.send_ref), channel_id=1, source_target_pairs={{0,128},{128,0},{1,129},{129,1},{2,130},{130,2},{3,131},{131,3},{4... | collective-permute-start | bytes 491528 | tf_op jit(solution)/shard_map/ppermute | solution.py:379
  8.1 0.7 copy-start.21
  19.4 1.7 copy-start
  21.1 1.1 copy-start.4
  22.3 41.1 %copy-start.7 = (bf16[640,1920]{1,0:T(8,128)(2,1)S(1)}, bf16[640,1920]{1,0:T(8,128)(2,1)}, u32[]{:S(2)}) copy-start(bf16[640,1920]{1,0:T(8,128)(2,1)} %wqkv_ref.4) | copy-start | bytes 7372804
  22.3 41.1 %copy-start.10 = (bf16[640,640]{1,0:T(8,128)(2,1)S(1)}, bf16[640,640]{1,0:T(8,128)(2,1)}, u32[]{:S(2)}) copy-start(bf16[640,640]{1,0:T(8,128)(2,1)} %wout_ref.4) | copy-start | bytes 2457604
  26.3 0.8 copy-start.15
  27.1 0.7 copy-start.17
  27.8 9.9 %copy-start.11 = (bf16[128,640]{1,0:T(8,128)(2,1)}, bf16[128,640]{1,0:T(8,128)(2,1)S(1)}, u32[]{:S(2)}) copy-start(bf16[128,640]{1,0:T(8,128)(2,1)S(1)} %get-tuple-element.42.og_ref) | copy-start | bytes 491524
  27.8 41.2 %copy-start.13 = (bf16[128,1920]{1,0:T(8,128)(2,1)}, bf16[128,1920]{1,0:T(8,128)(2,1)S(1)}, u32[]{:S(2)}) copy-start(bf16[128,1920]{1,0:T(8,128)(2,1)S(1)} %get-tuple-element.50.packed_ref) | copy-start | bytes 1474564
  37.7 52.5 %copy-start.8 = (f32[128,640]{1,0:T(8,128)}, f32[128,640]{1,0:T(8,128)S(1)}, u32[]{:S(2)}) copy-start(f32[128,640]{1,0:T(8,128)S(1)} %get-tuple-element.46.normed_ref.ntwo_ref) | copy-start | bytes 983044
  69.0 5.4 %collective-permute-start.6 = (bf16[128,2560]{1,0:T(8,128)(2,1)}, bf16[128,2560]{1,0:T(8,128)(2,1)S(1)}, u32[]{:S(2)}, u32[]{:S(2)}) collective-permute-start(bf16[128,2560]{1,0:T(8,128)(2,1)} %get-tuple-element.65), channel_id=1, source_target_pairs={{0,4},{4,0},{1,5},{5,1},{2,6},{6,2},{3,7},{7,3},{8,12},{12,8},{9,1... | collective-permute-start | bytes 1966088 | tf_op jit(solution)/shard_map/ppermute | solution.py:379
  70.3 16.3 %all-to-all-start.3 = ((bf16[32,4,1280]{2,1,0:T(4,128)(2,1)}), bf16[32,4,1280]{2,1,0:T(4,128)(2,1)S(1)}, u32[]{:S(2)}, u32[]{:S(2)}) async-start(bf16[32,4,1280]{2,1,0:T(4,128)(2,1)} %get-tuple-element.45), calls=%async_computation.3 | async-start | bytes 655360 | tf_op jit(solution)/shard_map/all_to_all | solution.py:376
  86.6 23.6 %all-to-all-start.8 = ((bf16[4,160,1280]{2,1,0:T(8,128)(2,1)}), bf16[4,160,1280]{2,1,0:T(8,128)(2,1)S(1)}, u32[]{:S(2)}, u32[]{:S(2)}) async-start(bf16[4,160,1280]{2,1,0:T(8,128)(2,1)} %bitcast.9), calls=%async_computation.8 | async-start | bytes 3276800 | tf_op jit(solution)/shard_map/all_to_all | solution.py:384
  91.4 0.7 copy-start.19
  92.1 0.7 copy-start.27
  92.7 0.6 copy-start.29
  93.4 0.6 copy-start.30
  110.2 1.2 copy-start.2
  111.4 10.9 %all-to-all-start.4 = ((f32[8,16,128]{2,1,0:T(8,128)}), f32[8,16,128]{2,1,0:T(8,128)}, u32[]{:S(2)}, u32[]{:S(2)}) async-start(f32[8,16,128]{2,1,0:T(8,128)} %copy-done.29), calls=%async_computation.4 | async-start | bytes 131072 | tf_op jit(solution)/shard_map/all_to_all | solution.py:373
  115.6 1.4 copy-start.3
  117.0 9.8 %copy-start.1 = (bf16[640,1920]{1,0:T(8,128)(2,1)S(1)}, bf16[640,1920]{1,0:T(8,128)(2,1)}, u32[]{:S(2)}) copy-start(bf16[640,1920]{1,0:T(8,128)(2,1)} %wqkv_ref.5) | copy-start | bytes 7372804
  117.0 9.8 %copy-start.12 = (bf16[128,640]{1,0:T(8,128)(2,1)S(1)}, bf16[128,640]{1,0:T(8,128)(2,1)}, u32[]{:S(2)}) copy-start(bf16[128,640]{1,0:T(8,128)(2,1)} %copy-done.11) | copy-start | bytes 491524
  117.3 0.9 copy-start.6
  122.3 26.2 %all-to-all-start.9 = ((bf16[16,10,1280]{2,1,0:T(8,128)(2,1)}), bf16[16,10,1280]{2,1,0:T(8,128)(2,1)}, u32[]{:S(2)}, u32[]{:S(2)}) async-start(bf16[16,10,1280]{2,1,0:T(8,128)(2,1)} %copy-done.6), calls=%async_computation.9 | async-start | bytes 1310720 | tf_op jit(solution)/shard_map/all_to_all | solution.py:387
  126.8 1.1 copy-start.5
  128.0 1.0 copy-start.9
  129.0 1.0 copy-start.14
  130.0 1.0 copy-start.16
  131.0 0.9 copy-start.18
  131.9 0.9 copy-start.20
  139.5 0.7 copy-start.23
  140.2 0.6 copy-start.32
  140.8 4.9 %collective-permute-start.3 = (bf16[128,2560]{1,0:T(8,128)(2,1)S(1)}, bf16[128,2560]{1,0:T(8,128)(2,1)S(1)}, u32[]{:S(2)}, u32[]{:S(2)}) collective-permute-start(bf16[128,2560]{1,0:T(8,128)(2,1)S(1)} %get-tuple-element.63), channel_id=1, source_target_pairs={{0,4},{4,0},{1,5},{5,1},{2,6},{6,2},{3,7},{7,3},{8,12},{12,8},{9,1... | collective-permute-start | bytes 1966088 | tf_op jit(solution)/shard_map/ppermute | solution.py:379
  148.6 5.4 %copy-start.31 = (bf16[64,640]{1,0:T(8,128)(2,1)S(1)}, bf16[64,640]{1,0:T(8,128)(2,1)}, u32[]{:S(2)}) copy-start(bf16[64,640]{1,0:T(8,128)(2,1)} %copy-done.30) | copy-start | bytes 245764
  148.6 8.0 %copy-start.33 = (bf16[64,640]{1,0:T(8,128)(2,1)S(1)}, bf16[64,640]{1,0:T(8,128)(2,1)}, u32[]{:S(2)}) copy-start(bf16[64,640]{1,0:T(8,128)(2,1)} %copy-done.32) | copy-start | bytes 245764
  148.6 24.8 %all-to-all-start.6 = ((bf16[4,160,1280]{2,1,0:T(8,128)(2,1)}), bf16[4,160,1280]{2,1,0:T(8,128)(2,1)S(1)}, u32[]{:S(2)}, u32[]{:S(2)}) async-start(bf16[4,160,1280]{2,1,0:T(8,128)(2,1)} %bitcast.8), calls=%async_computation.6 | async-start | bytes 3276800 | tf_op jit(solution)/shard_map/all_to_all | solution.py:384
  153.4 24.4 %collective-permute-start.7 = (bf16[10,1280]{1,0:T(8,128)(2,1)S(1)}, bf16[10,1280]{1,0:T(8,128)(2,1)S(1)}, u32[]{:S(2)}, u32[]{:S(2)}) collective-permute-start(bf16[10,1280]{1,0:T(8,128)(2,1)S(1)} %shard_map.129), channel_id=1, source_target_pairs={{0,128},{128,0},{1,129},{129,1},{2,130},{130,2},{3,131},{131,3},{4... | collective-permute-start | bytes 76808 | tf_op jit(solution)/shard_map/ppermute | solution.py:379
  153.9 39.9 %collective-permute-start.2 = (bf16[64,640]{1,0:T(8,128)(2,1)S(1)}, bf16[64,640]{1,0:T(8,128)(2,1)S(1)}, u32[]{:S(2)}, u32[]{:S(2)}) collective-permute-start(bf16[64,640]{1,0:T(8,128)(2,1)S(1)} %copy-done.31), channel_id=1, source_target_pairs={{0,128},{128,0},{1,129},{129,1},{2,130},{130,2},{3,131},{131,3},{4... | collective-permute-start | bytes 245768 | tf_op jit(solution)/shard_map/ppermute | solution.py:379
  156.5 37.3 %collective-permute-start.1 = (bf16[64,640]{1,0:T(8,128)(2,1)S(1)}, bf16[64,640]{1,0:T(8,128)(2,1)S(1)}, u32[]{:S(2)}, u32[]{:S(2)}) collective-permute-start(bf16[64,640]{1,0:T(8,128)(2,1)S(1)} %copy-done.33), channel_id=1, source_target_pairs={{0,128},{128,0},{1,129},{129,1},{2,130},{130,2},{3,131},{131,3},{4... | collective-permute-start | bytes 245768 | tf_op jit(solution)/shard_map/ppermute | solution.py:379
  173.4 10.0 %all-to-all-start.5 = ((f32[8,16,128]{2,1,0:T(8,128)}), f32[8,16,128]{2,1,0:T(8,128)S(1)}, u32[]{:S(2)}, u32[]{:S(2)}) async-start(f32[8,16,128]{2,1,0:T(8,128)} %get-tuple-element.54), calls=%async_computation.5 | async-start | bytes 131072 | tf_op jit(solution)/shard_map/all_to_all | solution.py:373
  176.7 17.1 %copy-start.22 = (bf16[64,1280]{1,0:T(8,128)(2,1)S(1)}, bf16[64,1280]{1,0:T(8,128)(2,1)}, u32[]{:S(2)}) copy-start(bf16[64,1280]{1,0:T(8,128)(2,1)} %copy-done.21) | copy-start | bytes 491524
  176.8 17.1 %copy-start.24 = (f32[64,640]{1,0:T(8,128)S(1)}, f32[64,640]{1,0:T(8,128)}, u32[]{:S(2)}) copy-start(f32[64,640]{1,0:T(8,128)} %copy-done.23) | copy-start | bytes 491524
  176.8 17.1 %copy-start.28 = (bf16[64,640]{1,0:T(8,128)(2,1)S(1)}, bf16[64,640]{1,0:T(8,128)(2,1)}, u32[]{:S(2)}) copy-start(bf16[64,640]{1,0:T(8,128)(2,1)} %copy-done.27) | copy-start | bytes 245764
  183.4 25.1 %all-to-all-start.7 = ((bf16[16,10,1280]{2,1,0:T(8,128)(2,1)}), bf16[16,10,1280]{2,1,0:T(8,128)(2,1)S(1)}, u32[]{:S(2)}, u32[]{:S(2)}) async-start(bf16[16,10,1280]{2,1,0:T(8,128)(2,1)} %shard_map.125), calls=%async_computation.7 | async-start | bytes 1310720 | tf_op jit(solution)/shard_map/all_to_all | solution.py:387
  191.1 5.4 %collective-permute-start.8 = (bf16[5,1280]{1,0:T(8,128)(2,1)S(1)}, bf16[5,1280]{1,0:T(8,128)(2,1)S(1)}, u32[]{:S(2)}, u32[]{:S(2)}) collective-permute-start(bf16[5,1280]{1,0:T(8,128)(2,1)S(1)} %broadcast_select_fusion.2), channel_id=1, source_target_pairs={{0,4},{4,0},{1,5},{5,1},{2,6},{6,2},{3,7},{7,3},{8,12},{12,8},{9,1... | collective-permute-start | bytes 38408 | tf_op jit(solution)/shard_map/ppermute | solution.py:379
  208.5 4.4 %collective-permute-start.4 = (bf16[10,1280]{1,0:T(8,128)(2,1)S(1)}, bf16[10,1280]{1,0:T(8,128)(2,1)S(1)}, u32[]{:S(2)}, u32[]{:S(2)}) collective-permute-start(bf16[10,1280]{1,0:T(8,128)(2,1)S(1)} %shard_map.126), channel_id=1, source_target_pairs={{0,128},{128,0},{1,129},{129,1},{2,130},{130,2},{3,131},{131,3},{4... | collective-permute-start | bytes 76808 | tf_op jit(solution)/shard_map/ppermute | solution.py:379
  213.0 5.5 %collective-permute-start.5 = (bf16[5,1280]{1,0:T(8,128)(2,1)S(1)}, bf16[5,1280]{1,0:T(8,128)(2,1)S(1)}, u32[]{:S(2)}, u32[]{:S(2)}) collective-permute-start(bf16[5,1280]{1,0:T(8,128)(2,1)S(1)} %broadcast_select_fusion.6), channel_id=1, source_target_pairs={{0,4},{4,0},{1,5},{5,1},{2,6},{6,2},{3,7},{7,3},{8,12},{12,8},{9,1... | collective-permute-start | bytes 38408 | tf_op jit(solution)/shard_map/ppermute | solution.py:379

commit v2 on v1

v2 whole, which is shorter than its diff:
```python
import functools

import jax
import jax.numpy as jnp
import numpy as np
from jax import lax
from jax.experimental import pallas as pl
from jax.experimental.pallas import tpu as pltpu
from jax.sharding import Mesh, PartitionSpec as P

HEADS = 10
HD = 64
GROUPS = 32
EPS = 1e-05
D = 640
CH = D // GROUPS
VIEWS = 8
PX = 16
T = VIEWS * PX
HALF = T // 2
SCALE = HD ** (-0.5)
F32 = jnp.float32
BF16 = jnp.bfloat16
VMEM_LIMIT = 32


def group_matrix():
    row = lax.broadcasted_iota(jnp.int32, (D, 128), 0)
    low = lax.broadcasted_iota(jnp.int32, (D, 128), 1) * CH
    return ((row >= low) & (row < low + CH)).astype(F32).astype(BF16)


def three_parts(rows):
    high = rows.astype(BF16)
    rest = rows - high.astype(F32)
    middle = rest.astype(BF16)
    return high, middle, (rest - middle.astype(F32)).astype(BF16)


def exact_product(rows, member, dims):
    count = rows.shape[0]
    stacked = jnp.concatenate([part.astype(F32) for part in three_parts(rows)], axis=0).astype(BF16)
    out = lax.dot_general(stacked, member, (dims, ((), ())), preferred_element_type=F32)
    return out[:count] + (out[count : 2 * count] + out[2 * count :])


def to_groups(rows, member):
    return exact_product(rows, member, ((1,), (0,)))


def to_channels(groups, member):
    return exact_product(groups, member, ((1,), (1,)))


def both_sums(grad, normed, member):
    return to_groups(jnp.concatenate([view_sum(grad), view_sum(grad * normed)], axis=0), member)


def view_sum(tokens):
    return jnp.sum(tokens.reshape(tokens.shape[0] // PX, PX, D), axis=1)


def per_token(rows):
    return jnp.broadcast_to(rows[:, None, :], (rows.shape[0], PX, D)).reshape(rows.shape[0] * PX, D)


def partial_stats(tokens, member):
    mean = to_groups(view_sum(tokens), member) * (1.0 / (PX * CH))
    centred = tokens - per_token(to_channels(mean, member))
    return jnp.concatenate([mean, to_groups(view_sum(centred * centred), member)], axis=0)


def merge_stats(means, spreads, entries):
    count = len(means)
    mean = sum(means) * (1.0 / count)
    spread = sum(spreads)
    for other in means:
        gap = other - mean
        spread = spread + gap * gap * float(PX * CH)
    return mean, lax.rsqrt(spread * (1.0 / entries) + EPS)


def spread_out(ref, both):
    ref[...] = jnp.broadcast_to(both[None], ref.shape)


def mm(left, right):
    return jnp.dot(left, right, preferred_element_type=F32)


def mm_t(left, right):
    return lax.dot_general(left, right, (((1,), (1,)), ((), ())), preferred_element_type=F32)


def t_mm(left, right):
    return lax.dot_general(left, right, (((0,), (0,)), ((), ())), preferred_element_type=F32)


def lane_low(rows):
    return lax.broadcasted_iota(jnp.int32, (rows, 128), 1) < HD


def both_heads(pair):
    low = lane_low(pair.shape[0])
    zero = jnp.zeros_like(pair)
    return jnp.concatenate([jnp.where(low, pair, zero), jnp.where(low, zero, pair)], axis=0)


def join_heads(stacked):
    return jnp.where(lane_low(T), stacked[:T], stacked[T:])


def same_sequence(period):
    row = lax.broadcasted_iota(jnp.int32, (2 * T, T), 0)
    col = lax.broadcasted_iota(jnp.int32, (2 * T, T), 1)
    return ((row ^ col) & (period - 1)) == 0


def softmax_pair(stacked_q, keys, allowed):
    scores = jnp.where(allowed, mm_t(stacked_q, keys) * SCALE, -1e30)
    top = jnp.max(scores, axis=-1, keepdims=True)
    weights = jnp.exp(scores - top)
    return weights / jnp.sum(weights, axis=-1, keepdims=True)


def pair_of(index):
    return slice(index * 128, (index + 1) * 128)


def attend(packed, allowed):
    outs = []
    for pair in range(HEADS // 2):
        q = both_heads(packed[:, pair_of(pair)])
        k = packed[:, pair_of(pair + 5)]
        v = packed[:, pair_of(pair + 10)]
        prob = softmax_pair(q, k, allowed).astype(BF16)
        outs.append(join_heads(mm(prob, v)).astype(BF16))
    return jnp.concatenate(outs, axis=1)


def attend_back(grad, packed, allowed):
    dqs, dks, dvs = [], [], []
    for pair in range(HEADS // 2):
        q = both_heads(packed[:, pair_of(pair)])
        k = packed[:, pair_of(pair + 5)]
        v = packed[:, pair_of(pair + 10)]
        g = both_heads(grad[:, pair_of(pair)])
        prob = softmax_pair(q, k, allowed)
        dvs.append(t_mm(prob.astype(BF16), g).astype(BF16))
        dprob = mm_t(g, v)
        dscore = prob * (dprob - jnp.sum(dprob * prob, axis=-1, keepdims=True))
        dscore = (dscore * SCALE).astype(BF16)
        dqs.append(join_heads(mm(dscore, k)).astype(BF16))
        dks.append(t_mm(dscore, q).astype(BF16))
    return jnp.concatenate(dqs + dks + dvs, axis=1)


def halves(ref, first):
    low = ref[:, 0, 0:PX, :].reshape(HALF, D)
    high = ref[:, 0, PX : 2 * PX, :].reshape(HALF, D)
    return jnp.where(first, low, high), jnp.where(first, high, low)


def regrouped(own_ref, other_ref, first):
    mine, theirs = halves(own_ref, first)[0], halves(other_ref, first)[0]
    return jnp.concatenate([jnp.where(first, mine, theirs), jnp.where(first, theirs, mine)], axis=0)


def k_first_stats(place, x_ref, stats_ref):
    keep, give = halves(x_ref, place[0] == 0)
    tokens = jnp.concatenate([keep, give], axis=0).astype(F32)
    spread_out(stats_ref, partial_stats(tokens, group_matrix()))


def normalized(x, rows, member):
    channels = to_channels(rows, member)
    return (x - per_token(channels[:VIEWS])) * per_token(channels[VIEWS:])


def k_view(entries, place, x_ref, other_ref, g_ref, wqkv_ref, wout_ref, stream_ref, saved_ref, own_ref, stats_ref):
    first = place[0] == 0
    member = group_matrix()
    sources = g_ref.shape[0]
    half = VIEWS // 2

    def side(low):
        chosen = range(low, low + sources // 2)
        means = [g_ref[s, a * half : (a + 1) * half, :] for s in chosen for a in range(2)]
        spreads = [g_ref[s, VIEWS + a * half : VIEWS + (a + 1) * half, :] for s in chosen for a in range(2)]
        return merge_stats(means, spreads, entries)

    low, high = side(0), side(sources // 2)
    rows = jnp.concatenate([low[0], high[0], low[1], high[1]], axis=0)
    own_ref[...] = rows
    x = regrouped(x_ref, other_ref, first).astype(F32)
    packed = mm(normalized(x, rows, member).astype(BF16), wqkv_ref[...]).astype(BF16)
    saved_ref[:, : 3 * D] = packed
    mixed = attend(packed, same_sequence(PX))
    saved_ref[:, 3 * D :] = mixed
    stream = x + mm(mixed, wout_ref[...])
    stream_ref[...] = stream
    spread_out(stats_ref, partial_stats(stream, member))


def k_norm_two(entries, place, stream_ref, grad_ref, other_ref, g_ref, send_ref, rows_ref):
    member = group_matrix()
    sources = range(g_ref.shape[0])
    mean, inverse = merge_stats(
        [g_ref[s, 0:VIEWS, :] for s in sources], [g_ref[s, VIEWS:, :] for s in sources], entries
    )
    rows = jnp.concatenate([mean, inverse], axis=0)
    rows_ref[...] = rows
    shape = send_ref.shape[:2] + (D,)
    send_ref[:, :, :D] = normalized(stream_ref[...], rows, member).astype(BF16).reshape(shape)
    send_ref[:, :, D:] = regrouped(grad_ref, other_ref, place[0] == 0).reshape(shape)


def weight_sides(core, hidden, mixed, packed_grad, grad, keep_ref, give_ref):
    first = core == 0
    quarter = packed_grad[:, :D], packed_grad[:, D : 2 * D], packed_grad[:, 2 * D :], grad
    keep_ref[:, :D] = hidden
    give_ref[:, :D] = hidden
    keep_ref[:, D : 2 * D] = jnp.where(first, hidden, mixed)
    give_ref[:, D : 2 * D] = jnp.where(first, mixed, hidden)
    for slot in range(2):
        cols = slice((2 + slot) * D, (3 + slot) * D)
        keep_ref[:, cols] = jnp.where(first, quarter[slot], quarter[2 + slot])
        give_ref[:, cols] = jnp.where(first, quarter[2 + slot], quarter[slot])


def k_time(place, recv_ref, wqkv_ref, wout_ref, back_ref, keep_ref, give_ref):
    hidden = recv_ref[:, :, :D].reshape(T, D)
    grad = recv_ref[:, :, D:].reshape(T, D)
    allowed = same_sequence(recv_ref.shape[1])
    packed = mm(hidden, wqkv_ref[...]).astype(BF16)
    mixed = attend(packed, allowed)
    shape = back_ref.shape[:2] + (D,)
    back_ref[:, :, :D] = mm(mixed, wout_ref[...]).astype(BF16).reshape(shape)
    packed_grad = attend_back(mm_t(grad, wout_ref[...]).astype(BF16), packed, allowed)
    back_ref[:, :, D:] = mm_t(packed_grad, wqkv_ref[...]).astype(BF16).reshape(shape)
    weight_sides(place[1], hidden, mixed, packed_grad, grad, keep_ref, give_ref)


def k_back_stats(back_ref, stream_ref, rows_ref, stats_ref):
    member = group_matrix()
    normed = normalized(stream_ref[...], rows_ref[...], member)
    grad = back_ref[:, :, D:].reshape(T, D).astype(F32)
    spread_out(stats_ref, both_sums(grad, normed, member))


def k_view_back(entries, place, back_ref, stream_ref, rows_ref, g_ref, og_ref, ogother_ref, x_ref, other_ref, own_ref,
                saved_ref, wout_ref, keep_ref, give_ref, pgrad_ref, stream_grad_ref, normed_ref, sums_ref):
    first = place[0] == 0
    member = group_matrix()
    sums = g_ref[0]
    for s in range(1, g_ref.shape[0]):
        sums = sums + g_ref[s]
    sums_ref[...] = sums
    channels = to_channels(jnp.concatenate([sums * (1.0 / entries), rows_ref[...], own_ref[...]], axis=0), member)
    m1, m2, mean, inverse, mean_one, inverse_one = (
        per_token(channels[k * VIEWS : (k + 1) * VIEWS]) for k in range(6)
    )
    normed_two = (stream_ref[...] - mean) * inverse
    ghid = back_ref[:, :, D:].reshape(T, D).astype(F32)
    grad_stream = regrouped(og_ref, ogother_ref, first).astype(F32) + inverse * (ghid - m1 - normed_two * m2)
    stream_grad_ref[...] = grad_stream
    grad_b = grad_stream.astype(BF16)
    packed_grad = attend_back(mm_t(grad_b, wout_ref[...]).astype(BF16), saved_ref[:, : 3 * D], same_sequence(PX))
    pgrad_ref[...] = packed_grad
    normed = (regrouped(x_ref, other_ref, first).astype(F32) - mean_one) * inverse_one
    normed_ref[...] = normed
    weight_sides(place[1], normed.astype(BF16), saved_ref[:, 3 * D :], packed_grad, grad_b, keep_ref, give_ref)


def k_view_stats(place, pgrad_ref, stream_grad_ref, back_ref, stream_ref, none_ref, own_ref, wqkv_ref,
                 ukeep_ref, okeep_ref, send_ref, stats_ref):
    first = place[0] == 0
    member = group_matrix()
    grad = mm_t(pgrad_ref[...], wqkv_ref[...]).astype(BF16).astype(F32)
    stats = both_sums(grad, none_ref[...], member)
    stats_ref[...] = stats
    partly = stream_grad_ref[...] + per_token(to_channels(own_ref[VIEWS:, :], member)) * grad
    temporal = back_ref[:, :, :D].reshape(T, D).astype(F32)
    out = (stream_ref[...] + temporal).astype(BF16)
    ukeep_ref[...] = jnp.where(first, partly[:HALF], partly[HALF:])
    okeep_ref[...] = jnp.where(first, out[:HALF], out[HALF:])
    send_ref[:, :D] = jnp.where(first, partly[HALF:], partly[:HALF]).astype(BF16)
    send_ref[:, D:] = jnp.where(first, out[HALF:], out[:HALF])


def k_finish(entries, place, g_ref, sumstwo_ref, own_ref, x_ref, ukeep_ref, okeep_ref, recv_ref,
             out_ref, grad_ref, sums_ref):
    first = place[0] == 0
    member = group_matrix()
    half = VIEWS // 2
    sums = g_ref[...]

    def mine(rows):
        return jnp.where(first, rows[:half], rows[half:])

    s1, s2 = mine(sums[:VIEWS]), mine(sums[VIEWS:])
    sums_ref[0] = s1
    sums_ref[1] = s2
    sums_ref[2] = mine(sumstwo_ref[0:VIEWS, :])
    sums_ref[3] = mine(sumstwo_ref[VIEWS:, :])
    inverse = mine(own_ref[VIEWS:, :])
    scale = inverse * (1.0 / entries)
    rows = jnp.concatenate([mine(own_ref[0:VIEWS, :]), inverse, s1 * scale, s2 * scale], axis=0)
    channels = to_channels(rows, member)
    mean_c, inverse_c, a, b = (per_token(channels[k * half : (k + 1) * half]) for k in range(4))

    def finished(part, x):
        normed = (x.astype(F32) - mean_c) * inverse_c
        return (part.astype(F32) - a - normed * b).astype(BF16)

    x_keep, x_give = halves(x_ref, first)
    keep = finished(ukeep_ref[...], x_keep)
    other = finished(recv_ref[:, :D], x_give)
    shape = (half, PX, D)
    grad_ref[:, 0:PX, :] = jnp.where(first, keep, other).reshape(shape)
    grad_ref[:, PX:, :] = jnp.where(first, other, keep).reshape(shape)
    okeep, orecv = okeep_ref[...], recv_ref[:, D:]
    out_ref[:, 0:PX, :] = jnp.where(first, okeep, orecv).reshape(shape)
    out_ref[:, PX:, :] = jnp.where(first, orecv, okeep).reshape(shape)


def added32(*refs):
    total = refs[0][...].astype(F32)
    for ref in refs[1:]:
        total = total + ref[...].astype(F32)
    return total


def added(*refs):
    return added32(*refs).astype(BF16)


def split_rows(total, refs, cols=slice(None)):
    rows = total.shape[0] // len(refs)
    for s, ref in enumerate(refs):
        ref[:, cols] = total[s * rows : (s + 1) * rows]


def weight_tile(unit, places, keep_ref, recv_ref):
    row = lax.broadcasted_iota(jnp.int32, (D, D), 0)
    left = jnp.concatenate([keep_ref[:, unit * D : (unit + 1) * D], recv_ref[:, unit * D : (unit + 1) * D]], axis=0)
    cols = slice((2 + unit) * D, (3 + unit) * D)
    right = jnp.concatenate([keep_ref[:, cols], recv_ref[:, cols]], axis=0)
    order = (row == places).astype(BF16)
    return t_mm(mm(left, order).astype(BF16), right).astype(BF16)


def k_weights_time(place, table_ref, keep_ref, recv_ref, *out_refs):
    places = table_ref[place[2]]
    for unit in range(2):
        split_rows(weight_tile(unit, places, keep_ref, recv_ref), out_refs, slice(unit * D, (unit + 1) * D))


def k_weights_view(table_ref, keep_ref, recv_ref, out_ref):
    places = table_ref[table_ref.shape[0] - 1]
    for unit in range(2):
        out_ref[:, unit * D : (unit + 1) * D] = weight_tile(unit, places, keep_ref, recv_ref)


def k_sum_time(*refs):
    split_rows(added(*refs[:4]), refs[4:])


def k_sum_rows(parts_ref, *refs):
    times, out_ref = refs[:4], refs[4]
    chips = out_ref.shape[0]
    rows = times[0].shape[0]
    count = parts_ref.shape[0] // rows
    view = sum(parts_ref[s * rows : (s + 1) * rows, :].astype(F32) for s in range(count))
    time = added32(*times)
    units = [view[:, :D], view[:, D:], time[:, :D], time[:, D:]]
    for row in range(out_ref.shape[2] // D):
        block = jnp.stack([unit[row * chips : (row + 1) * chips] for unit in units], axis=1)
        out_ref[:, :, row * D : (row + 1) * D] = block.astype(BF16)


def k_sum(parts_ref, out_ref):
    total = parts_ref[0].astype(F32)
    for s in range(1, parts_ref.shape[0]):
        total = total + parts_ref[s].astype(F32)
    out_ref[...] = total.astype(BF16)


def k_rows(place, near_ref, far_ref, vqkv_ref, vout_ref, tqkv_ref, tout_ref):
    both = jnp.where(place[0] == place[1], near_ref[...].astype(F32), far_ref[...].astype(F32))
    low, high = both[:4], both[4:]
    for row in range(vout_ref.shape[0]):
        cols = slice(row * D, (row + 1) * D)
        line = slice(row, row + 1)
        for unit, qkv_ref, out_ref in ((0, vqkv_ref, vout_ref), (2, tqkv_ref, tout_ref)):
            qkv_ref[line, :D] = low[unit : unit + 1, cols].astype(BF16)
            qkv_ref[line, D : 2 * D] = low[unit + 1 : unit + 2, cols].astype(BF16)
            qkv_ref[line, 2 * D :] = high[unit : unit + 1, cols].astype(BF16)
            out_ref[line, :] = high[unit + 1 : unit + 2, cols].astype(BF16)


def call(kernel, outs, *args, place=None, us=2, vmem=VMEM_LIMIT):
    specs = [pl.BlockSpec(memory_space=pltpu.VMEM)] * len(args)
    if place is not None:
        specs = [pl.BlockSpec(memory_space=pltpu.SMEM)] + specs
        args = (place,) + args
    return pl.pallas_call(
        kernel,
        out_shape=[jax.ShapeDtypeStruct(shape, dtype) for shape, dtype in outs],
        in_specs=specs,
        out_specs=[pl.BlockSpec(memory_space=pltpu.VMEM)] * len(outs),
        compiler_params=pltpu.CompilerParams(vmem_limit_bytes=vmem * 1024 * 1024),
        cost_estimate=pl.CostEstimate(flops=int(us * 1e9), bytes_accessed=int(us * 3e6), transcendentals=0),
    )(*args)


def row_table(z, xl, core, dp):
    rows = D // (z * xl * core * dp)
    ring = core * xl
    chip = np.arange(z).reshape(1, 1, 1, z)
    row = np.arange(rows).reshape(1, 1, rows, 1)

    def place(y, x):
        return ((((chip * xl + x % xl) * core + x // xl) * dp + y) * rows + row).reshape(1, -1)

    table = []
    for me_x in range(ring):
        for me_dp in range(dp):
            y, x = (me_dp + np.arange(dp)) % dp, (me_x + np.arange(ring)) % ring
            table.append(place(y.reshape(dp, 1, 1, 1), x.reshape(1, ring, 1, 1)))
    table.append(place(np.arange(dp).reshape(1, dp, 1, 1), np.arange(ring).reshape(ring, 1, 1, 1)))
    return np.stack(table).astype(np.int32)


def body(sizes, level_in, out_grad, view_qkv, view_out, time_qkv, time_out):
    z, xl, core, dp = sizes
    frames = z * xl * core
    entries = float(dp * 2 * PX * CH)
    frame_axes = ("z", "xl", "core")
    mates = ("view", "dp")
    group = 2 * dp
    spot = (lax.axis_index("view") * xl + lax.axis_index("xl")) * dp + lax.axis_index("dp")
    place = jnp.stack([lax.axis_index("view"), lax.axis_index("core"), spot]).astype(jnp.int32)
    table = jnp.asarray(row_table(z, xl, core, dp))
    rows = D // (z * xl * core * dp)
    stats = ((group, 2 * VIEWS, 128), F32)
    tok32, tok16 = ((T, D), F32), ((T, D), BF16)
    half32, half16 = ((HALF, D), F32), ((HALF, D), BF16)
    wide = ((T, 4 * D), BF16)
    moved = ((frames, T // frames, 2 * D), BF16)

    def share(field):
        return lax.all_to_all(field, mates, 0, 0, tiled=True)

    def transpose(field):
        return lax.all_to_all(field, frame_axes, 0, 0, tiled=True)

    def swap(field, axis):
        return lax.ppermute(field, axis, [(0, 1), (1, 0)])

    def shifted(pieces, axis):
        return [
            lax.ppermute(piece, axis, [(i, (i + step + 1) % 4) for i in range(4)]) for step, piece in enumerate(pieces)
        ]

    def crossed(field, step):
        return field + lax.ppermute(field, "dp", [(i, i ^ step) for i in range(dp)])

    views = VIEWS // 2
    rows16 = ((2 * VIEWS, 128), F32)
    x_other, og_other = swap(level_in, "view"), swap(out_grad, "view")
    (st1,) = call(k_first_stats, [stats], level_in, place=place)
    stream, saved, own, st2 = call(
        functools.partial(k_view, entries), [tok32, wide, rows16, stats],
        level_in, x_other, share(st1), view_qkv, view_out, place=place, us=4,
    )
    out_field, rows_two = call(
        functools.partial(k_norm_two, entries), [moved, rows16], stream, out_grad, og_other, share(st2), place=place
    )
    back, keep_two, give_two = call(
        k_time, [moved, wide, wide], transpose(out_field), time_qkv, time_out, place=place, us=6
    )
    mine, *pieces = call(
        k_weights_time, [((D // 4, 2 * D), BF16)] * 4, table, keep_two, swap(give_two, "core"), place=place, us=3
    )
    moved_back, _ = lax.optimization_barrier((transpose(back), pieces))
    time_parts = [mine, *shifted(pieces, "dp")]
    (st3,) = call(k_back_stats, [stats], moved_back, stream, rows_two, us=1)
    shared, time_parts = lax.optimization_barrier((share(st3), time_parts))
    keep_one, give_one, pgrad, stream_grad, normed_one, sums_two = call(
        functools.partial(k_view_back, entries), [wide, wide, ((T, 3 * D), BF16), tok32, tok32, rows16],
        moved_back, stream, rows_two, shared, out_grad, og_other, level_in, x_other, own, saved, view_out,
        place=place, us=5,
    )
    u_keep, o_keep, send_back, st4 = call(
        k_view_stats, [half32, half16, ((HALF, 2 * D), BF16), rows16],
        pgrad, stream_grad, moved_back, stream, normed_one, own, view_qkv, place=place, us=3,
    )
    taken, st4 = lax.optimization_barrier((swap(give_one, "core"), st4))
    (partial,) = call(k_weights_view, [((D, 2 * D), BF16)], table, keep_one, taken, place=None, us=3)
    time_parts, partial = lax.optimization_barrier((time_parts, partial))
    parts = lax.all_to_all(partial, ("view", "xl", "dp"), 0, 0, tiled=True)
    mine, *pieces = call(k_sum_time, [((D // 16, 2 * D), BF16)] * 4, *time_parts)
    time_parts = [mine, *shifted(pieces, ("view", "xl"))]
    parts, time_parts, st4 = lax.optimization_barrier((parts, time_parts, st4 + swap(st4, "view")))
    (by_z,) = call(k_sum_rows, [((z, 4, rows * D), BF16)], parts, *time_parts)
    by_z, st4, send_back = lax.optimization_barrier((by_z, st4, send_back))
    by_z = lax.all_to_all(by_z, "z", 0, 0, tiled=True)
    recv_back = swap(send_back, "view")
    st4 = crossed(crossed(st4, 1), 2)
    by_z, st4 = lax.optimization_barrier((by_z, st4))
    (summed,) = call(k_sum, [((4, rows * D), BF16)], by_z)
    level_out, level_in_grad, sums = call(
        functools.partial(k_finish, entries),
        [((views, 2 * PX, D), BF16), ((views, 2 * PX, D), BF16), ((4, views, 128), F32)],
        st4, sums_two, own, level_in, u_keep, o_keep, recv_back, place=place, us=3,
    )
    first = place[1] == 0
    near = swap(summed, "core")
    pair = jnp.concatenate([jnp.where(first, summed, near), jnp.where(first, near, summed)], axis=0)
    qkv_row, out_row = ((rows, 3 * D), BF16), ((rows, D), BF16)
    view_qkv_grad, view_out_grad, time_qkv_grad, time_out_grad = call(
        k_rows, [qkv_row, out_row, qkv_row, out_row], pair, swap(pair, "view"), place=place
    )
    return (
        level_out.reshape(level_in.shape),
        level_in_grad.reshape(level_in.shape),
        view_qkv_grad,
        view_out_grad,
        time_qkv_grad,
        time_out_grad,
        sums[:, :, :GROUPS].reshape(2, 2, views, 1, GROUPS),
    )


def solution(mesh):
    frames, dp = mesh.shape["frame"], mesh.shape["dp"]
    sizes = (frames // 4, 2, 2, dp)
    fine = Mesh(mesh.devices.reshape((2,) + sizes), ("view", "z", "xl", "core", "dp"))
    split = ("z", "xl", "core")
    tokens = P("view", split, "dp", None)
    rows = P(split + ("dp",), None)
    return jax.shard_map(
        functools.partial(body, sizes),
        mesh=fine,
        in_specs=(tokens, tokens, P(), P(), P(), P()),
        out_specs=(tokens, tokens, rows, rows, rows, rows, P(None, None, "view", split, None)),
        check_vma=False,
    )
```

time: 221 us -> 171 us (0.77)
  waiting for transfers between devices: 68.3 us -> 43.9 us
  local copies, waits for them, and re-layouts: 21.5 us -> 8.4 us
  blocking collectives: 45.4 us -> 38.6 us
  Pallas kernels: 31.4 us -> 28.1 us
    all_to_all x4 -> x2, waiting for transfers between devices: 44.6 us -> 2.08 us  [the longest x1 2.08 us: body(): by_z = lax.all_to_all(by_z, 'z', 0, 0, tiled=True)]
    ppermute x9 -> x8, waiting for transfers between devices: 4.76 us -> 23.6 us  [swap(): return lax.ppermute(field, axis, [(0, 1), (1, 0)])]
    unnamed x68 -> x58, local copies, waits for them, and re-layouts: 20.1 us -> 8.4 us
    ppermute x0 -> x8, starting transfers between devices: none -> 11.5 us  [the longest x6 7.9 us: shifted(): lax.ppermute(piece, axis, [(i, (i + step + 1) % 4) for i in range(4)])]
    all_to_all x4 -> x2, starting transfers between devices: 19.5 us -> 11.5 us  [the longest x1 6.51 us: body(): by_z = lax.all_to_all(by_z, 'z', 0, 0, tiled=True)]
    all_to_all x2 -> x1, blocking collectives: 19.8 us -> 12.6 us  [share(): return lax.all_to_all(field, mates, 0, 0, tiled=True)]
    all_to_all x1, waiting for transfers between devices: 9.34 us -> 4.92 us  [transpose(): return lax.all_to_all(field, frame_axes, 0, 0, tiled=True)]
    ppermute x9 -> x8, starting transfers between devices: 19.9 us -> 15.6 us  [swap(): return lax.ppermute(field, axis, [(0, 1), (1, 0)])]
  transfers between devices with their start and end apart: 16 -> 21, of which waited for: 9 -> 8; matrix products, arithmetic and copies ran while one was open for 1% -> 0% of each run, Pallas kernels for 9% -> 7%
where the time goes in v2:
time: 171 us; the launch traced here: 170 us
  starting transfers between devices  49.7 us (29%)
  waiting for transfers between devices  43.9 us (26%)
  blocking collectives  38.6 us (23%)
  Pallas kernels  28.1 us (16%)
  local copies, waits for them, and re-layouts  8.4 us (5%)
    pallas_call x14, Pallas kernels, call(): pl.pallas_call(kernel, out_shape=[jax.ShapeDtypeStruct(shape, dtype) for...  28.1 us
    all_to_all x1, blocking collectives, transpose(): return lax.all_to_all(field, frame_axes, 0, 0, tiled=True)  26 us
    ppermute x8, waiting for transfers between devices, swap(): return lax.ppermute(field, axis, [(0, 1), (1, 0)])  23.6 us
    ppermute x8, starting transfers between devices, swap(): return lax.ppermute(field, axis, [(0, 1), (1, 0)])  15.6 us
    all_to_all x1, blocking collectives, share(): return lax.all_to_all(field, mates, 0, 0, tiled=True)  12.6 us
    all_to_all x2, waiting for transfers between devices, share(): return lax.all_to_all(field, mates, 0, 0, tiled=True)  10.3 us
    unnamed x58, local copies, waits for them, and re-layouts  8.4 us
    ppermute x6, starting transfers between devices, shifted(): lax.ppermute(piece, axis, [(i, (i + step + 1) % 4) for i in range(4)])  7.9 us
  transfers between devices with their start and end apart: 21, of which 8 were waited for; matrix products, arithmetic and copies ran while one was open for 0% of the time, Pallas kernels for 7%

profile of v2, /device:TPU:1, one launch (start us, length us, event | category | flops | bytes accessed | tf_op | source)
XLA Modules:
  0.0 169.8 jit_solution(9438515375950989541)
XLA Ops:
  0.6 3.7 %collective-permute-start = (bf16[4,1,32,640]{3,2,1,0:T(8,128)(2,1)}, bf16[4,1,32,640]{3,2,1,0:T(8,128)(2,1)S(1)}, u32[]{:S(2)}, u32[]{:S(2)}) collective-permute-start(bf16[4,1,32,640]{3,2,1,0:T(8,128)(2,1)} %x_ref.7), channel_id=1, source_target_pairs={{0,128},{128,0},{1,129},{129,1},{2,130},{130,2},{3,131},{131,3},{4... | collective-permute-start | bytes 491528 | tf_op jit(solution)/shard_map/ppermute | solution.py:459
  4.3 0.1 pad_add_fusion.place
  4.4 0.9 copy-done.8
  5.3 1.9 %shard_map.126 = f32[8,16,128]{2,1,0:T(8,128)} custom-call(s32[3]{0:T(128)S(1)} %pad_add_fusion.place, bf16[4,1,32,640]{3,2,1,0:T(8,128)(2,1)S(1)} %copy-done.8), custom_call_target="tpu_custom_call" | custom-call | flops 2000000000 | bytes 6000000 | tf_op jit(solution)/shard_map/pallas_call | solution.py:407
  7.2 4.2 %all-to-all-start = ((f32[8,16,128]{2,1,0:T(8,128)}), f32[8,16,128]{2,1,0:T(8,128)S(1)}, u32[]{:S(2)}, u32[]{:S(2)}) async-start(f32[8,16,128]{2,1,0:T(8,128)} %shard_map.126), calls=%async_computation | async-start | bytes 131072 | tf_op jit(solution)/shard_map/all_to_all | solution.py:453
  11.4 3.0 %collective-permute-start.1 = (bf16[4,1,32,640]{3,2,1,0:T(8,128)(2,1)S(1)}, bf16[4,1,32,640]{3,2,1,0:T(8,128)(2,1)S(1)}, u32[]{:S(2)}, u32[]{:S(2)}) collective-permute-start(bf16[4,1,32,640]{3,2,1,0:T(8,128)(2,1)S(1)} %copy-done.7), channel_id=1, source_target_pairs={{0,128},{128,0},{1,129},{129,1},{2,130},{130,2},{3,131},{131,3},{4... | collective-permute-start | bytes 491528 | tf_op jit(solution)/shard_map/ppermute | solution.py:459
  14.4 3.7 %all-to-all-done.g_ref = f32[8,16,128]{2,1,0:T(8,128)S(1)} async-done(((f32[8,16,128]{2,1,0:T(8,128)}), f32[8,16,128]{2,1,0:T(8,128)S(1)}, u32[]{:S(2)}, u32[]{:S(2)}) %all-to-all-start) | async-done | bytes 65568 | tf_op jit(solution)/shard_map/all_to_all | solution.py:453
  18.1 0.0 collective-permute-done.other_ref
  18.1 0.0 copy-start.1
  18.1 1.7 copy-done.1
  19.8 3.4 %shard_map.127 = (f32[128,640]{1,0:T(8,128)S(1)}, bf16[128,2560]{1,0:T(8,128)(2,1)S(1)}, f32[16,128]{1,0:T(8,128)S(1)}, f32[8,16,128]{2,1,0:T(8,128)}) custom-call(s32[3]{0:T(128)S(1)} %pad_add_fusion.place, bf16[4,1,32,640]{3,2,1,0:T(8,128)(2,1)S(1)} %copy-done.9, bf16[4,1,32,640]{3,2,1,0:T(8,128)(2,1)S(1)} %collective-permute-done.other_ref, ...), custom_call_target="tpu_custom_call" | custom-call | flops 4000000000 | bytes 12000000 | tf_op jit(solution)/shard_map/pallas_call | solution.py:407
  23.2 0.8 copy-done.23
  24.0 3.3 %all-to-all-start.1 = ((f32[8,16,128]{2,1,0:T(8,128)}), f32[8,16,128]{2,1,0:T(8,128)S(1)}, u32[]{:S(2)}, u32[]{:S(2)}) async-start(f32[8,16,128]{2,1,0:T(8,128)} %get-tuple-element.66), calls=%async_computation.1 | async-start | bytes 131072 | tf_op jit(solution)/shard_map/all_to_all | solution.py:453
  27.4 0.0 collective-permute-done.1.other_ref.ogother_ref
  27.4 0.0 copy-start.14
  27.4 6.6 %all-to-all-done.1.g_ref = f32[8,16,128]{2,1,0:T(8,128)S(1)} async-done(((f32[8,16,128]{2,1,0:T(8,128)}), f32[8,16,128]{2,1,0:T(8,128)S(1)}, u32[]{:S(2)}, u32[]{:S(2)}) %all-to-all-start.1) | async-done | bytes 65568 | tf_op jit(solution)/shard_map/all_to_all | solution.py:453
  34.0 0.9 shard_map.128
  34.9 26.0 %all_to_all.42.recv_ref = bf16[32,4,1280]{2,1,0:T(4,128)(2,1)S(1)} all-to-all(bf16[32,4,1280]{2,1,0:T(4,128)(2,1)S(1)} %get-tuple-element.67), channel_id=1, replica_groups=mesh['view'=2,'z'=8,'xl'=2,'core'=2,'dp'=4] {'z','xl','core'}, dimensions={0} | all-to-all | bytes 655360 | tf_op jit(solution)/shard_map/all_to_all | solution.py:456
  60.9 5.6 %shard_map.129 = (bf16[32,4,1280]{2,1,0:T(4,128)(2,1)}, bf16[128,2560]{1,0:T(8,128)(2,1)S(1)}, bf16[128,2560]{1,0:T(8,128)(2,1)S(1)}) custom-call(s32[3]{0:T(128)S(1)} %pad_add_fusion.place, bf16[32,4,1280]{2,1,0:T(4,128)(2,1)S(1)} %all_to_all.42.recv_ref, bf16[640,1920]{1,0:T(8,128)(2,1)S(1)} %copy-done, bf16[640,640]{1,0:T(8,128)(2,1)S(1)} %copy-done.3), custom_call_target="tpu_custom_call" | custom-call | flops 6000000000 | bytes 18000000 | tf_op jit(solution)/shard_map/pallas_call | solution.py:407
  66.5 1.3 collective-permute-start.2
  67.8 3.7 %all-to-all-start.3 = ((bf16[32,4,1280]{2,1,0:T(4,128)(2,1)}), bf16[32,4,1280]{2,1,0:T(4,128)(2,1)S(1)}, u32[]{:S(2)}, u32[]{:S(2)}) async-start(bf16[32,4,1280]{2,1,0:T(4,128)(2,1)} %get-tuple-element.68), calls=%async_computation.3 | async-start | bytes 655360 | tf_op jit(solution)/shard_map/all_to_all | solution.py:456
  71.4 0.0 collective-permute-done.2.recv_ref
  71.5 1.1 copy-done.22
  72.6 3.0 %shard_map.130 = (bf16[160,1280]{1,0:T(8,128)(2,1)S(1)}, bf16[160,1280]{1,0:T(8,128)(2,1)}, bf16[160,1280]{1,0:T(8,128)(2,1)}, bf16[160,1280]{1,0:T(8,128)(2,1)S(1)}) custom-call(s32[3]{0:T(128)S(1)} %pad_add_fusion.place, s32[17,1,640]{2,1,0:T(1,128)S(1)} %copy-done.16, bf16[128,2560]{1,0:T(8,128)(2,1)S(1)} %copy-done.22, ...), custom_call_target="tpu_custom_call" | custom-call | flops 3000000000 | bytes 9000000 | tf_op jit(solution)/shard_map/pallas_call | solution.py:407
  75.5 0.8 copy-done.19
  76.3 0.3 collective-permute-start.3
  76.6 1.8 %collective-permute-start.4 = (bf16[160,1280]{1,0:T(8,128)(2,1)}, bf16[160,1280]{1,0:T(8,128)(2,1)S(1)}, u32[]{:S(2)}, u32[]{:S(2)}) collective-permute-start(bf16[160,1280]{1,0:T(8,128)(2,1)} %get-tuple-element.72), channel_id=1, source_target_pairs={{0,2},{1,3},{2,0},{3,1},{4,6},{5,7},{6,4},{7,5},{8,10},{9,11},{10,... | collective-permute-start | bytes 1228808 | tf_op jit(solution)/shard_map/ppermute | solution.py:463
  78.3 0.8 collective-permute-start.5
  79.2 4.9 %all-to-all-done.3.back_ref = bf16[32,4,1280]{2,1,0:T(4,128)(2,1)S(1)} async-done(((bf16[32,4,1280]{2,1,0:T(4,128)(2,1)}), bf16[32,4,1280]{2,1,0:T(4,128)(2,1)S(1)}, u32[]{:S(2)}, u32[]{:S(2)}) %all-to-all-start.3) | async-done | bytes 327712 | tf_op jit(solution)/shard_map/all_to_all | solution.py:456
  84.1 1.0 copy-done.18
  85.1 0.6 shard_map.131
  85.6 12.6 %all_to_all.43.g_ref = f32[8,16,128]{2,1,0:T(8,128)S(1)} all-to-all(f32[8,16,128]{2,1,0:T(8,128)S(1)} %shard_map.131), channel_id=1, replica_groups=mesh['view'=2,'z'=8,'xl'=2,'core'=2,'dp'=4] {'view','dp'}, dimensions={0} | all-to-all | bytes 131072 | tf_op jit(solution)/shard_map/all_to_all | solution.py:453
  98.3 0.0 copy-start.15
  98.3 1.0 copy-done.15
  99.3 3.9 %shard_map.132 = (bf16[128,2560]{1,0:T(8,128)(2,1)S(1)}, bf16[128,2560]{1,0:T(8,128)(2,1)S(1)}, bf16[128,1920]{1,0:T(8,128)(2,1)S(1)}, f32[128,640]{1,0:T(8,128)...) custom-call(s32[3]{0:T(128)S(1)} %pad_add_fusion.place, bf16[32,4,1280]{2,1,0:T(4,128)(2,1)S(1)} %all-to-all-done.3.back_ref, ...), custom_call_target="tpu_custom_call" | custom-call | flops 5000000000 | bytes 15000000 | tf_op jit(solution)/shard_map/pallas_call | solution.py:407
  103.2 1.5 collective-permute-start.6
  104.7 1.8 %shard_map.133 = (f32[64,640]{1,0:T(8,128)S(1)}, bf16[64,640]{1,0:T(8,128)(2,1)S(1)}, bf16[64,1280]{1,0:T(8,128)(2,1)S(1)}, f32[16,128]{1,0:T(8,128)S(1)}) custom-call(s32[3]{0:T(128)S(1)} %pad_add_fusion.place, bf16[128,1920]{1,0:T(8,128)(2,1)S(1)} %get-tuple-element.86.pgrad_ref, f32[128,640]{1,0:T(8,128)S(1)} %get-tuple-element.87.stream_grad_ref, ...), custom_call_target="tpu_custom_call" | custom-call | flops 3000000000 | bytes 9000000 | tf_op jit(solution)/shard_map/pallas_call | solution.py:407
  106.5 0.0 copy-start.25
  106.5 0.0 copy-start.27
  106.5 0.0 collective-permute-done.6.recv_ref
  106.6 2.8 %shard_map.134 = bf16[640,1280]{1,0:T(8,128)(2,1)} custom-call(s32[17,1,640]{2,1,0:T(1,128)S(1)} %copy-done.16, bf16[128,2560]{1,0:T(8,128)(2,1)S(1)} %get-tuple-element.84.keep_ref, bf16[128,2560]{1,0:T(8,128)(2,1)S(1)} %collective-permute-done.6.recv_ref), custom_call_target="tpu_custom_call" | custom-call | flops 3000000000 | bytes 9000000 | tf_op jit(solution)/shard_map/pallas_call | solution.py:407
  109.4 5.0 %all-to-all-start.5 = ((bf16[16,40,1280]{2,1,0:T(8,128)(2,1)}), bf16[16,40,1280]{2,1,0:T(8,128)(2,1)S(1)}, u32[]{:S(2)}, u32[]{:S(2)}) async-start(bf16[16,40,1280]{2,1,0:T(8,128)(2,1)} %bitcast.3), calls=%async_computation.5 | async-start | bytes 3276800 | tf_op jit(solution)/shard_map/all_to_all | solution.py:502
  114.4 1.0 copy-done.20
  115.4 0.2 shard_map.135
  115.6 1.4 collective-permute-start.7
  117.0 2.4 %collective-permute-start.8 = (bf16[40,1280]{1,0:T(8,128)(2,1)S(1)}, bf16[40,1280]{1,0:T(8,128)(2,1)S(1)}, u32[]{:S(2)}, u32[]{:S(2)}) collective-permute-start(bf16[40,1280]{1,0:T(8,128)(2,1)S(1)} %get-tuple-element.98), channel_id=1, source_target_pairs={{0,128},{8,136},{128,0},{136,8},{1,129},{9,137},{129,1},{137,9},{2... | collective-permute-start | bytes 307208 | tf_op jit(solution)/shard_map/ppermute | solution.py:463
  119.4 1.2 collective-permute-start.9
  120.6 0.1 collective-permute-start.10
  120.7 19.4 %collective-permute-done.10 = f32[16,128]{1,0:T(8,128)S(1)} collective-permute-done((f32[16,128]{1,0:T(8,128)S(1)}, f32[16,128]{1,0:T(8,128)S(1)}, u32[]{:S(2)}, u32[]{:S(2)}) %collective-permute-start.10) | collective-permute-done | bytes 8224 | tf_op jit(solution)/shard_map/ppermute | solution.py:459
  140.2 0.0 collective-permute-done.9.refs_3_
  140.2 0.0 all-to-all-done.5
  140.2 1.2 shard_map.136
  141.4 6.5 %all-to-all-start.6 = ((bf16[8,4,3200]{2,1,0:T(4,128)(2,1)}), bf16[8,4,3200]{2,1,0:T(4,128)(2,1)S(1)}, u32[]{:S(2)}, u32[]{:S(2)}) async-start(bf16[8,4,3200]{2,1,0:T(4,128)(2,1)} %shard_map.136), calls=%async_computation.6 | async-start | bytes 409600 | tf_op jit(solution)/shard_map/all_to_all | solution.py:508
  147.9 1.2 collective-permute-start.11
  149.1 1.3 collective-permute-done.11
  150.4 2.4 %collective-permute-start.12 = (f32[16,128]{1,0:T(8,128)S(1)}, f32[16,128]{1,0:T(8,128)S(1)}, u32[]{:S(2)}, u32[]{:S(2)}) collective-permute-start(f32[16,128]{1,0:T(8,128)S(1)} %add.18), channel_id=1, source_target_pairs={{0,2},{1,3},{2,0},{3,1},{4,6},{5,7},{6,4},{7,5},{8,10},{9,11},{10,... | collective-permute-start | bytes 24584 | tf_op jit(solution)/shard_map/ppermute | solution.py:467
  152.9 1.6 collective-permute-done.12
  154.5 2.1 %all-to-all-done.6.parts_ref = bf16[8,4,3200]{2,1,0:T(4,128)(2,1)S(1)} async-done(((bf16[8,4,3200]{2,1,0:T(4,128)(2,1)}), bf16[8,4,3200]{2,1,0:T(4,128)(2,1)S(1)}, u32[]{:S(2)}, u32[]{:S(2)}) %all-to-all-start.6) | async-done | bytes 204832 | tf_op jit(solution)/shard_map/all_to_all | solution.py:508
  156.6 3.0 %collective-permute-start.14 = (bf16[4,3200]{1,0:T(4,128)(2,1)S(1)}, bf16[4,3200]{1,0:T(4,128)(2,1)S(1)}, u32[]{:S(2)}, u32[]{:S(2)}) collective-permute-start(bf16[4,3200]{1,0:T(4,128)(2,1)S(1)} %shard_map.138), channel_id=1, source_target_pairs={{0,4},{4,0},{1,5},{5,1},{2,6},{6,2},{3,7},{7,3},{8,12},{12,8},{9,1... | collective-permute-start | bytes 76808 | tf_op jit(solution)/shard_map/ppermute | solution.py:459
  159.7 1.3 collective-permute-start.13
  161.1 1.7 %collective-permute-start.15 = (bf16[8,3200]{1,0:T(8,128)(2,1)S(1)}, bf16[8,3200]{1,0:T(8,128)(2,1)S(1)}, u32[]{:S(2)}, u32[]{:S(2)}) collective-permute-start(bf16[8,3200]{1,0:T(8,128)(2,1)S(1)} %pad_maximum_fusion.near_ref), channel_id=1, source_target_pairs={{0,128},{128,0},{1,129},{129,1},{2,130},{130,2},{3,131},{131,3},{4... | collective-permute-start | bytes 153608 | tf_op jit(solution)/shard_map/ppermute | solution.py:459
  162.8 4.1 %collective-permute-done.13.recv_ref = bf16[64,1280]{1,0:T(8,128)(2,1)S(1)} collective-permute-done((bf16[64,1280]{1,0:T(8,128)(2,1)S(1)}, bf16[64,1280]{1,0:T(8,128)(2,1)S(1)}, u32[]{:S(2)}, u32[]{:S(2)}) %collective-permute-start.13) | collective-permute-done | bytes 163872 | tf_op jit(solution)/shard_map/ppermute | solution.py:459
  167.0 1.6 shard_map.137
  168.6 1.2 shard_map.139
  (58 shorter events, 0.2 us)
Async XLA Ops:
  0.6 17.5 %collective-permute-start = (bf16[4,1,32,640]{3,2,1,0:T(8,128)(2,1)}, bf16[4,1,32,640]{3,2,1,0:T(8,128)(2,1)S(1)}, u32[]{:S(2)}, u32[]{:S(2)}) collective-permute-start(bf16[4,1,32,640]{3,2,1,0:T(8,128)(2,1)} %x_ref.7), channel_id=1, source_target_pairs={{0,128},{128,0},{1,129},{129,1},{2,130},{130,2},{3,131},{131,3},{4... | collective-permute-start | bytes 491528 | tf_op jit(solution)/shard_map/ppermute | solution.py:459
  4.4 0.9 copy-start.8
  5.3 6.1 %copy-start.7 = (bf16[4,1,32,640]{3,2,1,0:T(8,128)(2,1)S(1)}, bf16[4,1,32,640]{3,2,1,0:T(8,128)(2,1)}, u32[]{:S(2)}) copy-start(bf16[4,1,32,640]{3,2,1,0:T(8,128)(2,1)} %og_ref.1) | copy-start | bytes 491524
  5.3 12.8 %copy-start.4 = (bf16[640,640]{1,0:T(8,128)(2,1)S(1)}, bf16[640,640]{1,0:T(8,128)(2,1)}, u32[]{:S(2)}) copy-start(bf16[640,640]{1,0:T(8,128)(2,1)} %wout_ref.5) | copy-start | bytes 2457604
  5.3 12.8 %copy-start.9 = (bf16[4,1,32,640]{3,2,1,0:T(8,128)(2,1)S(1)}, bf16[4,1,32,640]{3,2,1,0:T(8,128)(2,1)}, u32[]{:S(2)}) copy-start(bf16[4,1,32,640]{3,2,1,0:T(8,128)(2,1)} %x_ref.7) | copy-start | bytes 491524
  7.2 10.9 %all-to-all-start = ((f32[8,16,128]{2,1,0:T(8,128)}), f32[8,16,128]{2,1,0:T(8,128)S(1)}, u32[]{:S(2)}, u32[]{:S(2)}) async-start(f32[8,16,128]{2,1,0:T(8,128)} %shard_map.126), calls=%async_computation | async-start | bytes 131072 | tf_op jit(solution)/shard_map/all_to_all | solution.py:453
  11.4 16.0 %collective-permute-start.1 = (bf16[4,1,32,640]{3,2,1,0:T(8,128)(2,1)S(1)}, bf16[4,1,32,640]{3,2,1,0:T(8,128)(2,1)S(1)}, u32[]{:S(2)}, u32[]{:S(2)}) collective-permute-start(bf16[4,1,32,640]{3,2,1,0:T(8,128)(2,1)S(1)} %copy-done.7), channel_id=1, source_target_pairs={{0,128},{128,0},{1,129},{129,1},{2,130},{130,2},{3,131},{131,3},{4... | collective-permute-start | bytes 491528 | tf_op jit(solution)/shard_map/ppermute | solution.py:459
  18.1 1.7 copy-start.1
  19.8 3.4 %copy-start.12 = (bf16[4,1,32,640]{3,2,1,0:T(8,128)(2,1)}, bf16[4,1,32,640]{3,2,1,0:T(8,128)(2,1)S(1)}, u32[]{:S(2)}) copy-start(bf16[4,1,32,640]{3,2,1,0:T(8,128)(2,1)S(1)} %collective-permute-done.other_ref) | copy-start | bytes 491524
  23.2 0.9 copy-start.23
  24.0 10.9 %copy-start.17 = (f32[128,640]{1,0:T(8,128)}, f32[128,640]{1,0:T(8,128)S(1)}, u32[]{:S(2)}) copy-start(f32[128,640]{1,0:T(8,128)S(1)} %get-tuple-element.65.stream_ref) | copy-start | bytes 983044
  24.0 10.0 %all-to-all-start.1 = ((f32[8,16,128]{2,1,0:T(8,128)}), f32[8,16,128]{2,1,0:T(8,128)S(1)}, u32[]{:S(2)}, u32[]{:S(2)}) async-start(f32[8,16,128]{2,1,0:T(8,128)} %get-tuple-element.66), calls=%async_computation.1 | async-start | bytes 131072 | tf_op jit(solution)/shard_map/all_to_all | solution.py:453
  27.4 7.5 %copy-start.14 = (bf16[4,1,32,640]{3,2,1,0:T(8,128)(2,1)}, bf16[4,1,32,640]{3,2,1,0:T(8,128)(2,1)S(1)}, u32[]{:S(2)}) copy-start(bf16[4,1,32,640]{3,2,1,0:T(8,128)(2,1)S(1)} %collective-permute-done.1.other_ref.ogother_ref) | copy-start | bytes 491524
  34.0 26.9 %copy-start = (bf16[640,1920]{1,0:T(8,128)(2,1)S(1)}, bf16[640,1920]{1,0:T(8,128)(2,1)}, u32[]{:S(2)}) copy-start(bf16[640,1920]{1,0:T(8,128)(2,1)} %wqkv_ref.4) | copy-start | bytes 7372804
  34.0 26.9 %copy-start.3 = (bf16[640,640]{1,0:T(8,128)(2,1)S(1)}, bf16[640,640]{1,0:T(8,128)(2,1)}, u32[]{:S(2)}) copy-start(bf16[640,640]{1,0:T(8,128)(2,1)} %wout_ref.4) | copy-start | bytes 2457604
  60.9 10.6 %copy-start.16 = (s32[17,1,640]{2,1,0:T(1,128)S(1)}, s32[17,1,640]{2,1,0:T(1,128)}, u32[]{:S(2)}) copy-start(s32[17,1,640]{2,1,0:T(1,128)} %constant.24.clone.table_ref) | copy-start | bytes 130564
  66.5 5.0 %copy-start.21 = (bf16[128,2560]{1,0:T(8,128)(2,1)}, bf16[128,2560]{1,0:T(8,128)(2,1)S(1)}, u32[]{:S(2)}) copy-start(bf16[128,2560]{1,0:T(8,128)(2,1)S(1)} %get-tuple-element.69.keep_ref) | copy-start | bytes 1966084
  66.5 4.9 %collective-permute-start.2 = (bf16[128,2560]{1,0:T(8,128)(2,1)S(1)}, bf16[128,2560]{1,0:T(8,128)(2,1)S(1)}, u32[]{:S(2)}, u32[]{:S(2)}) collective-permute-start(bf16[128,2560]{1,0:T(8,128)(2,1)S(1)} %get-tuple-element.70), channel_id=1, source_target_pairs={{0,4},{4,0},{1,5},{5,1},{2,6},{6,2},{3,7},{7,3},{8,12},{12,8},{9,1... | collective-permute-start | bytes 1966088 | tf_op jit(solution)/shard_map/ppermute | solution.py:459
  67.8 16.3 %all-to-all-start.3 = ((bf16[32,4,1280]{2,1,0:T(4,128)(2,1)}), bf16[32,4,1280]{2,1,0:T(4,128)(2,1)S(1)}, u32[]{:S(2)}, u32[]{:S(2)}) async-start(bf16[32,4,1280]{2,1,0:T(4,128)(2,1)} %get-tuple-element.68), calls=%async_computation.3 | async-start | bytes 655360 | tf_op jit(solution)/shard_map/all_to_all | solution.py:456
  71.5 1.1 copy-start.22
  75.5 0.8 copy-start.19
  76.3 22.0 %copy-start.10 = (bf16[4,1,32,640]{3,2,1,0:T(8,128)(2,1)S(1)}, bf16[4,1,32,640]{3,2,1,0:T(8,128)(2,1)}, u32[]{:S(2)}) copy-start(bf16[4,1,32,640]{3,2,1,0:T(8,128)(2,1)} %x_ref.7) | copy-start | bytes 491524
  76.3 22.0 %copy-start.13 = (bf16[4,1,32,640]{3,2,1,0:T(8,128)(2,1)S(1)}, bf16[4,1,32,640]{3,2,1,0:T(8,128)(2,1)}, u32[]{:S(2)}) copy-start(bf16[4,1,32,640]{3,2,1,0:T(8,128)(2,1)} %copy-done.12) | copy-start | bytes 491524
  76.3 21.9 %collective-permute-start.3 = (bf16[160,1280]{1,0:T(8,128)(2,1)}, bf16[160,1280]{1,0:T(8,128)(2,1)S(1)}, u32[]{:S(2)}, u32[]{:S(2)}) collective-permute-start(bf16[160,1280]{1,0:T(8,128)(2,1)} %get-tuple-element.71), channel_id=1, source_target_pairs={{0,1},{1,2},{2,3},{3,0},{4,5},{5,6},{6,7},{7,4},{8,9},{9,10},{10,1... | collective-permute-start | bytes 1228808 | tf_op jit(solution)/shard_map/ppermute | solution.py:463
  76.6 21.6 %collective-permute-start.4 = (bf16[160,1280]{1,0:T(8,128)(2,1)}, bf16[160,1280]{1,0:T(8,128)(2,1)S(1)}, u32[]{:S(2)}, u32[]{:S(2)}) collective-permute-start(bf16[160,1280]{1,0:T(8,128)(2,1)} %get-tuple-element.72), channel_id=1, source_target_pairs={{0,2},{1,3},{2,0},{3,1},{4,6},{5,7},{6,4},{7,5},{8,10},{9,11},{10,... | collective-permute-start | bytes 1228808 | tf_op jit(solution)/shard_map/ppermute | solution.py:463
  78.3 19.9 %collective-permute-start.5 = (bf16[160,1280]{1,0:T(8,128)(2,1)S(1)}, bf16[160,1280]{1,0:T(8,128)(2,1)S(1)}, u32[]{:S(2)}, u32[]{:S(2)}) collective-permute-start(bf16[160,1280]{1,0:T(8,128)(2,1)S(1)} %get-tuple-element.73), channel_id=1, source_target_pairs={{0,3},{1,0},{2,1},{3,2},{4,7},{5,4},{6,5},{7,6},{8,11},{9,8},{10,9... | collective-permute-start | bytes 1228808 | tf_op jit(solution)/shard_map/ppermute | solution.py:463
  84.1 1.0 copy-start.18
  85.1 13.2 %copy-start.24 = (bf16[128,2560]{1,0:T(8,128)(2,1)S(1)}, bf16[128,2560]{1,0:T(8,128)(2,1)}, u32[]{:S(2)}) copy-start(bf16[128,2560]{1,0:T(8,128)(2,1)} %copy-done.23) | copy-start | bytes 1966084
  98.2 5.0 %copy-start.5 = (bf16[160,1280]{1,0:T(8,128)(2,1)}, bf16[160,1280]{1,0:T(8,128)(2,1)S(1)}, u32[]{:S(2)}) copy-start(bf16[160,1280]{1,0:T(8,128)(2,1)S(1)} %collective-permute-done.5.refs_3_) | copy-start | bytes 1228804
  98.3 1.0 copy-start.15
  99.3 5.4 %copy-start.2 = (bf16[640,1920]{1,0:T(8,128)(2,1)S(1)}, bf16[640,1920]{1,0:T(8,128)(2,1)}, u32[]{:S(2)}) copy-start(bf16[640,1920]{1,0:T(8,128)(2,1)} %wqkv_ref.5) | copy-start | bytes 7372804
  103.2 3.3 %collective-permute-start.6 = (bf16[128,2560]{1,0:T(8,128)(2,1)S(1)}, bf16[128,2560]{1,0:T(8,128)(2,1)S(1)}, u32[]{:S(2)}, u32[]{:S(2)}) collective-permute-start(bf16[128,2560]{1,0:T(8,128)(2,1)S(1)} %get-tuple-element.85), channel_id=1, source_target_pairs={{0,4},{4,0},{1,5},{5,1},{2,6},{6,2},{3,7},{7,3},{8,12},{12,8},{9,1... | collective-permute-start | bytes 1966088 | tf_op jit(solution)/shard_map/ppermute | solution.py:459
  106.5 2.9 %copy-start.25 = (f32[64,640]{1,0:T(8,128)}, f32[64,640]{1,0:T(8,128)S(1)}, u32[]{:S(2)}) copy-start(f32[64,640]{1,0:T(8,128)S(1)} %get-tuple-element.112.ukeep_ref) | copy-start | bytes 491524
  106.5 2.9 %copy-start.27 = (bf16[64,640]{1,0:T(8,128)(2,1)}, bf16[64,640]{1,0:T(8,128)(2,1)S(1)}, u32[]{:S(2)}) copy-start(bf16[64,640]{1,0:T(8,128)(2,1)S(1)} %get-tuple-element.113.okeep_ref) | copy-start | bytes 245764
  109.4 5.0 %copy-start.6 = (bf16[160,1280]{1,0:T(8,128)(2,1)S(1)}, bf16[160,1280]{1,0:T(8,128)(2,1)}, u32[]{:S(2)}) copy-start(bf16[160,1280]{1,0:T(8,128)(2,1)} %copy-done.5) | copy-start | bytes 1228804
  109.4 30.8 %all-to-all-start.5 = ((bf16[16,40,1280]{2,1,0:T(8,128)(2,1)}), bf16[16,40,1280]{2,1,0:T(8,128)(2,1)S(1)}, u32[]{:S(2)}, u32[]{:S(2)}) async-start(bf16[16,40,1280]{2,1,0:T(8,128)(2,1)} %bitcast.3), calls=%async_computation.5 | async-start | bytes 3276800 | tf_op jit(solution)/shard_map/all_to_all | solution.py:502
  114.4 1.0 copy-start.20
  115.6 24.6 %collective-permute-start.7 = (bf16[40,1280]{1,0:T(8,128)(2,1)S(1)}, bf16[40,1280]{1,0:T(8,128)(2,1)S(1)}, u32[]{:S(2)}, u32[]{:S(2)}) collective-permute-start(bf16[40,1280]{1,0:T(8,128)(2,1)S(1)} %get-tuple-element.97), channel_id=1, source_target_pairs={{0,8},{8,128},{128,136},{136,0},{1,9},{9,129},{129,137},{137,1},{2... | collective-permute-start | bytes 307208 | tf_op jit(solution)/shard_map/ppermute | solution.py:463
  117.0 23.1 %collective-permute-start.8 = (bf16[40,1280]{1,0:T(8,128)(2,1)S(1)}, bf16[40,1280]{1,0:T(8,128)(2,1)S(1)}, u32[]{:S(2)}, u32[]{:S(2)}) collective-permute-start(bf16[40,1280]{1,0:T(8,128)(2,1)S(1)} %get-tuple-element.98), channel_id=1, source_target_pairs={{0,128},{8,136},{128,0},{136,8},{1,129},{9,137},{129,1},{137,9},{2... | collective-permute-start | bytes 307208 | tf_op jit(solution)/shard_map/ppermute | solution.py:463
  119.4 20.7 %collective-permute-start.9 = (bf16[40,1280]{1,0:T(8,128)(2,1)S(1)}, bf16[40,1280]{1,0:T(8,128)(2,1)S(1)}, u32[]{:S(2)}, u32[]{:S(2)}) collective-permute-start(bf16[40,1280]{1,0:T(8,128)(2,1)S(1)} %get-tuple-element.99), channel_id=1, source_target_pairs={{0,136},{8,0},{128,8},{136,128},{1,137},{9,1},{129,9},{137,129},{2... | collective-permute-start | bytes 307208 | tf_op jit(solution)/shard_map/ppermute | solution.py:463
  120.6 19.5 %collective-permute-start.10 = (f32[16,128]{1,0:T(8,128)S(1)}, f32[16,128]{1,0:T(8,128)S(1)}, u32[]{:S(2)}, u32[]{:S(2)}) collective-permute-start(f32[16,128]{1,0:T(8,128)S(1)} %get-tuple-element.100), channel_id=1, source_target_pairs={{0,128},{128,0},{1,129},{129,1},{2,130},{130,2},{3,131},{131,3},{4... | collective-permute-start | bytes 24584 | tf_op jit(solution)/shard_map/ppermute | solution.py:459
  141.4 15.2 %all-to-all-start.6 = ((bf16[8,4,3200]{2,1,0:T(4,128)(2,1)}), bf16[8,4,3200]{2,1,0:T(4,128)(2,1)S(1)}, u32[]{:S(2)}, u32[]{:S(2)}) async-start(bf16[8,4,3200]{2,1,0:T(4,128)(2,1)} %shard_map.136), calls=%async_computation.6 | async-start | bytes 409600 | tf_op jit(solution)/shard_map/all_to_all | solution.py:508
  147.9 2.5 %collective-permute-start.11 = (f32[16,128]{1,0:T(8,128)S(1)}, f32[16,128]{1,0:T(8,128)S(1)}, u32[]{:S(2)}, u32[]{:S(2)}) collective-permute-start(f32[16,128]{1,0:T(8,128)S(1)} %add.17), channel_id=1, source_target_pairs={{0,1},{1,0},{2,3},{3,2},{4,5},{5,4},{6,7},{7,6},{8,9},{9,8},{10,11... | collective-permute-start | bytes 24584 | tf_op jit(solution)/shard_map/ppermute | solution.py:467
  150.4 4.1 %collective-permute-start.12 = (f32[16,128]{1,0:T(8,128)S(1)}, f32[16,128]{1,0:T(8,128)S(1)}, u32[]{:S(2)}, u32[]{:S(2)}) collective-permute-start(f32[16,128]{1,0:T(8,128)S(1)} %add.18), channel_id=1, source_target_pairs={{0,2},{1,3},{2,0},{3,1},{4,6},{5,7},{6,4},{7,5},{8,10},{9,11},{10,... | collective-permute-start | bytes 24584 | tf_op jit(solution)/shard_map/ppermute | solution.py:467
  154.5 12.4 %copy-start.11 = (bf16[4,1,32,640]{3,2,1,0:T(8,128)(2,1)S(1)}, bf16[4,1,32,640]{3,2,1,0:T(8,128)(2,1)}, u32[]{:S(2)}) copy-start(bf16[4,1,32,640]{3,2,1,0:T(8,128)(2,1)} %x_ref.7) | copy-start | bytes 491524
  154.5 12.4 %copy-start.26 = (f32[64,640]{1,0:T(8,128)S(1)}, f32[64,640]{1,0:T(8,128)}, u32[]{:S(2)}) copy-start(f32[64,640]{1,0:T(8,128)} %copy-done.25) | copy-start | bytes 491524
  154.5 12.4 %copy-start.28 = (bf16[64,640]{1,0:T(8,128)(2,1)S(1)}, bf16[64,640]{1,0:T(8,128)(2,1)}, u32[]{:S(2)}) copy-start(bf16[64,640]{1,0:T(8,128)(2,1)} %copy-done.27) | copy-start | bytes 245764
  156.6 4.4 %collective-permute-start.14 = (bf16[4,3200]{1,0:T(4,128)(2,1)S(1)}, bf16[4,3200]{1,0:T(4,128)(2,1)S(1)}, u32[]{:S(2)}, u32[]{:S(2)}) collective-permute-start(bf16[4,3200]{1,0:T(4,128)(2,1)S(1)} %shard_map.138), channel_id=1, source_target_pairs={{0,4},{4,0},{1,5},{5,1},{2,6},{6,2},{3,7},{7,3},{8,12},{12,8},{9,1... | collective-permute-start | bytes 76808 | tf_op jit(solution)/shard_map/ppermute | solution.py:459
  159.7 7.3 %collective-permute-start.13 = (bf16[64,1280]{1,0:T(8,128)(2,1)S(1)}, bf16[64,1280]{1,0:T(8,128)(2,1)S(1)}, u32[]{:S(2)}, u32[]{:S(2)}) collective-permute-start(bf16[64,1280]{1,0:T(8,128)(2,1)S(1)} %get-tuple-element.114), channel_id=1, source_target_pairs={{0,128},{128,0},{1,129},{129,1},{2,130},{130,2},{3,131},{131,3},{4... | collective-permute-start | bytes 491528 | tf_op jit(solution)/shard_map/ppermute | solution.py:459
  161.1 7.5 %collective-permute-start.15 = (bf16[8,3200]{1,0:T(8,128)(2,1)S(1)}, bf16[8,3200]{1,0:T(8,128)(2,1)S(1)}, u32[]{:S(2)}, u32[]{:S(2)}) collective-permute-start(bf16[8,3200]{1,0:T(8,128)(2,1)S(1)} %pad_maximum_fusion.near_ref), channel_id=1, source_target_pairs={{0,128},{128,0},{1,129},{129,1},{2,130},{130,2},{3,131},{131,3},{4... | collective-permute-start | bytes 153608 | tf_op jit(solution)/shard_map/ppermute | solution.py:459

commit v3 on v2

--- a/solution.py
+++ b/solution.py
@@ -116,42 +116,48 @@
     return ((row ^ col) & (period - 1)) == 0
 
 
-def softmax_pair(stacked_q, keys, allowed):
-    scores = jnp.where(allowed, mm_t(stacked_q, keys) * SCALE, -1e30)
+def softmax_all(stacked_q, keys, allowed):
+    scores = jnp.concatenate([mm_t(q, k) for q, k in zip(stacked_q, keys)], axis=0)
+    allowed = jnp.concatenate([allowed] * len(keys), axis=0)
+    scores = jnp.where(allowed, scores * SCALE, -1e30)
     top = jnp.max(scores, axis=-1, keepdims=True)
     weights = jnp.exp(scores - top)
-    return weights / jnp.sum(weights, axis=-1, keepdims=True)
+    return weights * (1.0 / jnp.sum(weights, axis=-1, keepdims=True))
 
 
 def pair_of(index):
     return slice(index * 128, (index + 1) * 128)
 
 
+def pieces_of(packed, first):
+    return [packed[:, pair_of(first + pair)] for pair in range(HEADS // 2)]
+
+
+def rows_of(stacked, pair):
+    return stacked[pair * 2 * T : (pair + 1) * 2 * T]
+
+
 def attend(packed, allowed):
-    outs = []
-    for pair in range(HEADS // 2):
-        q = both_heads(packed[:, pair_of(pair)])
-        k = packed[:, pair_of(pair + 5)]
-        v = packed[:, pair_of(pair + 10)]
-        prob = softmax_pair(q, k, allowed).astype(BF16)
-        outs.append(join_heads(mm(prob, v)).astype(BF16))
-    return jnp.concatenate(outs, axis=1)
-
-
-def attend_back(grad, packed, allowed):
-    dqs, dks, dvs = [], [], []
-    for pair in range(HEADS // 2):
-        q = both_heads(packed[:, pair_of(pair)])
-        k = packed[:, pair_of(pair + 5)]
-        v = packed[:, pair_of(pair + 10)]
-        g = both_heads(grad[:, pair_of(pair)])
-        prob = softmax_pair(q, k, allowed)
-        dvs.append(t_mm(prob.astype(BF16), g).astype(BF16))
-        dprob = mm_t(g, v)
-        dscore = prob * (dprob - jnp.sum(dprob * prob, axis=-1, keepdims=True))
-        dscore = (dscore * SCALE).astype(BF16)
-        dqs.append(join_heads(mm(dscore, k)).astype(BF16))
-        dks.append(t_mm(dscore, q).astype(BF16))
+    q, k, v = [both_heads(piece) for piece in pieces_of(packed, 0)], pieces_of(packed, 5), pieces_of(packed, 10)
+    prob = softmax_all(q, k, allowed)
+    rounded = prob.astype(BF16)
+    outs = [join_heads(mm(rows_of(rounded, pair), v[pair])).astype(BF16) for pair in range(HEADS // 2)]
+    return jnp.concatenate(outs, axis=1), prob
+
+
+def attend_back(grad, packed, allowed, prob=None):
+    q, k, v = [both_heads(piece) for piece in pieces_of(packed, 0)], pieces_of(packed, 5), pieces_of(packed, 10)
+    g = [both_heads(piece) for piece in pieces_of(grad, 0)]
+    if prob is None:
+        prob = softmax_all(q, k, allowed)
+    rounded = prob.astype(BF16)
+    dprob = jnp.concatenate([mm_t(x, y) for x, y in zip(g, v)], axis=0)
+    dscore = prob * (dprob - jnp.sum(dprob * prob, axis=-1, keepdims=True))
+    dscore = (dscore * SCALE).astype(BF16)
+    pairs = range(HEADS // 2)
+    dvs = [t_mm(rows_of(rounded, pair), g[pair]).astype(BF16) for pair in pairs]
+    dqs = [join_heads(mm(rows_of(dscore, pair), k[pair])).astype(BF16) for pair in pairs]
+    dks = [t_mm(rows_of(dscore, pair), q[pair]).astype(BF16) for pair in pairs]
     return jnp.concatenate(dqs + dks + dvs, axis=1)
 
 
@@ -177,7 +183,7 @@
     return (x - per_token(channels[:VIEWS])) * per_token(channels[VIEWS:])
 
 
-def k_view(entries, place, x_ref, other_ref, g_ref, wqkv_ref, wout_ref, stream_ref, saved_ref, own_ref, stats_ref):
+def k_view(entries, place, x_ref, other_ref, g_ref, wqkv_ref, wout_ref, stream_ref, saved_ref, sides_ref, own_ref, stats_ref):
     first = place[0] == 0
     member = group_matrix()
     sources = g_ref.shape[0]
@@ -193,10 +199,12 @@
     rows = jnp.concatenate([low[0], high[0], low[1], high[1]], axis=0)
     own_ref[...] = rows
     x = regrouped(x_ref, other_ref, first).astype(F32)
-    packed = mm(normalized(x, rows, member).astype(BF16), wqkv_ref[...]).astype(BF16)
-    saved_ref[:, : 3 * D] = packed
-    mixed = attend(packed, same_sequence(PX))
-    saved_ref[:, 3 * D :] = mixed
+    hidden = normalized(x, rows, member).astype(BF16)
+    packed = mm(hidden, wqkv_ref[...]).astype(BF16)
+    saved_ref[...] = packed
+    mixed, _ = attend(packed, same_sequence(PX))
+    sides_ref[:, :D] = hidden
+    sides_ref[:, D:] = mixed
     stream = x + mm(mixed, wout_ref[...])
     stream_ref[...] = stream
     spread_out(stats_ref, partial_stats(stream, member))
@@ -217,13 +225,18 @@
 
 def weight_sides(core, hidden, mixed, packed_grad, grad, keep_ref, give_ref):
     first = core == 0
-    quarter = packed_grad[:, :D], packed_grad[:, D : 2 * D], packed_grad[:, 2 * D :], grad
     keep_ref[:, :D] = hidden
     give_ref[:, :D] = hidden
     keep_ref[:, D : 2 * D] = jnp.where(first, hidden, mixed)
     give_ref[:, D : 2 * D] = jnp.where(first, mixed, hidden)
+    right_sides(core, packed_grad, grad, keep_ref, give_ref, 2 * D)
+
+
+def right_sides(core, packed_grad, grad, keep_ref, give_ref, start=0):
+    first = core == 0
+    quarter = packed_grad[:, :D], packed_grad[:, D : 2 * D], packed_grad[:, 2 * D :], grad
     for slot in range(2):
-        cols = slice((2 + slot) * D, (3 + slot) * D)
+        cols = slice(start + slot * D, start + (slot + 1) * D)
         keep_ref[:, cols] = jnp.where(first, quarter[slot], quarter[2 + slot])
         give_ref[:, cols] = jnp.where(first, quarter[2 + slot], quarter[slot])
 
@@ -233,53 +246,50 @@
     grad = recv_ref[:, :, D:].reshape(T, D)
     allowed = same_sequence(recv_ref.shape[1])
     packed = mm(hidden, wqkv_ref[...]).astype(BF16)
-    mixed = attend(packed, allowed)
+    mixed, probs = attend(packed, allowed)
     shape = back_ref.shape[:2] + (D,)
     back_ref[:, :, :D] = mm(mixed, wout_ref[...]).astype(BF16).reshape(shape)
-    packed_grad = attend_back(mm_t(grad, wout_ref[...]).astype(BF16), packed, allowed)
+    packed_grad = attend_back(mm_t(grad, wout_ref[...]).astype(BF16), packed, allowed, probs)
     back_ref[:, :, D:] = mm_t(packed_grad, wqkv_ref[...]).astype(BF16).reshape(shape)
     weight_sides(place[1], hidden, mixed, packed_grad, grad, keep_ref, give_ref)
 
 
 def k_back_stats(back_ref, stream_ref, rows_ref, stats_ref):
     member = group_matrix()
-    normed = normalized(stream_ref[...], rows_ref[...], member)
     grad = back_ref[:, :, D:].reshape(T, D).astype(F32)
-    spread_out(stats_ref, both_sums(grad, normed, member))
-
-
-def k_view_back(entries, place, back_ref, stream_ref, rows_ref, g_ref, og_ref, ogother_ref, x_ref, other_ref, own_ref,
-                saved_ref, wout_ref, keep_ref, give_ref, pgrad_ref, stream_grad_ref, normed_ref, sums_ref):
+    spread_out(stats_ref, both_sums(grad, normalized(stream_ref[...], rows_ref[...], member), member))
+
+
+def k_view_back(entries, place, back_ref, stream_ref, rows_ref, g_ref, og_ref, ogother_ref, packed_ref, wout_ref,
+                keep_ref, give_ref, pgrad_ref, stream_grad_ref, sums_ref):
     first = place[0] == 0
     member = group_matrix()
     sums = g_ref[0]
     for s in range(1, g_ref.shape[0]):
         sums = sums + g_ref[s]
     sums_ref[...] = sums
-    channels = to_channels(jnp.concatenate([sums * (1.0 / entries), rows_ref[...], own_ref[...]], axis=0), member)
-    m1, m2, mean, inverse, mean_one, inverse_one = (
-        per_token(channels[k * VIEWS : (k + 1) * VIEWS]) for k in range(6)
-    )
+    channels = to_channels(jnp.concatenate([sums * (1.0 / entries), rows_ref[...]], axis=0), member)
+    m1, m2, mean, inverse = (per_token(channels[k * VIEWS : (k + 1) * VIEWS]) for k in range(4))
     normed_two = (stream_ref[...] - mean) * inverse
     ghid = back_ref[:, :, D:].reshape(T, D).astype(F32)
     grad_stream = regrouped(og_ref, ogother_ref, first).astype(F32) + inverse * (ghid - m1 - normed_two * m2)
     stream_grad_ref[...] = grad_stream
     grad_b = grad_stream.astype(BF16)
-    packed_grad = attend_back(mm_t(grad_b, wout_ref[...]).astype(BF16), saved_ref[:, : 3 * D], same_sequence(PX))
+    packed_grad = attend_back(mm_t(grad_b, wout_ref[...]).astype(BF16), packed_ref[...], same_sequence(PX))
     pgrad_ref[...] = packed_grad
-    normed = (regrouped(x_ref, other_ref, first).astype(F32) - mean_one) * inverse_one
-    normed_ref[...] = normed
-    weight_sides(place[1], normed.astype(BF16), saved_ref[:, 3 * D :], packed_grad, grad_b, keep_ref, give_ref)
-
-
-def k_view_stats(place, pgrad_ref, stream_grad_ref, back_ref, stream_ref, none_ref, own_ref, wqkv_ref,
+    right_sides(place[1], packed_grad, grad_b, keep_ref, give_ref)
+
+
+def k_view_stats(place, pgrad_ref, stream_grad_ref, back_ref, stream_ref, x_ref, other_ref, own_ref, wqkv_ref,
                  ukeep_ref, okeep_ref, send_ref, stats_ref):
     first = place[0] == 0
     member = group_matrix()
     grad = mm_t(pgrad_ref[...], wqkv_ref[...]).astype(BF16).astype(F32)
-    stats = both_sums(grad, none_ref[...], member)
-    stats_ref[...] = stats
-    partly = stream_grad_ref[...] + per_token(to_channels(own_ref[VIEWS:, :], member)) * grad
+    channels = to_channels(own_ref[...], member)
+    mean, inverse = per_token(channels[:VIEWS]), per_token(channels[VIEWS:])
+    normed = (regrouped(x_ref, other_ref, first).astype(F32) - mean) * inverse
+    stats_ref[...] = both_sums(grad, normed, member)
+    partly = stream_grad_ref[...] + inverse * grad
     temporal = back_ref[:, :, :D].reshape(T, D).astype(F32)
     out = (stream_ref[...] + temporal).astype(BF16)
     ukeep_ref[...] = jnp.where(first, partly[:HALF], partly[HALF:])
@@ -353,13 +363,24 @@
 def k_weights_time(place, table_ref, keep_ref, recv_ref, *out_refs):
     places = table_ref[place[2]]
     for unit in range(2):
-        split_rows(weight_tile(unit, places, keep_ref, recv_ref), out_refs, slice(unit * D, (unit + 1) * D))
-
-
-def k_weights_view(table_ref, keep_ref, recv_ref, out_ref):
-    places = table_ref[table_ref.shape[0] - 1]
+        total = weight_tile(unit, places, keep_ref, recv_ref)
+        split_rows(total, out_refs, slice(unit * D, (unit + 1) * D))
+
+
+def k_left_sides(place, column_ref, mine_ref, theirs_ref, left_ref):
+    first = place[1] == 0
+    order = (lax.broadcasted_iota(jnp.int32, (D, D), 1) == column_ref[...]).astype(BF16)
+    hidden = jnp.concatenate([mine_ref[:, :D], theirs_ref[:, :D]], axis=0)
+    mixed = jnp.concatenate([mine_ref[:, D:], theirs_ref[:, D:]], axis=0)
+    left_ref[0] = mm_t(order, hidden).astype(BF16)
+    left_ref[1] = mm_t(order, jnp.where(first, hidden, mixed)).astype(BF16)
+
+
+def k_weights_view(left_ref, mine_ref, theirs_ref, out_ref):
     for unit in range(2):
-        out_ref[:, unit * D : (unit + 1) * D] = weight_tile(unit, places, keep_ref, recv_ref)
+        cols = slice(unit * D, (unit + 1) * D)
+        right = jnp.concatenate([mine_ref[:, cols], theirs_ref[:, cols]], axis=0)
+        out_ref[:, cols] = mm(left_ref[unit], right).astype(BF16)
 
 
 def k_sum_time(*refs):
@@ -414,7 +435,7 @@
     )(*args)
 
 
-def row_table(z, xl, core, dp):
+def row_tables(z, xl, core, dp):
     rows = D // (z * xl * core * dp)
     ring = core * xl
     chip = np.arange(z).reshape(1, 1, 1, z)
@@ -428,8 +449,12 @@
         for me_dp in range(dp):
             y, x = (me_dp + np.arange(dp)) % dp, (me_x + np.arange(ring)) % ring
             table.append(place(y.reshape(dp, 1, 1, 1), x.reshape(1, ring, 1, 1)))
-    table.append(place(np.arange(dp).reshape(1, dp, 1, 1), np.arange(ring).reshape(ring, 1, 1, 1)))
-    return np.stack(table).astype(np.int32)
+    absolute = place(np.arange(dp).reshape(1, dp, 1, 1), np.arange(ring).reshape(ring, 1, 1, 1))
+    return np.stack(table).astype(np.int32), absolute.reshape(-1, 1).astype(np.int32)
+
+
+def view_rows(*sizes):
+    return row_tables(*sizes)[1]
 
 
 def body(sizes, level_in, out_grad, view_qkv, view_out, time_qkv, time_out):
@@ -441,7 +466,7 @@
     group = 2 * dp
     spot = (lax.axis_index("view") * xl + lax.axis_index("xl")) * dp + lax.axis_index("dp")
     place = jnp.stack([lax.axis_index("view"), lax.axis_index("core"), spot]).astype(jnp.int32)
-    table = jnp.asarray(row_table(z, xl, core, dp))
+    table = jnp.asarray(row_tables(z, xl, core, dp)[0])
     rows = D // (z * xl * core * dp)
     stats = ((group, 2 * VIEWS, 128), F32)
     tok32, tok16 = ((T, D), F32), ((T, D), BF16)
@@ -470,45 +495,43 @@
     rows16 = ((2 * VIEWS, 128), F32)
     x_other, og_other = swap(level_in, "view"), swap(out_grad, "view")
     (st1,) = call(k_first_stats, [stats], level_in, place=place)
-    stream, saved, own, st2 = call(
-        functools.partial(k_view, entries), [tok32, wide, rows16, stats],
+    stream, packed_one, sides, own, st2 = call(
+        functools.partial(k_view, entries), [tok32, ((T, 3 * D), BF16), ((T, 2 * D), BF16), rows16, stats],
         level_in, x_other, share(st1), view_qkv, view_out, place=place, us=4,
     )
+    column = jnp.asarray(view_rows(z, xl, core, dp))
+    (left,) = call(k_left_sides, [((2, D, 2 * T), BF16)], column, sides, swap(sides, "core"), place=place)
     out_field, rows_two = call(
         functools.partial(k_norm_two, entries), [moved, rows16], stream, out_grad, og_other, share(st2), place=place
     )
-    back, keep_two, give_two = call(
-        k_time, [moved, wide, wide], transpose(out_field), time_qkv, time_out, place=place, us=6
-    )
+    back, keep_two, give_two = call(k_time, [moved, wide, wide], transpose(out_field), time_qkv, time_out, place=place, us=6)
     mine, *pieces = call(
         k_weights_time, [((D // 4, 2 * D), BF16)] * 4, table, keep_two, swap(give_two, "core"), place=place, us=3
     )
-    moved_back, _ = lax.optimization_barrier((transpose(back), pieces))
+    moved_back, _, left = lax.optimization_barrier((transpose(back), pieces, left))
     time_parts = [mine, *shifted(pieces, "dp")]
     (st3,) = call(k_back_stats, [stats], moved_back, stream, rows_two, us=1)
     shared, time_parts = lax.optimization_barrier((share(st3), time_parts))
-    keep_one, give_one, pgrad, stream_grad, normed_one, sums_two = call(
-        functools.partial(k_view_back, entries), [wide, wide, ((T, 3 * D), BF16), tok32, tok32, rows16],
-        moved_back, stream, rows_two, shared, out_grad, og_other, level_in, x_other, own, saved, view_out,
-        place=place, us=5,
-    )
+    keep_one, give_one, pgrad, stream_grad, sums_two = call(
+        functools.partial(k_view_back, entries), [((T, 2 * D), BF16)] * 2 + [((T, 3 * D), BF16), tok32, rows16],
+        moved_back, stream, rows_two, shared, out_grad, og_other, packed_one, view_out, place=place, us=5,
+    )
+    (partial,) = call(k_weights_view, [((D, 2 * D), BF16)], left, keep_one, swap(give_one, "core"), us=1)
+    time_parts, partial, pgrad = lax.optimization_barrier((time_parts, partial, pgrad))
     u_keep, o_keep, send_back, st4 = call(
         k_view_stats, [half32, half16, ((HALF, 2 * D), BF16), rows16],
-        pgrad, stream_grad, moved_back, stream, normed_one, own, view_qkv, place=place, us=3,
-    )
-    taken, st4 = lax.optimization_barrier((swap(give_one, "core"), st4))
-    (partial,) = call(k_weights_view, [((D, 2 * D), BF16)], table, keep_one, taken, place=None, us=3)
-    time_parts, partial = lax.optimization_barrier((time_parts, partial))
+        pgrad, stream_grad, moved_back, stream, level_in, x_other, own, view_qkv, place=place, us=3,
+    )
     parts = lax.all_to_all(partial, ("view", "xl", "dp"), 0, 0, tiled=True)
     mine, *pieces = call(k_sum_time, [((D // 16, 2 * D), BF16)] * 4, *time_parts)
     time_parts = [mine, *shifted(pieces, ("view", "xl"))]
-    parts, time_parts, st4 = lax.optimization_barrier((parts, time_parts, st4 + swap(st4, "view")))
+    parts, time_parts, st4 = lax.optimization_barrier((parts, time_parts, crossed(crossed(st4, 2), 1)))
     (by_z,) = call(k_sum_rows, [((z, 4, rows * D), BF16)], parts, *time_parts)
     by_z, st4, send_back = lax.optimization_barrier((by_z, st4, send_back))
     by_z = lax.all_to_all(by_z, "z", 0, 0, tiled=True)
     recv_back = swap(send_back, "view")
-    st4 = crossed(crossed(st4, 1), 2)
-    by_z, st4 = lax.optimization_barrier((by_z, st4))
+    st4 = st4 + swap(st4, "view")
+    by_z, st4, recv_back = lax.optimization_barrier((by_z, st4, recv_back))
     (summed,) = call(k_sum, [((4, rows * D), BF16)], by_z)
     level_out, level_in_grad, sums = call(
         functools.partial(k_finish, entries),

time: 171 us -> 161 us (0.942)
  waiting for transfers between devices: 43.9 us -> 36.2 us
  Pallas kernels: 28.1 us -> 25.3 us
    ppermute x8 -> x9, waiting for transfers between devices: 23.6 us -> 6.64 us  [swap(): return lax.ppermute(field, axis, [(0, 1), (1, 0)])]
    ppermute x6, waiting for transfers between devices: 0.02 us -> 8.08 us  [shifted(): lax.ppermute(piece, axis, [(i, (i + step + 1) % 4) for i in range(4)])]
    pallas_call x14 -> x15, Pallas kernels: 28.1 us -> 25.3 us  [call(): pl.pallas_call(kernel, out_shape=[jax.ShapeDtypeStruct(shape, dtype) for...]
    ppermute x2, waiting for transfers between devices: 2.97 us -> 5.54 us  [crossed(): return field + lax.ppermute(field, 'dp', [(i, i ^ step) for i in range(dp)])]
    all_to_all x1, waiting for transfers between devices: 4.92 us -> 2.56 us  [transpose(): return lax.all_to_all(field, frame_axes, 0, 0, tiled=True)]
    ppermute x8 -> x9, starting transfers between devices: 15.6 us -> 16.9 us  [swap(): return lax.ppermute(field, axis, [(0, 1), (1, 0)])]
    unnamed x58 -> x72, local copies, waits for them, and re-layouts: 8.4 us -> 8.28 us
  transfers between devices with their start and end apart: 21 -> 22, of which waited for: 8 -> 12; matrix products, arithmetic and copies ran while one was open for 0% -> 0% of each run, Pallas kernels for 7% -> 8%
where the time goes in v3:
time: 161 us
  starting transfers between devices  51.1 us (32%)
  blocking collectives  38.7 us (24%)
  waiting for transfers between devices  36.2 us (22%)
  Pallas kernels  25.3 us (16%)
  local copies, waits for them, and re-layouts  8.28 us (5%)
    all_to_all x1, blocking collectives, transpose(): return lax.all_to_all(field, frame_axes, 0, 0, tiled=True)  26 us
    pallas_call x15, Pallas kernels, call(): pl.pallas_call(kernel, out_shape=[jax.ShapeDtypeStruct(shape, dtype) for...  25.3 us
    ppermute x9, starting transfers between devices, swap(): return lax.ppermute(field, axis, [(0, 1), (1, 0)])  16.9 us
    all_to_all x1, blocking collectives, share(): return lax.all_to_all(field, mates, 0, 0, tiled=True)  12.7 us
    all_to_all x2, waiting for transfers between devices, share(): return lax.all_to_all(field, mates, 0, 0, tiled=True)  10.3 us
    unnamed x72, local copies, waits for them, and re-layouts  8.28 us
    ppermute x6, waiting for transfers between devices, shifted(): lax.ppermute(piece, axis, [(i, (i + step + 1) % 4) for i in range(4)])  8.08 us
    ppermute x6, starting transfers between devices, shifted(): lax.ppermute(piece, axis, [(i, (i + step + 1) % 4) for i in range(4)])  7.92 us
  transfers between devices with their start and end apart: 22, of which 12 were waited for; matrix products, arithmetic and copies ran while one was open for 0% of the time, Pallas kernels for 8%

profile of v3, /device:TPU:1, one launch (start us, length us, event | category | flops | bytes accessed | tf_op | source)
XLA Modules:
  0.0 160.6 jit_solution(6088170736593614473)
XLA Ops:
  0.6 3.7 %collective-permute-start = (bf16[4,1,32,640]{3,2,1,0:T(8,128)(2,1)}, bf16[4,1,32,640]{3,2,1,0:T(8,128)(2,1)S(1)}, u32[]{:S(2)}, u32[]{:S(2)}) collective-permute-start(bf16[4,1,32,640]{3,2,1,0:T(8,128)(2,1)} %x_ref.7), channel_id=1, source_target_pairs={{0,128},{128,0},{1,129},{129,1},{2,130},{130,2},{3,131},{131,3},{4... | collective-permute-start | bytes 491528 | tf_op jit(solution)/shard_map/ppermute | solution.py:484
  4.3 0.1 pad_add_fusion.place
  4.4 0.9 copy-done.11
  5.3 1.9 %shard_map.135 = f32[8,16,128]{2,1,0:T(8,128)} custom-call(s32[3]{0:T(128)S(1)} %pad_add_fusion.place, bf16[4,1,32,640]{3,2,1,0:T(8,128)(2,1)S(1)} %copy-done.11), custom_call_target="tpu_custom_call" | custom-call | flops 2000000000 | bytes 6000000 | tf_op jit(solution)/shard_map/pallas_call | solution.py:428
  7.2 4.2 %all-to-all-start = ((f32[8,16,128]{2,1,0:T(8,128)}), f32[8,16,128]{2,1,0:T(8,128)S(1)}, u32[]{:S(2)}, u32[]{:S(2)}) async-start(f32[8,16,128]{2,1,0:T(8,128)} %shard_map.135), calls=%async_computation | async-start | bytes 131072 | tf_op jit(solution)/shard_map/all_to_all | solution.py:478
  11.4 3.0 %collective-permute-start.1 = (bf16[4,1,32,640]{3,2,1,0:T(8,128)(2,1)S(1)}, bf16[4,1,32,640]{3,2,1,0:T(8,128)(2,1)S(1)}, u32[]{:S(2)}, u32[]{:S(2)}) collective-permute-start(bf16[4,1,32,640]{3,2,1,0:T(8,128)(2,1)S(1)} %copy-done.9), channel_id=1, source_target_pairs={{0,128},{128,0},{1,129},{129,1},{2,130},{130,2},{3,131},{131,3},{4... | collective-permute-start | bytes 491528 | tf_op jit(solution)/shard_map/ppermute | solution.py:484
  14.4 3.7 %all-to-all-done.g_ref = f32[8,16,128]{2,1,0:T(8,128)S(1)} async-done(((f32[8,16,128]{2,1,0:T(8,128)}), f32[8,16,128]{2,1,0:T(8,128)S(1)}, u32[]{:S(2)}, u32[]{:S(2)}) %all-to-all-start) | async-done | bytes 65568 | tf_op jit(solution)/shard_map/all_to_all | solution.py:478
  18.1 0.0 collective-permute-done.other_ref
  18.1 0.0 copy-start.1
  18.1 1.7 %copy-done.1 = bf16[640,1920]{1,0:T(8,128)(2,1)S(1)} copy-done((bf16[640,1920]{1,0:T(8,128)(2,1)S(1)}, bf16[640,1920]{1,0:T(8,128)(2,1)}, u32[]{:S(2)}) %copy-start.1) | copy-done | bytes 2457624
  19.8 3.4 %shard_map.136 = (f32[128,640]{1,0:T(8,128)S(1)}, bf16[128,1920]{1,0:T(8,128)(2,1)S(1)}, bf16[128,1280]{1,0:T(8,128)(2,1)S(1)}, f32[16,128]{1,0:T(8,128)S(1)}, f32[8,16,128]{2,1,0:T(8,128)}) custom-call(s32[3]{0:T(128)S(1)} %pad_add_fusion.place, bf16[4,1,32,640]{3,2,1,0:T(8,128)(2,1)S(1)} %copy-done.12, ...), custom_call_target="tpu_custom_call" | custom-call | flops 4000000000 | bytes 12000000 | tf_op jit(solution)/shard_map/pallas_call | solution.py:428
  23.2 3.3 %all-to-all-start.1 = ((f32[8,16,128]{2,1,0:T(8,128)}), f32[8,16,128]{2,1,0:T(8,128)S(1)}, u32[]{:S(2)}, u32[]{:S(2)}) async-start(f32[8,16,128]{2,1,0:T(8,128)} %get-tuple-element.67), calls=%async_computation.1 | async-start | bytes 131072 | tf_op jit(solution)/shard_map/all_to_all | solution.py:478
  26.5 0.0 copy-start.16
  26.5 6.6 %all-to-all-done.1.g_ref = f32[8,16,128]{2,1,0:T(8,128)S(1)} async-done(((f32[8,16,128]{2,1,0:T(8,128)}), f32[8,16,128]{2,1,0:T(8,128)S(1)}, u32[]{:S(2)}, u32[]{:S(2)}) %all-to-all-start.1) | async-done | bytes 65568 | tf_op jit(solution)/shard_map/all_to_all | solution.py:478
  33.2 0.9 shard_map.137
  34.1 26.0 %all_to_all.42.recv_ref = bf16[32,4,1280]{2,1,0:T(4,128)(2,1)S(1)} all-to-all(bf16[32,4,1280]{2,1,0:T(4,128)(2,1)S(1)} %get-tuple-element.68), channel_id=1, replica_groups=mesh['view'=2,'z'=8,'xl'=2,'core'=2,'dp'=4] {'z','xl','core'}, dimensions={0} | all-to-all | bytes 655360 | tf_op jit(solution)/shard_map/all_to_all | solution.py:481
  60.0 4.2 %shard_map.138 = (bf16[32,4,1280]{2,1,0:T(4,128)(2,1)}, bf16[128,2560]{1,0:T(8,128)(2,1)S(1)}, bf16[128,2560]{1,0:T(8,128)(2,1)S(1)}) custom-call(s32[3]{0:T(128)S(1)} %pad_add_fusion.place, bf16[32,4,1280]{2,1,0:T(4,128)(2,1)S(1)} %all_to_all.42.recv_ref, bf16[640,1920]{1,0:T(8,128)(2,1)S(1)} %copy-done, bf16[640,640]{1,0:T(8,128)(2,1)S(1)} %copy-done.3), custom_call_target="tpu_custom_call" | custom-call | flops 6000000000 | bytes 18000000 | tf_op jit(solution)/shard_map/pallas_call | solution.py:428
  64.2 0.9 copy-done.32
  65.1 1.3 collective-permute-start.2
  66.4 3.7 %all-to-all-start.3 = ((bf16[32,4,1280]{2,1,0:T(4,128)(2,1)}), bf16[32,4,1280]{2,1,0:T(4,128)(2,1)S(1)}, u32[]{:S(2)}, u32[]{:S(2)}) async-start(bf16[32,4,1280]{2,1,0:T(4,128)(2,1)} %get-tuple-element.69), calls=%async_computation.3 | async-start | bytes 655360 | tf_op jit(solution)/shard_map/all_to_all | solution.py:481
  70.1 0.3 collective-permute-start.3
  70.4 1.1 copy-done.33
  71.5 2.8 %shard_map.139 = (bf16[160,1280]{1,0:T(8,128)(2,1)S(1)}, bf16[160,1280]{1,0:T(8,128)(2,1)}, bf16[160,1280]{1,0:T(8,128)(2,1)S(1)}, bf16[160,1280]{1,0:T(8,128)(2,1)S(1)}) custom-call(s32[3]{0:T(128)S(1)} %pad_add_fusion.place, s32[16,1,640]{2,1,0:T(1,128)S(1)} %copy-done.19, bf16[128,2560]{1,0:T(8,128)(2,1)S(1)} %copy-done.33, ...), custom_call_target="tpu_custom_call" | custom-call | flops 3000000000 | bytes 9000000 | tf_op jit(solution)/shard_map/pallas_call | solution.py:428
  74.3 0.8 copy-done.26
  75.0 0.3 collective-permute-start.4
  75.4 1.8 %collective-permute-start.5 = (bf16[160,1280]{1,0:T(8,128)(2,1)S(1)}, bf16[160,1280]{1,0:T(8,128)(2,1)S(1)}, u32[]{:S(2)}, u32[]{:S(2)}) collective-permute-start(bf16[160,1280]{1,0:T(8,128)(2,1)S(1)} %get-tuple-element.73), channel_id=1, source_target_pairs={{0,2},{1,3},{2,0},{3,1},{4,6},{5,7},{6,4},{7,5},{8,10},{9,11},{10,... | collective-permute-start | bytes 1228808 | tf_op jit(solution)/shard_map/ppermute | solution.py:488
  77.1 0.8 collective-permute-start.6
  77.9 0.0 collective-permute-done.3.theirs_ref
  78.0 1.3 shard_map.140.left_ref
  79.3 0.9 copy-done.20
  80.1 2.6 %all-to-all-done.3.back_ref = bf16[32,4,1280]{2,1,0:T(4,128)(2,1)S(1)} async-done(((bf16[32,4,1280]{2,1,0:T(4,128)(2,1)}), bf16[32,4,1280]{2,1,0:T(4,128)(2,1)S(1)}, u32[]{:S(2)}, u32[]{:S(2)}) %all-to-all-start.3) | async-done | bytes 327712 | tf_op jit(solution)/shard_map/all_to_all | solution.py:481
  82.7 1.0 copy-done.23
  83.7 0.6 shard_map.141
  84.3 12.7 %all_to_all.43.g_ref = f32[8,16,128]{2,1,0:T(8,128)S(1)} all-to-all(f32[8,16,128]{2,1,0:T(8,128)S(1)} %shard_map.141), channel_id=1, replica_groups=mesh['view'=2,'z'=8,'xl'=2,'core'=2,'dp'=4] {'view','dp'}, dimensions={0} | all-to-all | bytes 131072 | tf_op jit(solution)/shard_map/all_to_all | solution.py:478
  97.0 0.0 collective-permute-done.4.refs_1_
  97.1 2.3 %shard_map.142 = (bf16[128,1280]{1,0:T(8,128)(2,1)S(1)}, bf16[128,1280]{1,0:T(8,128)(2,1)S(1)}, bf16[128,1920]{1,0:T(8,128)(2,1)S(1)}, f32[128,640]{1,0:T(8,128)S(1)}, f32[16,128]{1,0:T(8,128)S(1)}) custom-call(s32[3]{0:T(128)S(1)} %pad_add_fusion.place, bf16[32,4,1280]{2,1,0:T(4,128)(2,1)S(1)} %all-to-all-done.3.back_ref, f32[128,640]{1,0:T(8,128)S(1)} %copy-done.24, ...), custom_call_target="tpu_custom_call" | custom-call | flops 5000000000 | bytes 15000000 | tf_op jit(solution)/shard_map/pallas_call | solution.py:428
  99.4 1.3 collective-permute-start.7
  100.7 1.3 collective-permute-done.7.theirs_ref
  101.9 1.9 %shard_map.143 = bf16[640,1280]{1,0:T(8,128)(2,1)} custom-call(bf16[2,640,256]{2,1,0:T(8,128)(2,1)S(1)} %copy-done.21, bf16[128,1280]{1,0:T(8,128)(2,1)S(1)} %get-tuple-element.86.mine_ref, bf16[128,1280]{1,0:T(8,128)(2,1)S(1)} %collective-permute-done.7.theirs_ref), custom_call_target="tpu_custom_call" | custom-call | flops 1000000000 | bytes 3000000 | tf_op jit(solution)/shard_map/pallas_call | solution.py:428
  103.8 5.1 %all-to-all-start.5 = ((bf16[16,40,1280]{2,1,0:T(8,128)(2,1)}), bf16[16,40,1280]{2,1,0:T(8,128)(2,1)S(1)}, u32[]{:S(2)}, u32[]{:S(2)}) async-start(bf16[16,40,1280]{2,1,0:T(8,128)(2,1)} %bitcast.3), calls=%async_computation.5 | async-start | bytes 3276800 | tf_op jit(solution)/shard_map/all_to_all | solution.py:525
  109.0 1.0 copy-done.27
  110.0 0.2 shard_map.144
  110.3 1.4 collective-permute-start.8
  111.7 2.4 %collective-permute-start.9 = (bf16[40,1280]{1,0:T(8,128)(2,1)S(1)}, bf16[40,1280]{1,0:T(8,128)(2,1)S(1)}, u32[]{:S(2)}, u32[]{:S(2)}) collective-permute-start(bf16[40,1280]{1,0:T(8,128)(2,1)S(1)} %get-tuple-element.96), channel_id=1, source_target_pairs={{0,128},{8,136},{128,0},{136,8},{1,129},{9,137},{129,1},{137,9},{2... | collective-permute-start | bytes 307208 | tf_op jit(solution)/shard_map/ppermute | solution.py:488
  114.1 1.2 collective-permute-start.10
  115.3 1.7 %shard_map.145 = (f32[64,640]{1,0:T(8,128)S(1)}, bf16[64,640]{1,0:T(8,128)(2,1)S(1)}, bf16[64,1280]{1,0:T(8,128)(2,1)S(1)}, f32[16,128]{1,0:T(8,128)S(1)}) custom-call(s32[3]{0:T(128)S(1)} %pad_add_fusion.place, bf16[128,1920]{1,0:T(8,128)(2,1)S(1)} %copy-done.29, f32[128,640]{1,0:T(8,128)S(1)} %copy-done.31, ...), custom_call_target="tpu_custom_call" | custom-call | flops 3000000000 | bytes 9000000 | tf_op jit(solution)/shard_map/pallas_call | solution.py:428
  117.0 2.8 %collective-permute-start.11 = (f32[16,128]{1,0:T(8,128)S(1)}, f32[16,128]{1,0:T(8,128)S(1)}, u32[]{:S(2)}, u32[]{:S(2)}) collective-permute-start(f32[16,128]{1,0:T(8,128)S(1)} %get-tuple-element.101), channel_id=1, source_target_pairs={{0,2},{1,3},{2,0},{3,1},{4,6},{5,7},{6,4},{7,5},{8,10},{9,11},{10,... | collective-permute-start | bytes 24584 | tf_op jit(solution)/shard_map/ppermute | solution.py:492
  119.8 2.1 %collective-permute-done.11 = f32[16,128]{1,0:T(8,128)S(1)} collective-permute-done((f32[16,128]{1,0:T(8,128)S(1)}, f32[16,128]{1,0:T(8,128)S(1)}, u32[]{:S(2)}, u32[]{:S(2)}) %collective-permute-start.11) | collective-permute-done | bytes 8224 | tf_op jit(solution)/shard_map/ppermute | solution.py:492
  122.0 0.6 collective-permute-start.12
  122.6 3.4 %collective-permute-done.12 = f32[16,128]{1,0:T(8,128)S(1)} collective-permute-done((f32[16,128]{1,0:T(8,128)S(1)}, f32[16,128]{1,0:T(8,128)S(1)}, u32[]{:S(2)}, u32[]{:S(2)}) %collective-permute-start.12) | collective-permute-done | bytes 8224 | tf_op jit(solution)/shard_map/ppermute | solution.py:492
  126.0 4.9 %collective-permute-done.8.refs_1_ = bf16[40,1280]{1,0:T(8,128)(2,1)S(1)} collective-permute-done((bf16[40,1280]{1,0:T(8,128)(2,1)S(1)}, bf16[40,1280]{1,0:T(8,128)(2,1)S(1)}, u32[]{:S(2)}, u32[]{:S(2)}) %collective-permute-start.8) | collective-permute-done | bytes 102432 | tf_op jit(solution)/shard_map/ppermute | solution.py:488
  131.0 3.1 %collective-permute-done.9.refs_2_ = bf16[40,1280]{1,0:T(8,128)(2,1)S(1)} collective-permute-done((bf16[40,1280]{1,0:T(8,128)(2,1)S(1)}, bf16[40,1280]{1,0:T(8,128)(2,1)S(1)}, u32[]{:S(2)}, u32[]{:S(2)}) %collective-permute-start.9) | collective-permute-done | bytes 102432 | tf_op jit(solution)/shard_map/ppermute | solution.py:488
  134.1 1.2 shard_map.146
  135.3 6.5 %all-to-all-start.6 = ((bf16[8,4,3200]{2,1,0:T(4,128)(2,1)}), bf16[8,4,3200]{2,1,0:T(4,128)(2,1)S(1)}, u32[]{:S(2)}, u32[]{:S(2)}) async-start(bf16[8,4,3200]{2,1,0:T(4,128)(2,1)} %shard_map.146), calls=%async_computation.6 | async-start | bytes 409600 | tf_op jit(solution)/shard_map/all_to_all | solution.py:531
  141.8 1.5 collective-permute-start.14
  143.3 1.5 collective-permute-start.13
  144.8 2.8 %collective-permute-done.13 = f32[16,128]{1,0:T(8,128)S(1)} collective-permute-done((f32[16,128]{1,0:T(8,128)S(1)}, f32[16,128]{1,0:T(8,128)S(1)}, u32[]{:S(2)}, u32[]{:S(2)}) %collective-permute-start.13) | collective-permute-done | bytes 8224 | tf_op jit(solution)/shard_map/ppermute | solution.py:484
  147.6 3.0 %all-to-all-done.6.parts_ref = bf16[8,4,3200]{2,1,0:T(4,128)(2,1)S(1)} async-done(((bf16[8,4,3200]{2,1,0:T(4,128)(2,1)}), bf16[8,4,3200]{2,1,0:T(4,128)(2,1)S(1)}, u32[]{:S(2)}, u32[]{:S(2)}) %all-to-all-start.6) | async-done | bytes 204832 | tf_op jit(solution)/shard_map/all_to_all | solution.py:531
  150.6 3.3 %collective-permute-start.15 = (bf16[4,3200]{1,0:T(4,128)(2,1)S(1)}, bf16[4,3200]{1,0:T(4,128)(2,1)S(1)}, u32[]{:S(2)}, u32[]{:S(2)}) collective-permute-start(bf16[4,3200]{1,0:T(4,128)(2,1)S(1)} %shard_map.148), channel_id=1, source_target_pairs={{0,4},{4,0},{1,5},{5,1},{2,6},{6,2},{3,7},{7,3},{8,12},{12,8},{9,1... | collective-permute-start | bytes 76808 | tf_op jit(solution)/shard_map/ppermute | solution.py:484
  153.9 0.9 collective-permute-done.15
  154.8 1.2 collective-permute-start.16
  156.0 1.6 %shard_map.147 = (bf16[4,32,640]{2,1,0:T(8,128)(2,1)}, bf16[4,32,640]{2,1,0:T(8,128)(2,1)}, f32[4,4,128]{2,1,0:T(4,128)}) custom-call(s32[3]{0:T(128)S(1)} %pad_add_fusion.place, f32[16,128]{1,0:T(8,128)S(1)} %add.19.g_ref, f32[16,128]{1,0:T(8,128)S(1)} %get-tuple-element.113.sumstwo_ref, f32[16,128]{1,0:T(8,128)S(1)} %get-tuple-element.100.own_ref, ...), custom_call_target="tpu_custom_call" | custom-call | flops 3000000000 | bytes 9000000 | tf_op jit(solution)/shard_map/pallas_call | solution.py:428
  157.6 1.7 %collective-permute-done.16.far_ref = bf16[8,3200]{1,0:T(8,128)(2,1)S(1)} collective-permute-done((bf16[8,3200]{1,0:T(8,128)(2,1)S(1)}, bf16[8,3200]{1,0:T(8,128)(2,1)S(1)}, u32[]{:S(2)}, u32[]{:S(2)}) %collective-permute-start.16) | collective-permute-done | bytes 51232 | tf_op jit(solution)/shard_map/ppermute | solution.py:484
  159.4 1.2 shard_map.149
  (75 shorter events, 0.2 us)
Async XLA Ops:
  0.6 17.5 %collective-permute-start = (bf16[4,1,32,640]{3,2,1,0:T(8,128)(2,1)}, bf16[4,1,32,640]{3,2,1,0:T(8,128)(2,1)S(1)}, u32[]{:S(2)}, u32[]{:S(2)}) collective-permute-start(bf16[4,1,32,640]{3,2,1,0:T(8,128)(2,1)} %x_ref.7), channel_id=1, source_target_pairs={{0,128},{128,0},{1,129},{129,1},{2,130},{130,2},{3,131},{131,3},{4... | collective-permute-start | bytes 491528 | tf_op jit(solution)/shard_map/ppermute | solution.py:484
  4.4 0.9 copy-start.11
  5.3 6.1 %copy-start.9 = (bf16[4,1,32,640]{3,2,1,0:T(8,128)(2,1)S(1)}, bf16[4,1,32,640]{3,2,1,0:T(8,128)(2,1)}, u32[]{:S(2)}) copy-start(bf16[4,1,32,640]{3,2,1,0:T(8,128)(2,1)} %og_ref.1) | copy-start | bytes 491524
  5.3 12.8 %copy-start.4 = (bf16[640,640]{1,0:T(8,128)(2,1)S(1)}, bf16[640,640]{1,0:T(8,128)(2,1)}, u32[]{:S(2)}) copy-start(bf16[640,640]{1,0:T(8,128)(2,1)} %wout_ref.5) | copy-start | bytes 2457604
  5.3 12.8 %copy-start.12 = (bf16[4,1,32,640]{3,2,1,0:T(8,128)(2,1)S(1)}, bf16[4,1,32,640]{3,2,1,0:T(8,128)(2,1)}, u32[]{:S(2)}) copy-start(bf16[4,1,32,640]{3,2,1,0:T(8,128)(2,1)} %x_ref.7) | copy-start | bytes 491524
  7.2 10.9 %all-to-all-start = ((f32[8,16,128]{2,1,0:T(8,128)}), f32[8,16,128]{2,1,0:T(8,128)S(1)}, u32[]{:S(2)}, u32[]{:S(2)}) async-start(f32[8,16,128]{2,1,0:T(8,128)} %shard_map.135), calls=%async_computation | async-start | bytes 131072 | tf_op jit(solution)/shard_map/all_to_all | solution.py:478
  11.4 15.1 %collective-permute-start.1 = (bf16[4,1,32,640]{3,2,1,0:T(8,128)(2,1)S(1)}, bf16[4,1,32,640]{3,2,1,0:T(8,128)(2,1)S(1)}, u32[]{:S(2)}, u32[]{:S(2)}) collective-permute-start(bf16[4,1,32,640]{3,2,1,0:T(8,128)(2,1)S(1)} %copy-done.9), channel_id=1, source_target_pairs={{0,128},{128,0},{1,129},{129,1},{2,130},{130,2},{3,131},{131,3},{4... | collective-permute-start | bytes 491528 | tf_op jit(solution)/shard_map/ppermute | solution.py:484
  18.1 1.7 %copy-start.1 = (bf16[640,1920]{1,0:T(8,128)(2,1)S(1)}, bf16[640,1920]{1,0:T(8,128)(2,1)}, u32[]{:S(2)}) copy-start(bf16[640,1920]{1,0:T(8,128)(2,1)} %wqkv_ref.5) | copy-start | bytes 7372804
  19.8 3.4 %copy-start.14 = (bf16[4,1,32,640]{3,2,1,0:T(8,128)(2,1)}, bf16[4,1,32,640]{3,2,1,0:T(8,128)(2,1)S(1)}, u32[]{:S(2)}) copy-start(bf16[4,1,32,640]{3,2,1,0:T(8,128)(2,1)S(1)} %collective-permute-done.other_ref) | copy-start | bytes 491524
  23.2 10.9 %copy-start.22 = (f32[128,640]{1,0:T(8,128)}, f32[128,640]{1,0:T(8,128)S(1)}, u32[]{:S(2)}) copy-start(f32[128,640]{1,0:T(8,128)S(1)} %get-tuple-element.66.stream_ref) | copy-start | bytes 983044
  23.2 10.9 %copy-start.34 = (bf16[128,1920]{1,0:T(8,128)(2,1)}, bf16[128,1920]{1,0:T(8,128)(2,1)S(1)}, u32[]{:S(2)}) copy-start(bf16[128,1920]{1,0:T(8,128)(2,1)S(1)} %get-tuple-element.85.packed_ref) | copy-start | bytes 1474564
  23.2 10.0 %all-to-all-start.1 = ((f32[8,16,128]{2,1,0:T(8,128)}), f32[8,16,128]{2,1,0:T(8,128)S(1)}, u32[]{:S(2)}, u32[]{:S(2)}) async-start(f32[8,16,128]{2,1,0:T(8,128)} %get-tuple-element.67), calls=%async_computation.1 | async-start | bytes 131072 | tf_op jit(solution)/shard_map/all_to_all | solution.py:478
  26.5 7.5 %copy-start.16 = (bf16[4,1,32,640]{3,2,1,0:T(8,128)(2,1)}, bf16[4,1,32,640]{3,2,1,0:T(8,128)(2,1)S(1)}, u32[]{:S(2)}) copy-start(bf16[4,1,32,640]{3,2,1,0:T(8,128)(2,1)S(1)} %collective-permute-done.1.other_ref.ogother_ref) | copy-start | bytes 491524
  33.2 26.9 %copy-start = (bf16[640,1920]{1,0:T(8,128)(2,1)S(1)}, bf16[640,1920]{1,0:T(8,128)(2,1)}, u32[]{:S(2)}) copy-start(bf16[640,1920]{1,0:T(8,128)(2,1)} %wqkv_ref.4) | copy-start | bytes 7372804
  33.2 26.9 %copy-start.3 = (bf16[640,640]{1,0:T(8,128)(2,1)S(1)}, bf16[640,640]{1,0:T(8,128)(2,1)}, u32[]{:S(2)}) copy-start(bf16[640,640]{1,0:T(8,128)(2,1)} %wout_ref.4) | copy-start | bytes 2457604
  60.0 10.3 %copy-start.19 = (s32[16,1,640]{2,1,0:T(1,128)S(1)}, s32[16,1,640]{2,1,0:T(1,128)}, u32[]{:S(2)}) copy-start(s32[16,1,640]{2,1,0:T(1,128)} %constant.26.clone.table_ref) | copy-start | bytes 122884
  64.2 0.9 copy-start.32
  65.1 5.3 %collective-permute-start.2 = (bf16[128,2560]{1,0:T(8,128)(2,1)S(1)}, bf16[128,2560]{1,0:T(8,128)(2,1)S(1)}, u32[]{:S(2)}, u32[]{:S(2)}) collective-permute-start(bf16[128,2560]{1,0:T(8,128)(2,1)S(1)} %get-tuple-element.71), channel_id=1, source_target_pairs={{0,4},{4,0},{1,5},{5,1},{2,6},{6,2},{3,7},{7,3},{8,12},{12,8},{9,1... | collective-permute-start | bytes 1966088 | tf_op jit(solution)/shard_map/ppermute | solution.py:484
  66.4 16.3 %all-to-all-start.3 = ((bf16[32,4,1280]{2,1,0:T(4,128)(2,1)}), bf16[32,4,1280]{2,1,0:T(4,128)(2,1)S(1)}, u32[]{:S(2)}, u32[]{:S(2)}) async-start(bf16[32,4,1280]{2,1,0:T(4,128)(2,1)} %get-tuple-element.69), calls=%async_computation.3 | async-start | bytes 655360 | tf_op jit(solution)/shard_map/all_to_all | solution.py:481
  70.1 7.9 %collective-permute-start.3 = (bf16[128,1280]{1,0:T(8,128)(2,1)S(1)}, bf16[128,1280]{1,0:T(8,128)(2,1)S(1)}, u32[]{:S(2)}, u32[]{:S(2)}) collective-permute-start(bf16[128,1280]{1,0:T(8,128)(2,1)S(1)} %get-tuple-element.75.mine_ref), channel_id=1, source_target_pairs={{0,4},{4,0},{1,5},{5,1},{2,6},{6,2},{3,7},{7,3},{8,12},{12,8},{9,1... | collective-permute-start | bytes 983048 | tf_op jit(solution)/shard_map/ppermute | solution.py:484
  70.4 1.1 copy-start.33
  71.5 6.5 %copy-start.18 = (s32[640,1]{1,0:T(8,128)S(1)}, s32[640,1]{1,0:T(8,128)}, u32[]{:S(2)}) copy-start(s32[640,1]{1,0:T(8,128)} %constant.27.clone.column_ref) | copy-start | bytes 7684
  74.3 0.8 copy-start.26
  75.0 21.9 %collective-permute-start.4 = (bf16[160,1280]{1,0:T(8,128)(2,1)}, bf16[160,1280]{1,0:T(8,128)(2,1)S(1)}, u32[]{:S(2)}, u32[]{:S(2)}) collective-permute-start(bf16[160,1280]{1,0:T(8,128)(2,1)} %get-tuple-element.72), channel_id=1, source_target_pairs={{0,1},{1,2},{2,3},{3,0},{4,5},{5,6},{6,7},{7,4},{8,9},{9,10},{10,1... | collective-permute-start | bytes 1228808 | tf_op jit(solution)/shard_map/ppermute | solution.py:488
  75.4 21.6 %collective-permute-start.5 = (bf16[160,1280]{1,0:T(8,128)(2,1)S(1)}, bf16[160,1280]{1,0:T(8,128)(2,1)S(1)}, u32[]{:S(2)}, u32[]{:S(2)}) collective-permute-start(bf16[160,1280]{1,0:T(8,128)(2,1)S(1)} %get-tuple-element.73), channel_id=1, source_target_pairs={{0,2},{1,3},{2,0},{3,1},{4,6},{5,7},{6,4},{7,5},{8,10},{9,11},{10,... | collective-permute-start | bytes 1228808 | tf_op jit(solution)/shard_map/ppermute | solution.py:488
  77.1 19.9 %collective-permute-start.6 = (bf16[160,1280]{1,0:T(8,128)(2,1)S(1)}, bf16[160,1280]{1,0:T(8,128)(2,1)S(1)}, u32[]{:S(2)}, u32[]{:S(2)}) collective-permute-start(bf16[160,1280]{1,0:T(8,128)(2,1)S(1)} %get-tuple-element.74), channel_id=1, source_target_pairs={{0,3},{1,0},{2,1},{3,2},{4,7},{5,4},{6,5},{7,6},{8,11},{9,8},{10,9... | collective-permute-start | bytes 1228808 | tf_op jit(solution)/shard_map/ppermute | solution.py:488
  79.3 0.9 copy-start.20
  80.1 16.9 %copy-start.10 = (bf16[4,1,32,640]{3,2,1,0:T(8,128)(2,1)S(1)}, bf16[4,1,32,640]{3,2,1,0:T(8,128)(2,1)}, u32[]{:S(2)}) copy-start(bf16[4,1,32,640]{3,2,1,0:T(8,128)(2,1)} %og_ref.1) | copy-start | bytes 491524
  80.1 16.9 %copy-start.17 = (bf16[4,1,32,640]{3,2,1,0:T(8,128)(2,1)S(1)}, bf16[4,1,32,640]{3,2,1,0:T(8,128)(2,1)}, u32[]{:S(2)}) copy-start(bf16[4,1,32,640]{3,2,1,0:T(8,128)(2,1)} %copy-done.16) | copy-start | bytes 491524
  82.7 1.0 copy-start.23
  83.7 13.4 %copy-start.24 = (f32[128,640]{1,0:T(8,128)S(1)}, f32[128,640]{1,0:T(8,128)}, u32[]{:S(2)}) copy-start(f32[128,640]{1,0:T(8,128)} %copy-done.22) | copy-start | bytes 983044
  83.7 13.4 %copy-start.35 = (bf16[128,1920]{1,0:T(8,128)(2,1)S(1)}, bf16[128,1920]{1,0:T(8,128)(2,1)}, u32[]{:S(2)}) copy-start(bf16[128,1920]{1,0:T(8,128)(2,1)} %copy-done.34) | copy-start | bytes 1474564
  97.0 2.4 %copy-start.5 = (bf16[160,1280]{1,0:T(8,128)(2,1)}, bf16[160,1280]{1,0:T(8,128)(2,1)S(1)}, u32[]{:S(2)}) copy-start(bf16[160,1280]{1,0:T(8,128)(2,1)S(1)} %collective-permute-done.5.refs_2_) | copy-start | bytes 1228804
  97.0 2.4 %copy-start.7 = (bf16[160,1280]{1,0:T(8,128)(2,1)}, bf16[160,1280]{1,0:T(8,128)(2,1)S(1)}, u32[]{:S(2)}) copy-start(bf16[160,1280]{1,0:T(8,128)(2,1)S(1)} %collective-permute-done.6.refs_3_) | copy-start | bytes 1228804
  97.1 4.9 %copy-start.21 = (bf16[2,640,256]{2,1,0:T(8,128)(2,1)S(1)}, bf16[2,640,256]{2,1,0:T(8,128)(2,1)}, u32[]{:S(2)}) copy-start(bf16[2,640,256]{2,1,0:T(8,128)(2,1)} %copy-done.20) | copy-start | bytes 1966084
  99.4 4.4 %copy-start.28 = (bf16[128,1920]{1,0:T(8,128)(2,1)}, bf16[128,1920]{1,0:T(8,128)(2,1)S(1)}, u32[]{:S(2)}) copy-start(bf16[128,1920]{1,0:T(8,128)(2,1)S(1)} %get-tuple-element.98.pgrad_ref) | copy-start | bytes 1474564
  99.4 4.4 %copy-start.30 = (f32[128,640]{1,0:T(8,128)}, f32[128,640]{1,0:T(8,128)S(1)}, u32[]{:S(2)}) copy-start(f32[128,640]{1,0:T(8,128)S(1)} %get-tuple-element.99.stream_grad_ref) | copy-start | bytes 983044
  99.4 2.5 %collective-permute-start.7 = (bf16[128,1280]{1,0:T(8,128)(2,1)S(1)}, bf16[128,1280]{1,0:T(8,128)(2,1)S(1)}, u32[]{:S(2)}, u32[]{:S(2)}) collective-permute-start(bf16[128,1280]{1,0:T(8,128)(2,1)S(1)} %get-tuple-element.87), channel_id=1, source_target_pairs={{0,4},{4,0},{1,5},{5,1},{2,6},{6,2},{3,7},{7,3},{8,12},{12,8},{9,1... | collective-permute-start | bytes 983048 | tf_op jit(solution)/shard_map/ppermute | solution.py:484
  103.8 5.2 %copy-start.6 = (bf16[160,1280]{1,0:T(8,128)(2,1)S(1)}, bf16[160,1280]{1,0:T(8,128)(2,1)}, u32[]{:S(2)}) copy-start(bf16[160,1280]{1,0:T(8,128)(2,1)} %copy-done.5) | copy-start | bytes 1228804
  103.8 5.2 %copy-start.8 = (bf16[160,1280]{1,0:T(8,128)(2,1)S(1)}, bf16[160,1280]{1,0:T(8,128)(2,1)}, u32[]{:S(2)}) copy-start(bf16[160,1280]{1,0:T(8,128)(2,1)} %copy-done.7) | copy-start | bytes 1228804
  103.8 30.3 %all-to-all-start.5 = ((bf16[16,40,1280]{2,1,0:T(8,128)(2,1)}), bf16[16,40,1280]{2,1,0:T(8,128)(2,1)S(1)}, u32[]{:S(2)}, u32[]{:S(2)}) async-start(bf16[16,40,1280]{2,1,0:T(8,128)(2,1)} %bitcast.3), calls=%async_computation.5 | async-start | bytes 3276800 | tf_op jit(solution)/shard_map/all_to_all | solution.py:525
  109.0 1.0 copy-start.27
  110.0 5.3 %copy-start.2 = (bf16[640,1920]{1,0:T(8,128)(2,1)S(1)}, bf16[640,1920]{1,0:T(8,128)(2,1)}, u32[]{:S(2)}) copy-start(bf16[640,1920]{1,0:T(8,128)(2,1)} %wqkv_ref.5) | copy-start | bytes 7372804
  110.0 5.3 %copy-start.13 = (bf16[4,1,32,640]{3,2,1,0:T(8,128)(2,1)S(1)}, bf16[4,1,32,640]{3,2,1,0:T(8,128)(2,1)}, u32[]{:S(2)}) copy-start(bf16[4,1,32,640]{3,2,1,0:T(8,128)(2,1)} %x_ref.7) | copy-start | bytes 491524
  110.0 5.3 %copy-start.15 = (bf16[4,1,32,640]{3,2,1,0:T(8,128)(2,1)S(1)}, bf16[4,1,32,640]{3,2,1,0:T(8,128)(2,1)}, u32[]{:S(2)}) copy-start(bf16[4,1,32,640]{3,2,1,0:T(8,128)(2,1)} %copy-done.14) | copy-start | bytes 491524
  110.0 5.3 %copy-start.25 = (f32[128,640]{1,0:T(8,128)S(1)}, f32[128,640]{1,0:T(8,128)}, u32[]{:S(2)}) copy-start(f32[128,640]{1,0:T(8,128)} %copy-done.22) | copy-start | bytes 983044
  110.0 5.3 %copy-start.29 = (bf16[128,1920]{1,0:T(8,128)(2,1)S(1)}, bf16[128,1920]{1,0:T(8,128)(2,1)}, u32[]{:S(2)}) copy-start(bf16[128,1920]{1,0:T(8,128)(2,1)} %copy-done.28) | copy-start | bytes 1474564
  110.0 5.3 %copy-start.31 = (f32[128,640]{1,0:T(8,128)S(1)}, f32[128,640]{1,0:T(8,128)}, u32[]{:S(2)}) copy-start(f32[128,640]{1,0:T(8,128)} %copy-done.30) | copy-start | bytes 983044
  110.3 20.7 %collective-permute-start.8 = (bf16[40,1280]{1,0:T(8,128)(2,1)S(1)}, bf16[40,1280]{1,0:T(8,128)(2,1)S(1)}, u32[]{:S(2)}, u32[]{:S(2)}) collective-permute-start(bf16[40,1280]{1,0:T(8,128)(2,1)S(1)} %get-tuple-element.95), channel_id=1, source_target_pairs={{0,8},{8,128},{128,136},{136,0},{1,9},{9,129},{129,137},{137,1},{2... | collective-permute-start | bytes 307208 | tf_op jit(solution)/shard_map/ppermute | solution.py:488
  111.7 22.4 %collective-permute-start.9 = (bf16[40,1280]{1,0:T(8,128)(2,1)S(1)}, bf16[40,1280]{1,0:T(8,128)(2,1)S(1)}, u32[]{:S(2)}, u32[]{:S(2)}) collective-permute-start(bf16[40,1280]{1,0:T(8,128)(2,1)S(1)} %get-tuple-element.96), channel_id=1, source_target_pairs={{0,128},{8,136},{128,0},{136,8},{1,129},{9,137},{129,1},{137,9},{2... | collective-permute-start | bytes 307208 | tf_op jit(solution)/shard_map/ppermute | solution.py:488
  114.1 20.0 %collective-permute-start.10 = (bf16[40,1280]{1,0:T(8,128)(2,1)S(1)}, bf16[40,1280]{1,0:T(8,128)(2,1)S(1)}, u32[]{:S(2)}, u32[]{:S(2)}) collective-permute-start(bf16[40,1280]{1,0:T(8,128)(2,1)S(1)} %get-tuple-element.97), channel_id=1, source_target_pairs={{0,136},{8,0},{128,8},{136,128},{1,137},{9,1},{129,9},{137,129},{2... | collective-permute-start | bytes 307208 | tf_op jit(solution)/shard_map/ppermute | solution.py:488
  117.0 4.9 %collective-permute-start.11 = (f32[16,128]{1,0:T(8,128)S(1)}, f32[16,128]{1,0:T(8,128)S(1)}, u32[]{:S(2)}, u32[]{:S(2)}) collective-permute-start(f32[16,128]{1,0:T(8,128)S(1)} %get-tuple-element.101), channel_id=1, source_target_pairs={{0,2},{1,3},{2,0},{3,1},{4,6},{5,7},{6,4},{7,5},{8,10},{9,11},{10,... | collective-permute-start | bytes 24584 | tf_op jit(solution)/shard_map/ppermute | solution.py:492
  122.0 4.0 %collective-permute-start.12 = (f32[16,128]{1,0:T(8,128)S(1)}, f32[16,128]{1,0:T(8,128)S(1)}, u32[]{:S(2)}, u32[]{:S(2)}) collective-permute-start(f32[16,128]{1,0:T(8,128)S(1)} %add.17), channel_id=1, source_target_pairs={{0,1},{1,0},{2,3},{3,2},{4,5},{5,4},{6,7},{7,6},{8,9},{9,8},{10,11... | collective-permute-start | bytes 24584 | tf_op jit(solution)/shard_map/ppermute | solution.py:492
  135.3 15.2 %all-to-all-start.6 = ((bf16[8,4,3200]{2,1,0:T(4,128)(2,1)}), bf16[8,4,3200]{2,1,0:T(4,128)(2,1)S(1)}, u32[]{:S(2)}, u32[]{:S(2)}) async-start(bf16[8,4,3200]{2,1,0:T(4,128)(2,1)} %shard_map.146), calls=%async_computation.6 | async-start | bytes 409600 | tf_op jit(solution)/shard_map/all_to_all | solution.py:531
  141.8 5.8 %collective-permute-start.14 = (bf16[64,1280]{1,0:T(8,128)(2,1)S(1)}, bf16[64,1280]{1,0:T(8,128)(2,1)S(1)}, u32[]{:S(2)}, u32[]{:S(2)}) collective-permute-start(bf16[64,1280]{1,0:T(8,128)(2,1)S(1)} %get-tuple-element.111), channel_id=1, source_target_pairs={{0,128},{128,0},{1,129},{129,1},{2,130},{130,2},{3,131},{131,3},{4... | collective-permute-start | bytes 491528 | tf_op jit(solution)/shard_map/ppermute | solution.py:484
  143.3 4.3 %collective-permute-start.13 = (f32[16,128]{1,0:T(8,128)S(1)}, f32[16,128]{1,0:T(8,128)S(1)}, u32[]{:S(2)}, u32[]{:S(2)}) collective-permute-start(f32[16,128]{1,0:T(8,128)S(1)} %add.18), channel_id=1, source_target_pairs={{0,128},{128,0},{1,129},{129,1},{2,130},{130,2},{3,131},{131,3},{4... | collective-permute-start | bytes 24584 | tf_op jit(solution)/shard_map/ppermute | solution.py:484
  150.6 4.1 %collective-permute-start.15 = (bf16[4,3200]{1,0:T(4,128)(2,1)S(1)}, bf16[4,3200]{1,0:T(4,128)(2,1)S(1)}, u32[]{:S(2)}, u32[]{:S(2)}) collective-permute-start(bf16[4,3200]{1,0:T(4,128)(2,1)S(1)} %shard_map.148), channel_id=1, source_target_pairs={{0,4},{4,0},{1,5},{5,1},{2,6},{6,2},{3,7},{7,3},{8,12},{12,8},{9,1... | collective-permute-start | bytes 76808 | tf_op jit(solution)/shard_map/ppermute | solution.py:484
  154.8 4.6 %collective-permute-start.16 = (bf16[8,3200]{1,0:T(8,128)(2,1)S(1)}, bf16[8,3200]{1,0:T(8,128)(2,1)S(1)}, u32[]{:S(2)}, u32[]{:S(2)}) collective-permute-start(bf16[8,3200]{1,0:T(8,128)(2,1)S(1)} %pad_maximum_fusion.near_ref), channel_id=1, source_target_pairs={{0,128},{128,0},{1,129},{129,1},{2,130},{130,2},{3,131},{131,3},{4... | collective-permute-start | bytes 153608 | tf_op jit(solution)/shard_map/ppermute | solution.py:484

commit v4 on v3

--- a/solution.py
+++ b/solution.py
@@ -172,9 +172,9 @@
     return jnp.concatenate([jnp.where(first, mine, theirs), jnp.where(first, theirs, mine)], axis=0)
 
 
-def k_first_stats(place, x_ref, stats_ref):
-    keep, give = halves(x_ref, place[0] == 0)
-    tokens = jnp.concatenate([keep, give], axis=0).astype(F32)
+def k_first_stats(x_ref, stats_ref):
+    low, high = x_ref[:, 0, 0:PX, :].reshape(HALF, D), x_ref[:, 0, PX : 2 * PX, :].reshape(HALF, D)
+    tokens = jnp.concatenate([low, high], axis=0).astype(F32)
     spread_out(stats_ref, partial_stats(tokens, group_matrix()))
 
 
@@ -348,22 +348,20 @@
 def split_rows(total, refs, cols=slice(None)):
     rows = total.shape[0] // len(refs)
     for s, ref in enumerate(refs):
-        ref[:, cols] = total[s * rows : (s + 1) * rows]
-
-
-def weight_tile(unit, places, keep_ref, recv_ref):
-    row = lax.broadcasted_iota(jnp.int32, (D, D), 0)
+        ref[:, cols] = total[s * rows : (s + 1) * rows].astype(BF16)
+
+
+def weight_tile(unit, order, keep_ref, recv_ref):
     left = jnp.concatenate([keep_ref[:, unit * D : (unit + 1) * D], recv_ref[:, unit * D : (unit + 1) * D]], axis=0)
     cols = slice((2 + unit) * D, (3 + unit) * D)
     right = jnp.concatenate([keep_ref[:, cols], recv_ref[:, cols]], axis=0)
-    order = (row == places).astype(BF16)
-    return t_mm(mm(left, order).astype(BF16), right).astype(BF16)
+    return t_mm(mm(left, order).astype(BF16), right)
 
 
 def k_weights_time(place, table_ref, keep_ref, recv_ref, *out_refs):
-    places = table_ref[place[2]]
+    order = (lax.broadcasted_iota(jnp.int32, (D, D), 0) == table_ref[place[2]]).astype(BF16)
     for unit in range(2):
-        total = weight_tile(unit, places, keep_ref, recv_ref)
+        total = weight_tile(unit, order, keep_ref, recv_ref)
         split_rows(total, out_refs, slice(unit * D, (unit + 1) * D))
 
 
@@ -384,7 +382,7 @@
 
 
 def k_sum_time(*refs):
-    split_rows(added(*refs[:4]), refs[4:])
+    split_rows(added32(*refs[:4]), refs[4:])
 
 
 def k_sum_rows(parts_ref, *refs):
@@ -392,7 +390,8 @@
     chips = out_ref.shape[0]
     rows = times[0].shape[0]
     count = parts_ref.shape[0] // rows
-    view = sum(parts_ref[s * rows : (s + 1) * rows, :].astype(F32) for s in range(count))
+    parts = parts_ref[...].astype(F32)
+    view = sum(parts[s * rows : (s + 1) * rows] for s in range(count))
     time = added32(*times)
     units = [view[:, :D], view[:, D:], time[:, :D], time[:, D:]]
     for row in range(out_ref.shape[2] // D):
@@ -409,15 +408,14 @@
 
 def k_rows(place, near_ref, far_ref, vqkv_ref, vout_ref, tqkv_ref, tout_ref):
     both = jnp.where(place[0] == place[1], near_ref[...].astype(F32), far_ref[...].astype(F32))
-    low, high = both[:4], both[4:]
-    for row in range(vout_ref.shape[0]):
-        cols = slice(row * D, (row + 1) * D)
-        line = slice(row, row + 1)
-        for unit, qkv_ref, out_ref in ((0, vqkv_ref, vout_ref), (2, tqkv_ref, tout_ref)):
-            qkv_ref[line, :D] = low[unit : unit + 1, cols].astype(BF16)
-            qkv_ref[line, D : 2 * D] = low[unit + 1 : unit + 2, cols].astype(BF16)
-            qkv_ref[line, 2 * D :] = high[unit : unit + 1, cols].astype(BF16)
-            out_ref[line, :] = high[unit + 1 : unit + 2, cols].astype(BF16)
+    rows = vout_ref.shape[0]
+
+    def lines(unit):
+        return jnp.concatenate([both[unit : unit + 1, row * D : (row + 1) * D] for row in range(rows)], axis=0)
+
+    for unit, qkv_ref, out_ref in ((0, vqkv_ref, vout_ref), (2, tqkv_ref, tout_ref)):
+        qkv_ref[...] = jnp.concatenate([lines(unit), lines(unit + 1), lines(unit + 4)], axis=1).astype(BF16)
+        out_ref[...] = lines(unit + 5).astype(BF16)
 
 
 def call(kernel, outs, *args, place=None, us=2, vmem=VMEM_LIMIT):
@@ -494,7 +492,7 @@
     views = VIEWS // 2
     rows16 = ((2 * VIEWS, 128), F32)
     x_other, og_other = swap(level_in, "view"), swap(out_grad, "view")
-    (st1,) = call(k_first_stats, [stats], level_in, place=place)
+    (st1,) = call(k_first_stats, [stats], level_in)
     stream, packed_one, sides, own, st2 = call(
         functools.partial(k_view, entries), [tok32, ((T, 3 * D), BF16), ((T, 2 * D), BF16), rows16, stats],
         level_in, x_other, share(st1), view_qkv, view_out, place=place, us=4,

time: 161 us -> 161 us (level)
  no operation moved by 1% of the time
where the time goes in v4:
time: 161 us; the launch traced here: 160 us
  starting transfers between devices  51.1 us (32%)
  blocking collectives  38.7 us (24%)
  waiting for transfers between devices  36.1 us (22%)
  Pallas kernels  24.8 us (15%)
  local copies, waits for them, and re-layouts  8.31 us (5%)
    all_to_all x1, blocking collectives, transpose(): return lax.all_to_all(field, frame_axes, 0, 0, tiled=True)  26 us
    pallas_call x15, Pallas kernels, call(): pl.pallas_call(kernel, out_shape=[jax.ShapeDtypeStruct(shape, dtype) for...  24.8 us
    ppermute x9, starting transfers between devices, swap(): return lax.ppermute(field, axis, [(0, 1), (1, 0)])  16.9 us
    all_to_all x1, blocking collectives, share(): return lax.all_to_all(field, mates, 0, 0, tiled=True)  12.7 us
    all_to_all x2, waiting for transfers between devices, share(): return lax.all_to_all(field, mates, 0, 0, tiled=True)  10.3 us
    unnamed x72, local copies, waits for them, and re-layouts  8.31 us
    ppermute x6, waiting for transfers between devices, shifted(): lax.ppermute(piece, axis, [(i, (i + step + 1) % 4) for i in range(4)])  8.06 us
    ppermute x6, starting transfers between devices, shifted(): lax.ppermute(piece, axis, [(i, (i + step + 1) % 4) for i in range(4)])  7.9 us
  transfers between devices with their start and end apart: 22, of which 12 were waited for; matrix products, arithmetic and copies ran while one was open for 0% of the time, Pallas kernels for 8%

profile of v4, /device:TPU:1, one launch (start us, length us, event | category | flops | bytes accessed | tf_op | source)
XLA Modules:
  0.0 160.1 jit_solution(7760315977973044133)
XLA Ops:
  0.6 0.0 copy-start.9
  0.7 3.7 %collective-permute-start = (bf16[4,1,32,640]{3,2,1,0:T(8,128)(2,1)}, bf16[4,1,32,640]{3,2,1,0:T(8,128)(2,1)S(1)}, u32[]{:S(2)}, u32[]{:S(2)}) collective-permute-start(bf16[4,1,32,640]{3,2,1,0:T(8,128)(2,1)} %x_ref.7), channel_id=1, source_target_pairs={{0,128},{128,0},{1,129},{129,1},{2,130},{130,2},{3,131},{131,3},{4... | collective-permute-start | bytes 491528 | tf_op jit(solution)/shard_map/ppermute | solution.py:482
  4.3 0.9 copy-done.11
  5.3 1.3 shard_map.135
  6.6 4.2 %all-to-all-start = ((f32[8,16,128]{2,1,0:T(8,128)}), f32[8,16,128]{2,1,0:T(8,128)S(1)}, u32[]{:S(2)}, u32[]{:S(2)}) async-start(f32[8,16,128]{2,1,0:T(8,128)} %shard_map.135), calls=%async_computation | async-start | bytes 131072 | tf_op jit(solution)/shard_map/all_to_all | solution.py:476
  10.8 3.0 %collective-permute-start.1 = (bf16[4,1,32,640]{3,2,1,0:T(8,128)(2,1)S(1)}, bf16[4,1,32,640]{3,2,1,0:T(8,128)(2,1)S(1)}, u32[]{:S(2)}, u32[]{:S(2)}) collective-permute-start(bf16[4,1,32,640]{3,2,1,0:T(8,128)(2,1)S(1)} %copy-done.9), channel_id=1, source_target_pairs={{0,128},{128,0},{1,129},{129,1},{2,130},{130,2},{3,131},{131,3},{4... | collective-permute-start | bytes 491528 | tf_op jit(solution)/shard_map/ppermute | solution.py:482
  13.8 0.1 pad_add_fusion.place
  13.9 3.7 %all-to-all-done.g_ref = f32[8,16,128]{2,1,0:T(8,128)S(1)} async-done(((f32[8,16,128]{2,1,0:T(8,128)}), f32[8,16,128]{2,1,0:T(8,128)S(1)}, u32[]{:S(2)}, u32[]{:S(2)}) %all-to-all-start) | async-done | bytes 65568 | tf_op jit(solution)/shard_map/all_to_all | solution.py:476
  17.5 0.0 copy-start.1
  17.5 1.7 %copy-done.1 = bf16[640,1920]{1,0:T(8,128)(2,1)S(1)} copy-done((bf16[640,1920]{1,0:T(8,128)(2,1)S(1)}, bf16[640,1920]{1,0:T(8,128)(2,1)}, u32[]{:S(2)}) %copy-start.1) | copy-done | bytes 2457624
  19.2 3.4 %shard_map.136 = (f32[128,640]{1,0:T(8,128)S(1)}, bf16[128,1920]{1,0:T(8,128)(2,1)S(1)}, bf16[128,1280]{1,0:T(8,128)(2,1)S(1)}, f32[16,128]{1,0:T(8,128)S(1)}, f32[8,16,128]{2,1,0:T(8,128)}) custom-call(s32[3]{0:T(128)S(1)} %pad_add_fusion.place, bf16[4,1,32,640]{3,2,1,0:T(8,128)(2,1)S(1)} %copy-done.12, ...), custom_call_target="tpu_custom_call" | custom-call | flops 4000000000 | bytes 12000000 | tf_op jit(solution)/shard_map/pallas_call | solution.py:426
  22.6 3.3 %all-to-all-start.1 = ((f32[8,16,128]{2,1,0:T(8,128)}), f32[8,16,128]{2,1,0:T(8,128)S(1)}, u32[]{:S(2)}, u32[]{:S(2)}) async-start(f32[8,16,128]{2,1,0:T(8,128)} %get-tuple-element.67), calls=%async_computation.1 | async-start | bytes 131072 | tf_op jit(solution)/shard_map/all_to_all | solution.py:476
  25.9 0.0 collective-permute-done.1.other_ref.ogother_ref
  26.0 0.0 copy-start.16
  26.0 6.6 %all-to-all-done.1.g_ref = f32[8,16,128]{2,1,0:T(8,128)S(1)} async-done(((f32[8,16,128]{2,1,0:T(8,128)}), f32[8,16,128]{2,1,0:T(8,128)S(1)}, u32[]{:S(2)}, u32[]{:S(2)}) %all-to-all-start.1) | async-done | bytes 65568 | tf_op jit(solution)/shard_map/all_to_all | solution.py:476
  32.6 0.9 shard_map.137
  33.5 26.0 %all_to_all.42.recv_ref = bf16[32,4,1280]{2,1,0:T(4,128)(2,1)S(1)} all-to-all(bf16[32,4,1280]{2,1,0:T(4,128)(2,1)S(1)} %get-tuple-element.68), channel_id=1, replica_groups=mesh['view'=2,'z'=8,'xl'=2,'core'=2,'dp'=4] {'z','xl','core'}, dimensions={0} | all-to-all | bytes 655360 | tf_op jit(solution)/shard_map/all_to_all | solution.py:479
  59.5 4.2 %shard_map.138 = (bf16[32,4,1280]{2,1,0:T(4,128)(2,1)}, bf16[128,2560]{1,0:T(8,128)(2,1)S(1)}, bf16[128,2560]{1,0:T(8,128)(2,1)S(1)}) custom-call(s32[3]{0:T(128)S(1)} %pad_add_fusion.place, bf16[32,4,1280]{2,1,0:T(4,128)(2,1)S(1)} %all_to_all.42.recv_ref, bf16[640,1920]{1,0:T(8,128)(2,1)S(1)} %copy-done, bf16[640,640]{1,0:T(8,128)(2,1)S(1)} %copy-done.3), custom_call_target="tpu_custom_call" | custom-call | flops 6000000000 | bytes 18000000 | tf_op jit(solution)/shard_map/pallas_call | solution.py:426
  63.7 0.9 copy-done.32
  64.5 1.3 collective-permute-start.2
  65.8 3.7 %all-to-all-start.3 = ((bf16[32,4,1280]{2,1,0:T(4,128)(2,1)}), bf16[32,4,1280]{2,1,0:T(4,128)(2,1)S(1)}, u32[]{:S(2)}, u32[]{:S(2)}) async-start(bf16[32,4,1280]{2,1,0:T(4,128)(2,1)} %get-tuple-element.69), calls=%async_computation.3 | async-start | bytes 655360 | tf_op jit(solution)/shard_map/all_to_all | solution.py:479
  69.5 0.3 collective-permute-start.3
  69.8 1.1 copy-done.33
  70.9 2.8 %shard_map.139 = (bf16[160,1280]{1,0:T(8,128)(2,1)S(1)}, bf16[160,1280]{1,0:T(8,128)(2,1)}, bf16[160,1280]{1,0:T(8,128)(2,1)S(1)}, bf16[160,1280]{1,0:T(8,128)(2,1)S(1)}) custom-call(s32[3]{0:T(128)S(1)} %pad_add_fusion.place, s32[16,1,640]{2,1,0:T(1,128)S(1)} %copy-done.19, bf16[128,2560]{1,0:T(8,128)(2,1)S(1)} %copy-done.33, ...), custom_call_target="tpu_custom_call" | custom-call | flops 3000000000 | bytes 9000000 | tf_op jit(solution)/shard_map/pallas_call | solution.py:426
  73.7 0.8 copy-done.26
  74.5 0.3 collective-permute-start.4
  74.8 1.8 %collective-permute-start.5 = (bf16[160,1280]{1,0:T(8,128)(2,1)S(1)}, bf16[160,1280]{1,0:T(8,128)(2,1)S(1)}, u32[]{:S(2)}, u32[]{:S(2)}) collective-permute-start(bf16[160,1280]{1,0:T(8,128)(2,1)S(1)} %get-tuple-element.73), channel_id=1, source_target_pairs={{0,2},{1,3},{2,0},{3,1},{4,6},{5,7},{6,4},{7,5},{8,10},{9,11},{10,... | collective-permute-start | bytes 1228808 | tf_op jit(solution)/shard_map/ppermute | solution.py:486
  76.5 0.8 collective-permute-start.6
  77.4 1.3 shard_map.140.left_ref
  78.7 0.9 copy-done.20
  79.6 2.6 %all-to-all-done.3.back_ref = bf16[32,4,1280]{2,1,0:T(4,128)(2,1)S(1)} async-done(((bf16[32,4,1280]{2,1,0:T(4,128)(2,1)}), bf16[32,4,1280]{2,1,0:T(4,128)(2,1)S(1)}, u32[]{:S(2)}, u32[]{:S(2)}) %all-to-all-start.3) | async-done | bytes 327712 | tf_op jit(solution)/shard_map/all_to_all | solution.py:479
  82.1 1.0 copy-done.23
  83.1 0.6 shard_map.141
  83.7 12.7 %all_to_all.43.g_ref = f32[8,16,128]{2,1,0:T(8,128)S(1)} all-to-all(f32[8,16,128]{2,1,0:T(8,128)S(1)} %shard_map.141), channel_id=1, replica_groups=mesh['view'=2,'z'=8,'xl'=2,'core'=2,'dp'=4] {'view','dp'}, dimensions={0} | all-to-all | bytes 131072 | tf_op jit(solution)/shard_map/all_to_all | solution.py:476
  96.4 0.0 collective-permute-done.6.refs_3_
  96.5 2.3 %shard_map.142 = (bf16[128,1280]{1,0:T(8,128)(2,1)S(1)}, bf16[128,1280]{1,0:T(8,128)(2,1)S(1)}, bf16[128,1920]{1,0:T(8,128)(2,1)S(1)}, f32[128,640]{1,0:T(8,128)S(1)}, f32[16,128]{1,0:T(8,128)S(1)}) custom-call(s32[3]{0:T(128)S(1)} %pad_add_fusion.place, bf16[32,4,1280]{2,1,0:T(4,128)(2,1)S(1)} %all-to-all-done.3.back_ref, f32[128,640]{1,0:T(8,128)S(1)} %copy-done.24, ...), custom_call_target="tpu_custom_call" | custom-call | flops 5000000000 | bytes 15000000 | tf_op jit(solution)/shard_map/pallas_call | solution.py:426
  98.9 1.3 collective-permute-start.7
  100.1 1.3 collective-permute-done.7.theirs_ref
  101.4 1.9 %shard_map.143 = bf16[640,1280]{1,0:T(8,128)(2,1)} custom-call(bf16[2,640,256]{2,1,0:T(8,128)(2,1)S(1)} %copy-done.21, bf16[128,1280]{1,0:T(8,128)(2,1)S(1)} %get-tuple-element.86.mine_ref, bf16[128,1280]{1,0:T(8,128)(2,1)S(1)} %collective-permute-done.7.theirs_ref), custom_call_target="tpu_custom_call" | custom-call | flops 1000000000 | bytes 3000000 | tf_op jit(solution)/shard_map/pallas_call | solution.py:426
  103.3 5.1 %all-to-all-start.5 = ((bf16[16,40,1280]{2,1,0:T(8,128)(2,1)}), bf16[16,40,1280]{2,1,0:T(8,128)(2,1)S(1)}, u32[]{:S(2)}, u32[]{:S(2)}) async-start(bf16[16,40,1280]{2,1,0:T(8,128)(2,1)} %bitcast.3), calls=%async_computation.5 | async-start | bytes 3276800 | tf_op jit(solution)/shard_map/all_to_all | solution.py:523
  108.4 1.0 copy-done.27
  109.4 0.2 shard_map.144
  109.7 1.4 collective-permute-start.8
  111.1 2.4 %collective-permute-start.9 = (bf16[40,1280]{1,0:T(8,128)(2,1)S(1)}, bf16[40,1280]{1,0:T(8,128)(2,1)S(1)}, u32[]{:S(2)}, u32[]{:S(2)}) collective-permute-start(bf16[40,1280]{1,0:T(8,128)(2,1)S(1)} %get-tuple-element.96), channel_id=1, source_target_pairs={{0,128},{8,136},{128,0},{136,8},{1,129},{9,137},{129,1},{137,9},{2... | collective-permute-start | bytes 307208 | tf_op jit(solution)/shard_map/ppermute | solution.py:486
  113.5 1.2 collective-permute-start.10
  114.7 1.7 %shard_map.145 = (f32[64,640]{1,0:T(8,128)S(1)}, bf16[64,640]{1,0:T(8,128)(2,1)S(1)}, bf16[64,1280]{1,0:T(8,128)(2,1)S(1)}, f32[16,128]{1,0:T(8,128)S(1)}) custom-call(s32[3]{0:T(128)S(1)} %pad_add_fusion.place, bf16[128,1920]{1,0:T(8,128)(2,1)S(1)} %copy-done.29, f32[128,640]{1,0:T(8,128)S(1)} %copy-done.31, ...), custom_call_target="tpu_custom_call" | custom-call | flops 3000000000 | bytes 9000000 | tf_op jit(solution)/shard_map/pallas_call | solution.py:426
  116.4 2.8 %collective-permute-start.11 = (f32[16,128]{1,0:T(8,128)S(1)}, f32[16,128]{1,0:T(8,128)S(1)}, u32[]{:S(2)}, u32[]{:S(2)}) collective-permute-start(f32[16,128]{1,0:T(8,128)S(1)} %get-tuple-element.101), channel_id=1, source_target_pairs={{0,2},{1,3},{2,0},{3,1},{4,6},{5,7},{6,4},{7,5},{8,10},{9,11},{10,... | collective-permute-start | bytes 24584 | tf_op jit(solution)/shard_map/ppermute | solution.py:490
  119.2 2.1 %collective-permute-done.11 = f32[16,128]{1,0:T(8,128)S(1)} collective-permute-done((f32[16,128]{1,0:T(8,128)S(1)}, f32[16,128]{1,0:T(8,128)S(1)}, u32[]{:S(2)}, u32[]{:S(2)}) %collective-permute-start.11) | collective-permute-done | bytes 8224 | tf_op jit(solution)/shard_map/ppermute | solution.py:490
  121.4 0.6 collective-permute-start.12
  122.0 3.4 %collective-permute-done.12 = f32[16,128]{1,0:T(8,128)S(1)} collective-permute-done((f32[16,128]{1,0:T(8,128)S(1)}, f32[16,128]{1,0:T(8,128)S(1)}, u32[]{:S(2)}, u32[]{:S(2)}) %collective-permute-start.12) | collective-permute-done | bytes 8224 | tf_op jit(solution)/shard_map/ppermute | solution.py:490
  125.4 4.9 %collective-permute-done.8.refs_1_ = bf16[40,1280]{1,0:T(8,128)(2,1)S(1)} collective-permute-done((bf16[40,1280]{1,0:T(8,128)(2,1)S(1)}, bf16[40,1280]{1,0:T(8,128)(2,1)S(1)}, u32[]{:S(2)}, u32[]{:S(2)}) %collective-permute-start.8) | collective-permute-done | bytes 102432 | tf_op jit(solution)/shard_map/ppermute | solution.py:486
  130.4 3.1 %collective-permute-done.9.refs_2_ = bf16[40,1280]{1,0:T(8,128)(2,1)S(1)} collective-permute-done((bf16[40,1280]{1,0:T(8,128)(2,1)S(1)}, bf16[40,1280]{1,0:T(8,128)(2,1)S(1)}, u32[]{:S(2)}, u32[]{:S(2)}) %collective-permute-start.9) | collective-permute-done | bytes 102432 | tf_op jit(solution)/shard_map/ppermute | solution.py:486
  133.5 1.3 shard_map.146
  134.8 6.5 %all-to-all-start.6 = ((bf16[8,4,3200]{2,1,0:T(4,128)(2,1)}), bf16[8,4,3200]{2,1,0:T(4,128)(2,1)S(1)}, u32[]{:S(2)}, u32[]{:S(2)}) async-start(bf16[8,4,3200]{2,1,0:T(4,128)(2,1)} %shard_map.146), calls=%async_computation.6 | async-start | bytes 409600 | tf_op jit(solution)/shard_map/all_to_all | solution.py:529
  141.3 1.5 collective-permute-start.14
  142.7 1.5 collective-permute-start.13
  144.2 2.8 %collective-permute-done.13 = f32[16,128]{1,0:T(8,128)S(1)} collective-permute-done((f32[16,128]{1,0:T(8,128)S(1)}, f32[16,128]{1,0:T(8,128)S(1)}, u32[]{:S(2)}, u32[]{:S(2)}) %collective-permute-start.13) | collective-permute-done | bytes 8224 | tf_op jit(solution)/shard_map/ppermute | solution.py:482
  147.0 3.0 %all-to-all-done.6.parts_ref = bf16[8,4,3200]{2,1,0:T(4,128)(2,1)S(1)} async-done(((bf16[8,4,3200]{2,1,0:T(4,128)(2,1)}), bf16[8,4,3200]{2,1,0:T(4,128)(2,1)S(1)}, u32[]{:S(2)}, u32[]{:S(2)}) %all-to-all-start.6) | async-done | bytes 204832 | tf_op jit(solution)/shard_map/all_to_all | solution.py:529
  150.1 3.3 %collective-permute-start.15 = (bf16[4,3200]{1,0:T(4,128)(2,1)S(1)}, bf16[4,3200]{1,0:T(4,128)(2,1)S(1)}, u32[]{:S(2)}, u32[]{:S(2)}) collective-permute-start(bf16[4,3200]{1,0:T(4,128)(2,1)S(1)} %shard_map.148), channel_id=1, source_target_pairs={{0,4},{4,0},{1,5},{5,1},{2,6},{6,2},{3,7},{7,3},{8,12},{12,8},{9,1... | collective-permute-start | bytes 76808 | tf_op jit(solution)/shard_map/ppermute | solution.py:482
  153.4 0.9 collective-permute-done.15
  154.3 1.2 collective-permute-start.16
  155.5 1.6 %shard_map.147 = (bf16[4,32,640]{2,1,0:T(8,128)(2,1)}, bf16[4,32,640]{2,1,0:T(8,128)(2,1)}, f32[4,4,128]{2,1,0:T(4,128)}) custom-call(s32[3]{0:T(128)S(1)} %pad_add_fusion.place, f32[16,128]{1,0:T(8,128)S(1)} %add.19.g_ref, f32[16,128]{1,0:T(8,128)S(1)} %get-tuple-element.113.sumstwo_ref, f32[16,128]{1,0:T(8,128)S(1)} %get-tuple-element.100.own_ref, ...), custom_call_target="tpu_custom_call" | custom-call | flops 3000000000 | bytes 9000000 | tf_op jit(solution)/shard_map/pallas_call | solution.py:426
  157.1 1.7 %collective-permute-done.16.far_ref = bf16[8,3200]{1,0:T(8,128)(2,1)S(1)} collective-permute-done((bf16[8,3200]{1,0:T(8,128)(2,1)S(1)}, bf16[8,3200]{1,0:T(8,128)(2,1)S(1)}, u32[]{:S(2)}, u32[]{:S(2)}) %collective-permute-start.16) | collective-permute-done | bytes 51232 | tf_op jit(solution)/shard_map/ppermute | solution.py:482
  158.9 1.2 shard_map.149
  (75 shorter events, 0.2 us)
Async XLA Ops:
  0.6 10.2 %copy-start.9 = (bf16[4,1,32,640]{3,2,1,0:T(8,128)(2,1)S(1)}, bf16[4,1,32,640]{3,2,1,0:T(8,128)(2,1)}, u32[]{:S(2)}) copy-start(bf16[4,1,32,640]{3,2,1,0:T(8,128)(2,1)} %og_ref.1) | copy-start | bytes 491524
  0.6 16.9 %copy-start.4 = (bf16[640,640]{1,0:T(8,128)(2,1)S(1)}, bf16[640,640]{1,0:T(8,128)(2,1)}, u32[]{:S(2)}) copy-start(bf16[640,640]{1,0:T(8,128)(2,1)} %wout_ref.5) | copy-start | bytes 2457604
  0.7 16.9 %collective-permute-start = (bf16[4,1,32,640]{3,2,1,0:T(8,128)(2,1)}, bf16[4,1,32,640]{3,2,1,0:T(8,128)(2,1)S(1)}, u32[]{:S(2)}, u32[]{:S(2)}) collective-permute-start(bf16[4,1,32,640]{3,2,1,0:T(8,128)(2,1)} %x_ref.7), channel_id=1, source_target_pairs={{0,128},{128,0},{1,129},{129,1},{2,130},{130,2},{3,131},{131,3},{4... | collective-permute-start | bytes 491528 | tf_op jit(solution)/shard_map/ppermute | solution.py:482
  4.3 0.9 copy-start.11
  5.3 12.3 %copy-start.12 = (bf16[4,1,32,640]{3,2,1,0:T(8,128)(2,1)S(1)}, bf16[4,1,32,640]{3,2,1,0:T(8,128)(2,1)}, u32[]{:S(2)}) copy-start(bf16[4,1,32,640]{3,2,1,0:T(8,128)(2,1)} %x_ref.7) | copy-start | bytes 491524
  6.6 10.9 %all-to-all-start = ((f32[8,16,128]{2,1,0:T(8,128)}), f32[8,16,128]{2,1,0:T(8,128)S(1)}, u32[]{:S(2)}, u32[]{:S(2)}) async-start(f32[8,16,128]{2,1,0:T(8,128)} %shard_map.135), calls=%async_computation | async-start | bytes 131072 | tf_op jit(solution)/shard_map/all_to_all | solution.py:476
  10.8 15.1 %collective-permute-start.1 = (bf16[4,1,32,640]{3,2,1,0:T(8,128)(2,1)S(1)}, bf16[4,1,32,640]{3,2,1,0:T(8,128)(2,1)S(1)}, u32[]{:S(2)}, u32[]{:S(2)}) collective-permute-start(bf16[4,1,32,640]{3,2,1,0:T(8,128)(2,1)S(1)} %copy-done.9), channel_id=1, source_target_pairs={{0,128},{128,0},{1,129},{129,1},{2,130},{130,2},{3,131},{131,3},{4... | collective-permute-start | bytes 491528 | tf_op jit(solution)/shard_map/ppermute | solution.py:482
  17.5 1.7 %copy-start.1 = (bf16[640,1920]{1,0:T(8,128)(2,1)S(1)}, bf16[640,1920]{1,0:T(8,128)(2,1)}, u32[]{:S(2)}) copy-start(bf16[640,1920]{1,0:T(8,128)(2,1)} %wqkv_ref.5) | copy-start | bytes 7372804
  19.2 3.4 %copy-start.14 = (bf16[4,1,32,640]{3,2,1,0:T(8,128)(2,1)}, bf16[4,1,32,640]{3,2,1,0:T(8,128)(2,1)S(1)}, u32[]{:S(2)}) copy-start(bf16[4,1,32,640]{3,2,1,0:T(8,128)(2,1)S(1)} %collective-permute-done.other_ref) | copy-start | bytes 491524
  22.6 10.9 %copy-start.22 = (f32[128,640]{1,0:T(8,128)}, f32[128,640]{1,0:T(8,128)S(1)}, u32[]{:S(2)}) copy-start(f32[128,640]{1,0:T(8,128)S(1)} %get-tuple-element.66.stream_ref) | copy-start | bytes 983044
  22.6 10.9 %copy-start.34 = (bf16[128,1920]{1,0:T(8,128)(2,1)}, bf16[128,1920]{1,0:T(8,128)(2,1)S(1)}, u32[]{:S(2)}) copy-start(bf16[128,1920]{1,0:T(8,128)(2,1)S(1)} %get-tuple-element.85.packed_ref) | copy-start | bytes 1474564
  22.6 10.0 %all-to-all-start.1 = ((f32[8,16,128]{2,1,0:T(8,128)}), f32[8,16,128]{2,1,0:T(8,128)S(1)}, u32[]{:S(2)}, u32[]{:S(2)}) async-start(f32[8,16,128]{2,1,0:T(8,128)} %get-tuple-element.67), calls=%async_computation.1 | async-start | bytes 131072 | tf_op jit(solution)/shard_map/all_to_all | solution.py:476
  26.0 7.5 %copy-start.16 = (bf16[4,1,32,640]{3,2,1,0:T(8,128)(2,1)}, bf16[4,1,32,640]{3,2,1,0:T(8,128)(2,1)S(1)}, u32[]{:S(2)}) copy-start(bf16[4,1,32,640]{3,2,1,0:T(8,128)(2,1)S(1)} %collective-permute-done.1.other_ref.ogother_ref) | copy-start | bytes 491524
  32.6 26.9 %copy-start = (bf16[640,1920]{1,0:T(8,128)(2,1)S(1)}, bf16[640,1920]{1,0:T(8,128)(2,1)}, u32[]{:S(2)}) copy-start(bf16[640,1920]{1,0:T(8,128)(2,1)} %wqkv_ref.4) | copy-start | bytes 7372804
  32.6 26.9 %copy-start.3 = (bf16[640,640]{1,0:T(8,128)(2,1)S(1)}, bf16[640,640]{1,0:T(8,128)(2,1)}, u32[]{:S(2)}) copy-start(bf16[640,640]{1,0:T(8,128)(2,1)} %wout_ref.4) | copy-start | bytes 2457604
  59.5 10.3 %copy-start.19 = (s32[16,1,640]{2,1,0:T(1,128)S(1)}, s32[16,1,640]{2,1,0:T(1,128)}, u32[]{:S(2)}) copy-start(s32[16,1,640]{2,1,0:T(1,128)} %constant.26.clone.table_ref) | copy-start | bytes 122884
  63.7 0.9 copy-start.32
  64.5 5.2 %collective-permute-start.2 = (bf16[128,2560]{1,0:T(8,128)(2,1)S(1)}, bf16[128,2560]{1,0:T(8,128)(2,1)S(1)}, u32[]{:S(2)}, u32[]{:S(2)}) collective-permute-start(bf16[128,2560]{1,0:T(8,128)(2,1)S(1)} %get-tuple-element.71), channel_id=1, source_target_pairs={{0,4},{4,0},{1,5},{5,1},{2,6},{6,2},{3,7},{7,3},{8,12},{12,8},{9,1... | collective-permute-start | bytes 1966088 | tf_op jit(solution)/shard_map/ppermute | solution.py:482
  65.8 16.3 %all-to-all-start.3 = ((bf16[32,4,1280]{2,1,0:T(4,128)(2,1)}), bf16[32,4,1280]{2,1,0:T(4,128)(2,1)S(1)}, u32[]{:S(2)}, u32[]{:S(2)}) async-start(bf16[32,4,1280]{2,1,0:T(4,128)(2,1)} %get-tuple-element.69), calls=%async_computation.3 | async-start | bytes 655360 | tf_op jit(solution)/shard_map/all_to_all | solution.py:479
  69.5 7.9 %collective-permute-start.3 = (bf16[128,1280]{1,0:T(8,128)(2,1)S(1)}, bf16[128,1280]{1,0:T(8,128)(2,1)S(1)}, u32[]{:S(2)}, u32[]{:S(2)}) collective-permute-start(bf16[128,1280]{1,0:T(8,128)(2,1)S(1)} %get-tuple-element.75.mine_ref), channel_id=1, source_target_pairs={{0,4},{4,0},{1,5},{5,1},{2,6},{6,2},{3,7},{7,3},{8,12},{12,8},{9,1... | collective-permute-start | bytes 983048 | tf_op jit(solution)/shard_map/ppermute | solution.py:482
  69.8 1.1 copy-start.33
  70.9 6.5 %copy-start.18 = (s32[640,1]{1,0:T(8,128)S(1)}, s32[640,1]{1,0:T(8,128)}, u32[]{:S(2)}) copy-start(s32[640,1]{1,0:T(8,128)} %constant.27.clone.column_ref) | copy-start | bytes 7684
  73.7 0.8 copy-start.26
  74.5 21.9 %collective-permute-start.4 = (bf16[160,1280]{1,0:T(8,128)(2,1)}, bf16[160,1280]{1,0:T(8,128)(2,1)S(1)}, u32[]{:S(2)}, u32[]{:S(2)}) collective-permute-start(bf16[160,1280]{1,0:T(8,128)(2,1)} %get-tuple-element.72), channel_id=1, source_target_pairs={{0,1},{1,2},{2,3},{3,0},{4,5},{5,6},{6,7},{7,4},{8,9},{9,10},{10,1... | collective-permute-start | bytes 1228808 | tf_op jit(solution)/shard_map/ppermute | solution.py:486
  74.8 21.7 %collective-permute-start.5 = (bf16[160,1280]{1,0:T(8,128)(2,1)S(1)}, bf16[160,1280]{1,0:T(8,128)(2,1)S(1)}, u32[]{:S(2)}, u32[]{:S(2)}) collective-permute-start(bf16[160,1280]{1,0:T(8,128)(2,1)S(1)} %get-tuple-element.73), channel_id=1, source_target_pairs={{0,2},{1,3},{2,0},{3,1},{4,6},{5,7},{6,4},{7,5},{8,10},{9,11},{10,... | collective-permute-start | bytes 1228808 | tf_op jit(solution)/shard_map/ppermute | solution.py:486
  76.5 19.9 %collective-permute-start.6 = (bf16[160,1280]{1,0:T(8,128)(2,1)S(1)}, bf16[160,1280]{1,0:T(8,128)(2,1)S(1)}, u32[]{:S(2)}, u32[]{:S(2)}) collective-permute-start(bf16[160,1280]{1,0:T(8,128)(2,1)S(1)} %get-tuple-element.74), channel_id=1, source_target_pairs={{0,3},{1,0},{2,1},{3,2},{4,7},{5,4},{6,5},{7,6},{8,11},{9,8},{10,9... | collective-permute-start | bytes 1228808 | tf_op jit(solution)/shard_map/ppermute | solution.py:486
  78.7 0.9 copy-start.20
  79.6 16.9 %copy-start.10 = (bf16[4,1,32,640]{3,2,1,0:T(8,128)(2,1)S(1)}, bf16[4,1,32,640]{3,2,1,0:T(8,128)(2,1)}, u32[]{:S(2)}) copy-start(bf16[4,1,32,640]{3,2,1,0:T(8,128)(2,1)} %og_ref.1) | copy-start | bytes 491524
  79.6 16.9 %copy-start.17 = (bf16[4,1,32,640]{3,2,1,0:T(8,128)(2,1)S(1)}, bf16[4,1,32,640]{3,2,1,0:T(8,128)(2,1)}, u32[]{:S(2)}) copy-start(bf16[4,1,32,640]{3,2,1,0:T(8,128)(2,1)} %copy-done.16) | copy-start | bytes 491524
  82.1 1.0 copy-start.23
  83.1 13.4 %copy-start.24 = (f32[128,640]{1,0:T(8,128)S(1)}, f32[128,640]{1,0:T(8,128)}, u32[]{:S(2)}) copy-start(f32[128,640]{1,0:T(8,128)} %copy-done.22) | copy-start | bytes 983044
  83.1 13.4 %copy-start.35 = (bf16[128,1920]{1,0:T(8,128)(2,1)S(1)}, bf16[128,1920]{1,0:T(8,128)(2,1)}, u32[]{:S(2)}) copy-start(bf16[128,1920]{1,0:T(8,128)(2,1)} %copy-done.34) | copy-start | bytes 1474564
  96.4 2.4 %copy-start.5 = (bf16[160,1280]{1,0:T(8,128)(2,1)}, bf16[160,1280]{1,0:T(8,128)(2,1)S(1)}, u32[]{:S(2)}) copy-start(bf16[160,1280]{1,0:T(8,128)(2,1)S(1)} %collective-permute-done.5.refs_2_) | copy-start | bytes 1228804
  96.4 2.4 %copy-start.7 = (bf16[160,1280]{1,0:T(8,128)(2,1)}, bf16[160,1280]{1,0:T(8,128)(2,1)S(1)}, u32[]{:S(2)}) copy-start(bf16[160,1280]{1,0:T(8,128)(2,1)S(1)} %collective-permute-done.6.refs_3_) | copy-start | bytes 1228804
  96.5 4.9 %copy-start.21 = (bf16[2,640,256]{2,1,0:T(8,128)(2,1)S(1)}, bf16[2,640,256]{2,1,0:T(8,128)(2,1)}, u32[]{:S(2)}) copy-start(bf16[2,640,256]{2,1,0:T(8,128)(2,1)} %copy-done.20) | copy-start | bytes 1966084
  98.8 4.4 %copy-start.28 = (bf16[128,1920]{1,0:T(8,128)(2,1)}, bf16[128,1920]{1,0:T(8,128)(2,1)S(1)}, u32[]{:S(2)}) copy-start(bf16[128,1920]{1,0:T(8,128)(2,1)S(1)} %get-tuple-element.98.pgrad_ref) | copy-start | bytes 1474564
  98.8 4.4 %copy-start.30 = (f32[128,640]{1,0:T(8,128)}, f32[128,640]{1,0:T(8,128)S(1)}, u32[]{:S(2)}) copy-start(f32[128,640]{1,0:T(8,128)S(1)} %get-tuple-element.99.stream_grad_ref) | copy-start | bytes 983044
  98.9 2.5 %collective-permute-start.7 = (bf16[128,1280]{1,0:T(8,128)(2,1)S(1)}, bf16[128,1280]{1,0:T(8,128)(2,1)S(1)}, u32[]{:S(2)}, u32[]{:S(2)}) collective-permute-start(bf16[128,1280]{1,0:T(8,128)(2,1)S(1)} %get-tuple-element.87), channel_id=1, source_target_pairs={{0,4},{4,0},{1,5},{5,1},{2,6},{6,2},{3,7},{7,3},{8,12},{12,8},{9,1... | collective-permute-start | bytes 983048 | tf_op jit(solution)/shard_map/ppermute | solution.py:482
  103.3 5.1 %copy-start.6 = (bf16[160,1280]{1,0:T(8,128)(2,1)S(1)}, bf16[160,1280]{1,0:T(8,128)(2,1)}, u32[]{:S(2)}) copy-start(bf16[160,1280]{1,0:T(8,128)(2,1)} %copy-done.5) | copy-start | bytes 1228804
  103.3 5.1 %copy-start.8 = (bf16[160,1280]{1,0:T(8,128)(2,1)S(1)}, bf16[160,1280]{1,0:T(8,128)(2,1)}, u32[]{:S(2)}) copy-start(bf16[160,1280]{1,0:T(8,128)(2,1)} %copy-done.7) | copy-start | bytes 1228804
  103.3 30.2 %all-to-all-start.5 = ((bf16[16,40,1280]{2,1,0:T(8,128)(2,1)}), bf16[16,40,1280]{2,1,0:T(8,128)(2,1)S(1)}, u32[]{:S(2)}, u32[]{:S(2)}) async-start(bf16[16,40,1280]{2,1,0:T(8,128)(2,1)} %bitcast.3), calls=%async_computation.5 | async-start | bytes 3276800 | tf_op jit(solution)/shard_map/all_to_all | solution.py:523
  108.4 1.0 copy-start.27
  109.4 5.3 %copy-start.2 = (bf16[640,1920]{1,0:T(8,128)(2,1)S(1)}, bf16[640,1920]{1,0:T(8,128)(2,1)}, u32[]{:S(2)}) copy-start(bf16[640,1920]{1,0:T(8,128)(2,1)} %wqkv_ref.5) | copy-start | bytes 7372804
  109.4 5.3 %copy-start.13 = (bf16[4,1,32,640]{3,2,1,0:T(8,128)(2,1)S(1)}, bf16[4,1,32,640]{3,2,1,0:T(8,128)(2,1)}, u32[]{:S(2)}) copy-start(bf16[4,1,32,640]{3,2,1,0:T(8,128)(2,1)} %x_ref.7) | copy-start | bytes 491524
  109.4 5.3 %copy-start.15 = (bf16[4,1,32,640]{3,2,1,0:T(8,128)(2,1)S(1)}, bf16[4,1,32,640]{3,2,1,0:T(8,128)(2,1)}, u32[]{:S(2)}) copy-start(bf16[4,1,32,640]{3,2,1,0:T(8,128)(2,1)} %copy-done.14) | copy-start | bytes 491524
  109.4 5.3 %copy-start.25 = (f32[128,640]{1,0:T(8,128)S(1)}, f32[128,640]{1,0:T(8,128)}, u32[]{:S(2)}) copy-start(f32[128,640]{1,0:T(8,128)} %copy-done.22) | copy-start | bytes 983044
  109.4 5.3 %copy-start.29 = (bf16[128,1920]{1,0:T(8,128)(2,1)S(1)}, bf16[128,1920]{1,0:T(8,128)(2,1)}, u32[]{:S(2)}) copy-start(bf16[128,1920]{1,0:T(8,128)(2,1)} %copy-done.28) | copy-start | bytes 1474564
  109.4 5.3 %copy-start.31 = (f32[128,640]{1,0:T(8,128)S(1)}, f32[128,640]{1,0:T(8,128)}, u32[]{:S(2)}) copy-start(f32[128,640]{1,0:T(8,128)} %copy-done.30) | copy-start | bytes 983044
  109.7 20.7 %collective-permute-start.8 = (bf16[40,1280]{1,0:T(8,128)(2,1)S(1)}, bf16[40,1280]{1,0:T(8,128)(2,1)S(1)}, u32[]{:S(2)}, u32[]{:S(2)}) collective-permute-start(bf16[40,1280]{1,0:T(8,128)(2,1)S(1)} %get-tuple-element.95), channel_id=1, source_target_pairs={{0,8},{8,128},{128,136},{136,0},{1,9},{9,129},{129,137},{137,1},{2... | collective-permute-start | bytes 307208 | tf_op jit(solution)/shard_map/ppermute | solution.py:486
  111.1 22.4 %collective-permute-start.9 = (bf16[40,1280]{1,0:T(8,128)(2,1)S(1)}, bf16[40,1280]{1,0:T(8,128)(2,1)S(1)}, u32[]{:S(2)}, u32[]{:S(2)}) collective-permute-start(bf16[40,1280]{1,0:T(8,128)(2,1)S(1)} %get-tuple-element.96), channel_id=1, source_target_pairs={{0,128},{8,136},{128,0},{136,8},{1,129},{9,137},{129,1},{137,9},{2... | collective-permute-start | bytes 307208 | tf_op jit(solution)/shard_map/ppermute | solution.py:486
  113.5 20.0 %collective-permute-start.10 = (bf16[40,1280]{1,0:T(8,128)(2,1)S(1)}, bf16[40,1280]{1,0:T(8,128)(2,1)S(1)}, u32[]{:S(2)}, u32[]{:S(2)}) collective-permute-start(bf16[40,1280]{1,0:T(8,128)(2,1)S(1)} %get-tuple-element.97), channel_id=1, source_target_pairs={{0,136},{8,0},{128,8},{136,128},{1,137},{9,1},{129,9},{137,129},{2... | collective-permute-start | bytes 307208 | tf_op jit(solution)/shard_map/ppermute | solution.py:486
  116.4 4.9 %collective-permute-start.11 = (f32[16,128]{1,0:T(8,128)S(1)}, f32[16,128]{1,0:T(8,128)S(1)}, u32[]{:S(2)}, u32[]{:S(2)}) collective-permute-start(f32[16,128]{1,0:T(8,128)S(1)} %get-tuple-element.101), channel_id=1, source_target_pairs={{0,2},{1,3},{2,0},{3,1},{4,6},{5,7},{6,4},{7,5},{8,10},{9,11},{10,... | collective-permute-start | bytes 24584 | tf_op jit(solution)/shard_map/ppermute | solution.py:490
  121.4 4.1 %collective-permute-start.12 = (f32[16,128]{1,0:T(8,128)S(1)}, f32[16,128]{1,0:T(8,128)S(1)}, u32[]{:S(2)}, u32[]{:S(2)}) collective-permute-start(f32[16,128]{1,0:T(8,128)S(1)} %add.17), channel_id=1, source_target_pairs={{0,1},{1,0},{2,3},{3,2},{4,5},{5,4},{6,7},{7,6},{8,9},{9,8},{10,11... | collective-permute-start | bytes 24584 | tf_op jit(solution)/shard_map/ppermute | solution.py:490
  134.8 15.3 %all-to-all-start.6 = ((bf16[8,4,3200]{2,1,0:T(4,128)(2,1)}), bf16[8,4,3200]{2,1,0:T(4,128)(2,1)S(1)}, u32[]{:S(2)}, u32[]{:S(2)}) async-start(bf16[8,4,3200]{2,1,0:T(4,128)(2,1)} %shard_map.146), calls=%async_computation.6 | async-start | bytes 409600 | tf_op jit(solution)/shard_map/all_to_all | solution.py:529
  141.3 5.8 %collective-permute-start.14 = (bf16[64,1280]{1,0:T(8,128)(2,1)S(1)}, bf16[64,1280]{1,0:T(8,128)(2,1)S(1)}, u32[]{:S(2)}, u32[]{:S(2)}) collective-permute-start(bf16[64,1280]{1,0:T(8,128)(2,1)S(1)} %get-tuple-element.111), channel_id=1, source_target_pairs={{0,128},{128,0},{1,129},{129,1},{2,130},{130,2},{3,131},{131,3},{4... | collective-permute-start | bytes 491528 | tf_op jit(solution)/shard_map/ppermute | solution.py:482
  142.7 4.3 %collective-permute-start.13 = (f32[16,128]{1,0:T(8,128)S(1)}, f32[16,128]{1,0:T(8,128)S(1)}, u32[]{:S(2)}, u32[]{:S(2)}) collective-permute-start(f32[16,128]{1,0:T(8,128)S(1)} %add.18), channel_id=1, source_target_pairs={{0,128},{128,0},{1,129},{129,1},{2,130},{130,2},{3,131},{131,3},{4... | collective-permute-start | bytes 24584 | tf_op jit(solution)/shard_map/ppermute | solution.py:482
  150.1 4.1 %collective-permute-start.15 = (bf16[4,3200]{1,0:T(4,128)(2,1)S(1)}, bf16[4,3200]{1,0:T(4,128)(2,1)S(1)}, u32[]{:S(2)}, u32[]{:S(2)}) collective-permute-start(bf16[4,3200]{1,0:T(4,128)(2,1)S(1)} %shard_map.148), channel_id=1, source_target_pairs={{0,4},{4,0},{1,5},{5,1},{2,6},{6,2},{3,7},{7,3},{8,12},{12,8},{9,1... | collective-permute-start | bytes 76808 | tf_op jit(solution)/shard_map/ppermute | solution.py:482
  154.3 4.6 %collective-permute-start.16 = (bf16[8,3200]{1,0:T(8,128)(2,1)S(1)}, bf16[8,3200]{1,0:T(8,128)(2,1)S(1)}, u32[]{:S(2)}, u32[]{:S(2)}) collective-permute-start(bf16[8,3200]{1,0:T(8,128)(2,1)S(1)} %pad_maximum_fusion.near_ref), channel_id=1, source_target_pairs={{0,128},{128,0},{1,129},{129,1},{2,130},{130,2},{3,131},{131,3},{4... | collective-permute-start | bytes 153608 | tf_op jit(solution)/shard_map/ppermute | solution.py:482

commit v5 on v4

--- a/solution.py
+++ b/solution.py
@@ -406,8 +406,11 @@
     out_ref[...] = total.astype(BF16)
 
 
-def k_rows(place, near_ref, far_ref, vqkv_ref, vout_ref, tqkv_ref, tout_ref):
-    both = jnp.where(place[0] == place[1], near_ref[...].astype(F32), far_ref[...].astype(F32))
+def k_rows(place, own_ref, core_ref, view_ref, corner_ref, vqkv_ref, vout_ref, tqkv_ref, tout_ref):
+    same, first = place[0] == place[1], place[1] == 0
+    mine = jnp.where(same, own_ref[...].astype(F32), view_ref[...].astype(F32))
+    other = jnp.where(same, core_ref[...].astype(F32), corner_ref[...].astype(F32))
+    both = jnp.concatenate([jnp.where(first, mine, other), jnp.where(first, other, mine)], axis=0)
     rows = vout_ref.shape[0]
 
     def lines(unit):
@@ -536,12 +539,11 @@
         [((views, 2 * PX, D), BF16), ((views, 2 * PX, D), BF16), ((4, views, 128), F32)],
         st4, sums_two, own, level_in, u_keep, o_keep, recv_back, place=place, us=3,
     )
-    first = place[1] == 0
-    near = swap(summed, "core")
-    pair = jnp.concatenate([jnp.where(first, summed, near), jnp.where(first, near, summed)], axis=0)
     qkv_row, out_row = ((rows, 3 * D), BF16), ((rows, D), BF16)
+    corner = lax.ppermute(summed, ("view", "core"), [(i, 3 - i) for i in range(4)])
     view_qkv_grad, view_out_grad, time_qkv_grad, time_out_grad = call(
-        k_rows, [qkv_row, out_row, qkv_row, out_row], pair, swap(pair, "view"), place=place
+        k_rows, [qkv_row, out_row, qkv_row, out_row],
+        summed, swap(summed, "core"), swap(summed, "view"), corner, place=place,
     )
     return (
         level_out.reshape(level_in.shape),

time: 161 us -> 161 us (level)
  waiting for transfers between devices: 36.1 us -> 34.3 us
    ppermute x0 -> x1, starting transfers between devices: none -> 4.33 us  [body(): lax.ppermute(summed, ('view', 'core'), [(i, 3 - i) for i in range(4)])]
    ppermute x9, starting transfers between devices: 16.9 us -> 14.2 us  [swap(): return lax.ppermute(field, axis, [(0, 1), (1, 0)])]
    ppermute x9, waiting for transfers between devices: 6.64 us -> 4.83 us  [swap(): return lax.ppermute(field, axis, [(0, 1), (1, 0)])]
  transfers between devices with their start and end apart: 22 -> 23, of which waited for: 12 -> 11; matrix products, arithmetic and copies ran while one was open for 0% -> 0% of each run, Pallas kernels for 8% -> 8%
where the time goes in v5:
time: 161 us; the launch traced here: 160 us
  starting transfers between devices  52.7 us (33%)
  blocking collectives  38.7 us (24%)
  waiting for transfers between devices  34.3 us (21%)
  Pallas kernels  24.8 us (15%)
  local copies, waits for them, and re-layouts  8.31 us (5%)
    all_to_all x1, blocking collectives, transpose(): return lax.all_to_all(field, frame_axes, 0, 0, tiled=True)  26 us
    pallas_call x15, Pallas kernels, call(): pl.pallas_call(kernel, out_shape=[jax.ShapeDtypeStruct(shape, dtype) for...  24.8 us
    ppermute x9, starting transfers between devices, swap(): return lax.ppermute(field, axis, [(0, 1), (1, 0)])  14.2 us
    all_to_all x1, blocking collectives, share(): return lax.all_to_all(field, mates, 0, 0, tiled=True)  12.7 us
    all_to_all x2, waiting for transfers between devices, share(): return lax.all_to_all(field, mates, 0, 0, tiled=True)  10.3 us
    unnamed x72, local copies, waits for them, and re-layouts  8.31 us
    ppermute x6, waiting for transfers between devices, shifted(): lax.ppermute(piece, axis, [(i, (i + step + 1) % 4) for i in range(4)])  8.09 us
    ppermute x6, starting transfers between devices, shifted(): lax.ppermute(piece, axis, [(i, (i + step + 1) % 4) for i in range(4)])  7.9 us
  transfers between devices with their start and end apart: 23, of which 11 were waited for; matrix products, arithmetic and copies ran while one was open for 0% of the time, Pallas kernels for 8%

profile of v5, /device:TPU:1, one launch (start us, length us, event | category | flops | bytes accessed | tf_op | source)
XLA Modules:
  0.0 159.9 jit_solution(9964772740254404890)
XLA Ops:
  0.6 0.0 copy-start.9
  0.7 3.7 %collective-permute-start = (bf16[4,1,32,640]{3,2,1,0:T(8,128)(2,1)}, bf16[4,1,32,640]{3,2,1,0:T(8,128)(2,1)S(1)}, u32[]{:S(2)}, u32[]{:S(2)}) collective-permute-start(bf16[4,1,32,640]{3,2,1,0:T(8,128)(2,1)} %x_ref.7), channel_id=1, source_target_pairs={{0,128},{128,0},{1,129},{129,1},{2,130},{130,2},{3,131},{131,3},{4... | collective-permute-start | bytes 491528 | tf_op jit(solution)/shard_map/ppermute | solution.py:485
  4.3 0.9 copy-done.11
  5.3 1.3 shard_map.135
  6.6 4.2 %all-to-all-start = ((f32[8,16,128]{2,1,0:T(8,128)}), f32[8,16,128]{2,1,0:T(8,128)S(1)}, u32[]{:S(2)}, u32[]{:S(2)}) async-start(f32[8,16,128]{2,1,0:T(8,128)} %shard_map.135), calls=%async_computation | async-start | bytes 131072 | tf_op jit(solution)/shard_map/all_to_all | solution.py:479
  10.8 3.0 %collective-permute-start.1 = (bf16[4,1,32,640]{3,2,1,0:T(8,128)(2,1)S(1)}, bf16[4,1,32,640]{3,2,1,0:T(8,128)(2,1)S(1)}, u32[]{:S(2)}, u32[]{:S(2)}) collective-permute-start(bf16[4,1,32,640]{3,2,1,0:T(8,128)(2,1)S(1)} %copy-done.9), channel_id=1, source_target_pairs={{0,128},{128,0},{1,129},{129,1},{2,130},{130,2},{3,131},{131,3},{4... | collective-permute-start | bytes 491528 | tf_op jit(solution)/shard_map/ppermute | solution.py:485
  13.8 0.1 pad_add_fusion.place
  13.9 3.7 %all-to-all-done.g_ref = f32[8,16,128]{2,1,0:T(8,128)S(1)} async-done(((f32[8,16,128]{2,1,0:T(8,128)}), f32[8,16,128]{2,1,0:T(8,128)S(1)}, u32[]{:S(2)}, u32[]{:S(2)}) %all-to-all-start) | async-done | bytes 65568 | tf_op jit(solution)/shard_map/all_to_all | solution.py:479
  17.5 0.0 collective-permute-done.other_ref
  17.5 0.0 copy-start.1
  17.5 1.7 %copy-done.1 = bf16[640,1920]{1,0:T(8,128)(2,1)S(1)} copy-done((bf16[640,1920]{1,0:T(8,128)(2,1)S(1)}, bf16[640,1920]{1,0:T(8,128)(2,1)}, u32[]{:S(2)}) %copy-start.1) | copy-done | bytes 2457624
  19.2 3.4 %shard_map.136 = (f32[128,640]{1,0:T(8,128)S(1)}, bf16[128,1920]{1,0:T(8,128)(2,1)S(1)}, bf16[128,1280]{1,0:T(8,128)(2,1)S(1)}, f32[16,128]{1,0:T(8,128)S(1)}, f32[8,16,128]{2,1,0:T(8,128)}) custom-call(s32[3]{0:T(128)S(1)} %pad_add_fusion.place, bf16[4,1,32,640]{3,2,1,0:T(8,128)(2,1)S(1)} %copy-done.12, ...), custom_call_target="tpu_custom_call" | custom-call | flops 4000000000 | bytes 12000000 | tf_op jit(solution)/shard_map/pallas_call | solution.py:429
  22.6 3.3 %all-to-all-start.1 = ((f32[8,16,128]{2,1,0:T(8,128)}), f32[8,16,128]{2,1,0:T(8,128)S(1)}, u32[]{:S(2)}, u32[]{:S(2)}) async-start(f32[8,16,128]{2,1,0:T(8,128)} %get-tuple-element.67), calls=%async_computation.1 | async-start | bytes 131072 | tf_op jit(solution)/shard_map/all_to_all | solution.py:479
  25.9 0.0 collective-permute-done.1.other_ref.ogother_ref
  26.0 0.0 copy-start.16
  26.0 6.6 %all-to-all-done.1.g_ref = f32[8,16,128]{2,1,0:T(8,128)S(1)} async-done(((f32[8,16,128]{2,1,0:T(8,128)}), f32[8,16,128]{2,1,0:T(8,128)S(1)}, u32[]{:S(2)}, u32[]{:S(2)}) %all-to-all-start.1) | async-done | bytes 65568 | tf_op jit(solution)/shard_map/all_to_all | solution.py:479
  32.6 0.9 shard_map.137
  33.5 26.0 %all_to_all.42.recv_ref = bf16[32,4,1280]{2,1,0:T(4,128)(2,1)S(1)} all-to-all(bf16[32,4,1280]{2,1,0:T(4,128)(2,1)S(1)} %get-tuple-element.68), channel_id=1, replica_groups=mesh['view'=2,'z'=8,'xl'=2,'core'=2,'dp'=4] {'z','xl','core'}, dimensions={0} | all-to-all | bytes 655360 | tf_op jit(solution)/shard_map/all_to_all | solution.py:482
  59.5 4.2 %shard_map.138 = (bf16[32,4,1280]{2,1,0:T(4,128)(2,1)}, bf16[128,2560]{1,0:T(8,128)(2,1)S(1)}, bf16[128,2560]{1,0:T(8,128)(2,1)S(1)}) custom-call(s32[3]{0:T(128)S(1)} %pad_add_fusion.place, bf16[32,4,1280]{2,1,0:T(4,128)(2,1)S(1)} %all_to_all.42.recv_ref, bf16[640,1920]{1,0:T(8,128)(2,1)S(1)} %copy-done, bf16[640,640]{1,0:T(8,128)(2,1)S(1)} %copy-done.3), custom_call_target="tpu_custom_call" | custom-call | flops 6000000000 | bytes 18000000 | tf_op jit(solution)/shard_map/pallas_call | solution.py:429
  63.7 0.9 copy-done.32
  64.5 1.3 collective-permute-start.2
  65.8 3.7 %all-to-all-start.3 = ((bf16[32,4,1280]{2,1,0:T(4,128)(2,1)}), bf16[32,4,1280]{2,1,0:T(4,128)(2,1)S(1)}, u32[]{:S(2)}, u32[]{:S(2)}) async-start(bf16[32,4,1280]{2,1,0:T(4,128)(2,1)} %get-tuple-element.69), calls=%async_computation.3 | async-start | bytes 655360 | tf_op jit(solution)/shard_map/all_to_all | solution.py:482
  69.5 0.3 collective-permute-start.3
  69.8 1.1 copy-done.33
  70.9 2.8 %shard_map.139 = (bf16[160,1280]{1,0:T(8,128)(2,1)S(1)}, bf16[160,1280]{1,0:T(8,128)(2,1)}, bf16[160,1280]{1,0:T(8,128)(2,1)S(1)}, bf16[160,1280]{1,0:T(8,128)(2,1)S(1)}) custom-call(s32[3]{0:T(128)S(1)} %pad_add_fusion.place, s32[16,1,640]{2,1,0:T(1,128)S(1)} %copy-done.19, bf16[128,2560]{1,0:T(8,128)(2,1)S(1)} %copy-done.33, ...), custom_call_target="tpu_custom_call" | custom-call | flops 3000000000 | bytes 9000000 | tf_op jit(solution)/shard_map/pallas_call | solution.py:429
  73.7 0.8 copy-done.26
  74.5 0.3 collective-permute-start.4
  74.8 1.8 %collective-permute-start.5 = (bf16[160,1280]{1,0:T(8,128)(2,1)S(1)}, bf16[160,1280]{1,0:T(8,128)(2,1)S(1)}, u32[]{:S(2)}, u32[]{:S(2)}) collective-permute-start(bf16[160,1280]{1,0:T(8,128)(2,1)S(1)} %get-tuple-element.73), channel_id=1, source_target_pairs={{0,2},{1,3},{2,0},{3,1},{4,6},{5,7},{6,4},{7,5},{8,10},{9,11},{10,... | collective-permute-start | bytes 1228808 | tf_op jit(solution)/shard_map/ppermute | solution.py:489
  76.5 0.8 collective-permute-start.6
  77.4 0.0 collective-permute-done.3.theirs_ref
  77.4 1.3 shard_map.140.left_ref
  78.7 0.9 copy-done.20
  79.6 2.6 %all-to-all-done.3.back_ref = bf16[32,4,1280]{2,1,0:T(4,128)(2,1)S(1)} async-done(((bf16[32,4,1280]{2,1,0:T(4,128)(2,1)}), bf16[32,4,1280]{2,1,0:T(4,128)(2,1)S(1)}, u32[]{:S(2)}, u32[]{:S(2)}) %all-to-all-start.3) | async-done | bytes 327712 | tf_op jit(solution)/shard_map/all_to_all | solution.py:482
  82.1 1.0 copy-done.23
  83.1 0.6 shard_map.141
  83.7 12.7 %all_to_all.43.g_ref = f32[8,16,128]{2,1,0:T(8,128)S(1)} all-to-all(f32[8,16,128]{2,1,0:T(8,128)S(1)} %shard_map.141), channel_id=1, replica_groups=mesh['view'=2,'z'=8,'xl'=2,'core'=2,'dp'=4] {'view','dp'}, dimensions={0} | all-to-all | bytes 131072 | tf_op jit(solution)/shard_map/all_to_all | solution.py:479
  96.5 2.3 %shard_map.142 = (bf16[128,1280]{1,0:T(8,128)(2,1)S(1)}, bf16[128,1280]{1,0:T(8,128)(2,1)S(1)}, bf16[128,1920]{1,0:T(8,128)(2,1)S(1)}, f32[128,640]{1,0:T(8,128)S(1)}, f32[16,128]{1,0:T(8,128)S(1)}) custom-call(s32[3]{0:T(128)S(1)} %pad_add_fusion.place, bf16[32,4,1280]{2,1,0:T(4,128)(2,1)S(1)} %all-to-all-done.3.back_ref, f32[128,640]{1,0:T(8,128)S(1)} %copy-done.24, ...), custom_call_target="tpu_custom_call" | custom-call | flops 5000000000 | bytes 15000000 | tf_op jit(solution)/shard_map/pallas_call | solution.py:429
  98.8 1.3 collective-permute-start.7
  100.1 1.3 collective-permute-done.7.theirs_ref
  101.4 1.9 %shard_map.143 = bf16[640,1280]{1,0:T(8,128)(2,1)} custom-call(bf16[2,640,256]{2,1,0:T(8,128)(2,1)S(1)} %copy-done.21, bf16[128,1280]{1,0:T(8,128)(2,1)S(1)} %get-tuple-element.86.mine_ref, bf16[128,1280]{1,0:T(8,128)(2,1)S(1)} %collective-permute-done.7.theirs_ref), custom_call_target="tpu_custom_call" | custom-call | flops 1000000000 | bytes 3000000 | tf_op jit(solution)/shard_map/pallas_call | solution.py:429
  103.3 5.1 %all-to-all-start.5 = ((bf16[16,40,1280]{2,1,0:T(8,128)(2,1)}), bf16[16,40,1280]{2,1,0:T(8,128)(2,1)S(1)}, u32[]{:S(2)}, u32[]{:S(2)}) async-start(bf16[16,40,1280]{2,1,0:T(8,128)(2,1)} %bitcast.3), calls=%async_computation.5 | async-start | bytes 3276800 | tf_op jit(solution)/shard_map/all_to_all | solution.py:526
  108.4 1.0 copy-done.27
  109.4 0.2 shard_map.144
  109.7 1.4 collective-permute-start.8
  111.1 2.4 %collective-permute-start.9 = (bf16[40,1280]{1,0:T(8,128)(2,1)S(1)}, bf16[40,1280]{1,0:T(8,128)(2,1)S(1)}, u32[]{:S(2)}, u32[]{:S(2)}) collective-permute-start(bf16[40,1280]{1,0:T(8,128)(2,1)S(1)} %get-tuple-element.96), channel_id=1, source_target_pairs={{0,128},{8,136},{128,0},{136,8},{1,129},{9,137},{129,1},{137,9},{2... | collective-permute-start | bytes 307208 | tf_op jit(solution)/shard_map/ppermute | solution.py:489
  113.5 1.2 collective-permute-start.10
  114.7 1.7 %shard_map.145 = (f32[64,640]{1,0:T(8,128)S(1)}, bf16[64,640]{1,0:T(8,128)(2,1)S(1)}, bf16[64,1280]{1,0:T(8,128)(2,1)S(1)}, f32[16,128]{1,0:T(8,128)S(1)}) custom-call(s32[3]{0:T(128)S(1)} %pad_add_fusion.place, bf16[128,1920]{1,0:T(8,128)(2,1)S(1)} %copy-done.29, f32[128,640]{1,0:T(8,128)S(1)} %copy-done.31, ...), custom_call_target="tpu_custom_call" | custom-call | flops 3000000000 | bytes 9000000 | tf_op jit(solution)/shard_map/pallas_call | solution.py:429
  116.4 2.8 %collective-permute-start.11 = (f32[16,128]{1,0:T(8,128)S(1)}, f32[16,128]{1,0:T(8,128)S(1)}, u32[]{:S(2)}, u32[]{:S(2)}) collective-permute-start(f32[16,128]{1,0:T(8,128)S(1)} %get-tuple-element.101), channel_id=1, source_target_pairs={{0,2},{1,3},{2,0},{3,1},{4,6},{5,7},{6,4},{7,5},{8,10},{9,11},{10,... | collective-permute-start | bytes 24584 | tf_op jit(solution)/shard_map/ppermute | solution.py:493
  119.2 2.2 %collective-permute-done.11 = f32[16,128]{1,0:T(8,128)S(1)} collective-permute-done((f32[16,128]{1,0:T(8,128)S(1)}, f32[16,128]{1,0:T(8,128)S(1)}, u32[]{:S(2)}, u32[]{:S(2)}) %collective-permute-start.11) | collective-permute-done | bytes 8224 | tf_op jit(solution)/shard_map/ppermute | solution.py:493
  121.4 0.6 collective-permute-start.12
  122.0 3.4 %collective-permute-done.12 = f32[16,128]{1,0:T(8,128)S(1)} collective-permute-done((f32[16,128]{1,0:T(8,128)S(1)}, f32[16,128]{1,0:T(8,128)S(1)}, u32[]{:S(2)}, u32[]{:S(2)}) %collective-permute-start.12) | collective-permute-done | bytes 8224 | tf_op jit(solution)/shard_map/ppermute | solution.py:493
  125.4 4.9 %collective-permute-done.8.refs_1_ = bf16[40,1280]{1,0:T(8,128)(2,1)S(1)} collective-permute-done((bf16[40,1280]{1,0:T(8,128)(2,1)S(1)}, bf16[40,1280]{1,0:T(8,128)(2,1)S(1)}, u32[]{:S(2)}, u32[]{:S(2)}) %collective-permute-start.8) | collective-permute-done | bytes 102432 | tf_op jit(solution)/shard_map/ppermute | solution.py:489
  130.4 3.1 %collective-permute-done.9.refs_2_ = bf16[40,1280]{1,0:T(8,128)(2,1)S(1)} collective-permute-done((bf16[40,1280]{1,0:T(8,128)(2,1)S(1)}, bf16[40,1280]{1,0:T(8,128)(2,1)S(1)}, u32[]{:S(2)}, u32[]{:S(2)}) %collective-permute-start.9) | collective-permute-done | bytes 102432 | tf_op jit(solution)/shard_map/ppermute | solution.py:489
  133.5 1.3 shard_map.146
  134.8 6.5 %all-to-all-start.6 = ((bf16[8,4,3200]{2,1,0:T(4,128)(2,1)}), bf16[8,4,3200]{2,1,0:T(4,128)(2,1)S(1)}, u32[]{:S(2)}, u32[]{:S(2)}) async-start(bf16[8,4,3200]{2,1,0:T(4,128)(2,1)} %shard_map.146), calls=%async_computation.6 | async-start | bytes 409600 | tf_op jit(solution)/shard_map/all_to_all | solution.py:532
  141.3 1.5 collective-permute-start.14
  142.8 1.5 collective-permute-start.13
  144.3 2.8 %collective-permute-done.13 = f32[16,128]{1,0:T(8,128)S(1)} collective-permute-done((f32[16,128]{1,0:T(8,128)S(1)}, f32[16,128]{1,0:T(8,128)S(1)}, u32[]{:S(2)}, u32[]{:S(2)}) %collective-permute-start.13) | collective-permute-done | bytes 8224 | tf_op jit(solution)/shard_map/ppermute | solution.py:485
  147.1 3.0 %all-to-all-done.6.parts_ref = bf16[8,4,3200]{2,1,0:T(4,128)(2,1)S(1)} async-done(((bf16[8,4,3200]{2,1,0:T(4,128)(2,1)}), bf16[8,4,3200]{2,1,0:T(4,128)(2,1)S(1)}, u32[]{:S(2)}, u32[]{:S(2)}) %all-to-all-start.6) | async-done | bytes 204832 | tf_op jit(solution)/shard_map/all_to_all | solution.py:532
  150.1 4.3 %collective-permute-start.17 = (bf16[4,3200]{1,0:T(4,128)(2,1)S(1)}, bf16[4,3200]{1,0:T(4,128)(2,1)S(1)}, u32[]{:S(2)}, u32[]{:S(2)}) collective-permute-start(bf16[4,3200]{1,0:T(4,128)(2,1)S(1)} %shard_map.148.own_ref), channel_id=1, source_target_pairs={{0,132},{4,128},{128,4},{132,0},{1,133},{5,129},{129,5},{133,1},{2... | collective-permute-start | bytes 76808 | tf_op jit(solution)/shard_map/ppermute | solution.py:543
  154.4 1.8 %collective-permute-start.16 = (bf16[4,3200]{1,0:T(4,128)(2,1)S(1)}, bf16[4,3200]{1,0:T(4,128)(2,1)S(1)}, u32[]{:S(2)}, u32[]{:S(2)}) collective-permute-start(bf16[4,3200]{1,0:T(4,128)(2,1)S(1)} %shard_map.148.own_ref), channel_id=1, source_target_pairs={{0,128},{128,0},{1,129},{129,1},{2,130},{130,2},{3,131},{131,3},{4... | collective-permute-start | bytes 76808 | tf_op jit(solution)/shard_map/ppermute | solution.py:485
  156.3 1.6 %shard_map.147 = (bf16[4,32,640]{2,1,0:T(8,128)(2,1)}, bf16[4,32,640]{2,1,0:T(8,128)(2,1)}, f32[4,4,128]{2,1,0:T(4,128)}) custom-call(s32[3]{0:T(128)S(1)} %pad_add_fusion.place, f32[16,128]{1,0:T(8,128)S(1)} %add.19.g_ref, f32[16,128]{1,0:T(8,128)S(1)} %get-tuple-element.113.sumstwo_ref, f32[16,128]{1,0:T(8,128)S(1)} %get-tuple-element.100.own_ref, ...), custom_call_target="tpu_custom_call" | custom-call | flops 3000000000 | bytes 9000000 | tf_op jit(solution)/shard_map/pallas_call | solution.py:429
  157.9 0.8 collective-permute-done.16.view_ref
  158.6 1.2 shard_map.149
  (75 shorter events, 0.2 us)
Async XLA Ops:
  0.6 10.2 %copy-start.9 = (bf16[4,1,32,640]{3,2,1,0:T(8,128)(2,1)S(1)}, bf16[4,1,32,640]{3,2,1,0:T(8,128)(2,1)}, u32[]{:S(2)}) copy-start(bf16[4,1,32,640]{3,2,1,0:T(8,128)(2,1)} %og_ref.1) | copy-start | bytes 491524
  0.6 16.9 %copy-start.4 = (bf16[640,640]{1,0:T(8,128)(2,1)S(1)}, bf16[640,640]{1,0:T(8,128)(2,1)}, u32[]{:S(2)}) copy-start(bf16[640,640]{1,0:T(8,128)(2,1)} %wout_ref.5) | copy-start | bytes 2457604
  0.7 16.9 %collective-permute-start = (bf16[4,1,32,640]{3,2,1,0:T(8,128)(2,1)}, bf16[4,1,32,640]{3,2,1,0:T(8,128)(2,1)S(1)}, u32[]{:S(2)}, u32[]{:S(2)}) collective-permute-start(bf16[4,1,32,640]{3,2,1,0:T(8,128)(2,1)} %x_ref.7), channel_id=1, source_target_pairs={{0,128},{128,0},{1,129},{129,1},{2,130},{130,2},{3,131},{131,3},{4... | collective-permute-start | bytes 491528 | tf_op jit(solution)/shard_map/ppermute | solution.py:485
  4.3 0.9 copy-start.11
  5.3 12.3 %copy-start.12 = (bf16[4,1,32,640]{3,2,1,0:T(8,128)(2,1)S(1)}, bf16[4,1,32,640]{3,2,1,0:T(8,128)(2,1)}, u32[]{:S(2)}) copy-start(bf16[4,1,32,640]{3,2,1,0:T(8,128)(2,1)} %x_ref.7) | copy-start | bytes 491524
  6.6 10.9 %all-to-all-start = ((f32[8,16,128]{2,1,0:T(8,128)}), f32[8,16,128]{2,1,0:T(8,128)S(1)}, u32[]{:S(2)}, u32[]{:S(2)}) async-start(f32[8,16,128]{2,1,0:T(8,128)} %shard_map.135), calls=%async_computation | async-start | bytes 131072 | tf_op jit(solution)/shard_map/all_to_all | solution.py:479
  10.8 15.1 %collective-permute-start.1 = (bf16[4,1,32,640]{3,2,1,0:T(8,128)(2,1)S(1)}, bf16[4,1,32,640]{3,2,1,0:T(8,128)(2,1)S(1)}, u32[]{:S(2)}, u32[]{:S(2)}) collective-permute-start(bf16[4,1,32,640]{3,2,1,0:T(8,128)(2,1)S(1)} %copy-done.9), channel_id=1, source_target_pairs={{0,128},{128,0},{1,129},{129,1},{2,130},{130,2},{3,131},{131,3},{4... | collective-permute-start | bytes 491528 | tf_op jit(solution)/shard_map/ppermute | solution.py:485
  17.5 1.7 %copy-start.1 = (bf16[640,1920]{1,0:T(8,128)(2,1)S(1)}, bf16[640,1920]{1,0:T(8,128)(2,1)}, u32[]{:S(2)}) copy-start(bf16[640,1920]{1,0:T(8,128)(2,1)} %wqkv_ref.5) | copy-start | bytes 7372804
  19.2 3.4 %copy-start.14 = (bf16[4,1,32,640]{3,2,1,0:T(8,128)(2,1)}, bf16[4,1,32,640]{3,2,1,0:T(8,128)(2,1)S(1)}, u32[]{:S(2)}) copy-start(bf16[4,1,32,640]{3,2,1,0:T(8,128)(2,1)S(1)} %collective-permute-done.other_ref) | copy-start | bytes 491524
  22.6 10.9 %copy-start.22 = (f32[128,640]{1,0:T(8,128)}, f32[128,640]{1,0:T(8,128)S(1)}, u32[]{:S(2)}) copy-start(f32[128,640]{1,0:T(8,128)S(1)} %get-tuple-element.66.stream_ref) | copy-start | bytes 983044
  22.6 10.9 %copy-start.34 = (bf16[128,1920]{1,0:T(8,128)(2,1)}, bf16[128,1920]{1,0:T(8,128)(2,1)S(1)}, u32[]{:S(2)}) copy-start(bf16[128,1920]{1,0:T(8,128)(2,1)S(1)} %get-tuple-element.85.packed_ref) | copy-start | bytes 1474564
  22.6 10.0 %all-to-all-start.1 = ((f32[8,16,128]{2,1,0:T(8,128)}), f32[8,16,128]{2,1,0:T(8,128)S(1)}, u32[]{:S(2)}, u32[]{:S(2)}) async-start(f32[8,16,128]{2,1,0:T(8,128)} %get-tuple-element.67), calls=%async_computation.1 | async-start | bytes 131072 | tf_op jit(solution)/shard_map/all_to_all | solution.py:479
  26.0 7.5 %copy-start.16 = (bf16[4,1,32,640]{3,2,1,0:T(8,128)(2,1)}, bf16[4,1,32,640]{3,2,1,0:T(8,128)(2,1)S(1)}, u32[]{:S(2)}) copy-start(bf16[4,1,32,640]{3,2,1,0:T(8,128)(2,1)S(1)} %collective-permute-done.1.other_ref.ogother_ref) | copy-start | bytes 491524
  32.6 26.9 %copy-start = (bf16[640,1920]{1,0:T(8,128)(2,1)S(1)}, bf16[640,1920]{1,0:T(8,128)(2,1)}, u32[]{:S(2)}) copy-start(bf16[640,1920]{1,0:T(8,128)(2,1)} %wqkv_ref.4) | copy-start | bytes 7372804
  32.6 26.9 %copy-start.3 = (bf16[640,640]{1,0:T(8,128)(2,1)S(1)}, bf16[640,640]{1,0:T(8,128)(2,1)}, u32[]{:S(2)}) copy-start(bf16[640,640]{1,0:T(8,128)(2,1)} %wout_ref.4) | copy-start | bytes 2457604
  59.5 10.3 %copy-start.19 = (s32[16,1,640]{2,1,0:T(1,128)S(1)}, s32[16,1,640]{2,1,0:T(1,128)}, u32[]{:S(2)}) copy-start(s32[16,1,640]{2,1,0:T(1,128)} %constant.24.clone.table_ref) | copy-start | bytes 122884
  63.7 0.9 copy-start.32
  64.5 5.2 %collective-permute-start.2 = (bf16[128,2560]{1,0:T(8,128)(2,1)S(1)}, bf16[128,2560]{1,0:T(8,128)(2,1)S(1)}, u32[]{:S(2)}, u32[]{:S(2)}) collective-permute-start(bf16[128,2560]{1,0:T(8,128)(2,1)S(1)} %get-tuple-element.71), channel_id=1, source_target_pairs={{0,4},{4,0},{1,5},{5,1},{2,6},{6,2},{3,7},{7,3},{8,12},{12,8},{9,1... | collective-permute-start | bytes 1966088 | tf_op jit(solution)/shard_map/ppermute | solution.py:485
  65.8 16.3 %all-to-all-start.3 = ((bf16[32,4,1280]{2,1,0:T(4,128)(2,1)}), bf16[32,4,1280]{2,1,0:T(4,128)(2,1)S(1)}, u32[]{:S(2)}, u32[]{:S(2)}) async-start(bf16[32,4,1280]{2,1,0:T(4,128)(2,1)} %get-tuple-element.69), calls=%async_computation.3 | async-start | bytes 655360 | tf_op jit(solution)/shard_map/all_to_all | solution.py:482
  69.5 7.9 %collective-permute-start.3 = (bf16[128,1280]{1,0:T(8,128)(2,1)S(1)}, bf16[128,1280]{1,0:T(8,128)(2,1)S(1)}, u32[]{:S(2)}, u32[]{:S(2)}) collective-permute-start(bf16[128,1280]{1,0:T(8,128)(2,1)S(1)} %get-tuple-element.75.mine_ref), channel_id=1, source_target_pairs={{0,4},{4,0},{1,5},{5,1},{2,6},{6,2},{3,7},{7,3},{8,12},{12,8},{9,1... | collective-permute-start | bytes 983048 | tf_op jit(solution)/shard_map/ppermute | solution.py:485
  69.8 1.1 copy-start.33
  70.9 6.5 %copy-start.18 = (s32[640,1]{1,0:T(8,128)S(1)}, s32[640,1]{1,0:T(8,128)}, u32[]{:S(2)}) copy-start(s32[640,1]{1,0:T(8,128)} %constant.25.clone.column_ref) | copy-start | bytes 7684
  73.7 0.8 copy-start.26
  74.5 21.9 %collective-permute-start.4 = (bf16[160,1280]{1,0:T(8,128)(2,1)}, bf16[160,1280]{1,0:T(8,128)(2,1)S(1)}, u32[]{:S(2)}, u32[]{:S(2)}) collective-permute-start(bf16[160,1280]{1,0:T(8,128)(2,1)} %get-tuple-element.72), channel_id=1, source_target_pairs={{0,1},{1,2},{2,3},{3,0},{4,5},{5,6},{6,7},{7,4},{8,9},{9,10},{10,1... | collective-permute-start | bytes 1228808 | tf_op jit(solution)/shard_map/ppermute | solution.py:489
  74.8 21.7 %collective-permute-start.5 = (bf16[160,1280]{1,0:T(8,128)(2,1)S(1)}, bf16[160,1280]{1,0:T(8,128)(2,1)S(1)}, u32[]{:S(2)}, u32[]{:S(2)}) collective-permute-start(bf16[160,1280]{1,0:T(8,128)(2,1)S(1)} %get-tuple-element.73), channel_id=1, source_target_pairs={{0,2},{1,3},{2,0},{3,1},{4,6},{5,7},{6,4},{7,5},{8,10},{9,11},{10,... | collective-permute-start | bytes 1228808 | tf_op jit(solution)/shard_map/ppermute | solution.py:489
  76.5 19.9 %collective-permute-start.6 = (bf16[160,1280]{1,0:T(8,128)(2,1)S(1)}, bf16[160,1280]{1,0:T(8,128)(2,1)S(1)}, u32[]{:S(2)}, u32[]{:S(2)}) collective-permute-start(bf16[160,1280]{1,0:T(8,128)(2,1)S(1)} %get-tuple-element.74), channel_id=1, source_target_pairs={{0,3},{1,0},{2,1},{3,2},{4,7},{5,4},{6,5},{7,6},{8,11},{9,8},{10,9... | collective-permute-start | bytes 1228808 | tf_op jit(solution)/shard_map/ppermute | solution.py:489
  78.7 0.9 copy-start.20
  79.6 16.9 %copy-start.10 = (bf16[4,1,32,640]{3,2,1,0:T(8,128)(2,1)S(1)}, bf16[4,1,32,640]{3,2,1,0:T(8,128)(2,1)}, u32[]{:S(2)}) copy-start(bf16[4,1,32,640]{3,2,1,0:T(8,128)(2,1)} %og_ref.1) | copy-start | bytes 491524
  79.6 16.9 %copy-start.17 = (bf16[4,1,32,640]{3,2,1,0:T(8,128)(2,1)S(1)}, bf16[4,1,32,640]{3,2,1,0:T(8,128)(2,1)}, u32[]{:S(2)}) copy-start(bf16[4,1,32,640]{3,2,1,0:T(8,128)(2,1)} %copy-done.16) | copy-start | bytes 491524
  82.1 1.0 copy-start.23
  83.1 13.4 %copy-start.24 = (f32[128,640]{1,0:T(8,128)S(1)}, f32[128,640]{1,0:T(8,128)}, u32[]{:S(2)}) copy-start(f32[128,640]{1,0:T(8,128)} %copy-done.22) | copy-start | bytes 983044
  83.1 13.4 %copy-start.35 = (bf16[128,1920]{1,0:T(8,128)(2,1)S(1)}, bf16[128,1920]{1,0:T(8,128)(2,1)}, u32[]{:S(2)}) copy-start(bf16[128,1920]{1,0:T(8,128)(2,1)} %copy-done.34) | copy-start | bytes 1474564
  96.4 2.4 %copy-start.5 = (bf16[160,1280]{1,0:T(8,128)(2,1)}, bf16[160,1280]{1,0:T(8,128)(2,1)S(1)}, u32[]{:S(2)}) copy-start(bf16[160,1280]{1,0:T(8,128)(2,1)S(1)} %collective-permute-done.5.refs_2_) | copy-start | bytes 1228804
  96.4 2.4 %copy-start.7 = (bf16[160,1280]{1,0:T(8,128)(2,1)}, bf16[160,1280]{1,0:T(8,128)(2,1)S(1)}, u32[]{:S(2)}) copy-start(bf16[160,1280]{1,0:T(8,128)(2,1)S(1)} %collective-permute-done.6.refs_3_) | copy-start | bytes 1228804
  96.5 4.9 %copy-start.21 = (bf16[2,640,256]{2,1,0:T(8,128)(2,1)S(1)}, bf16[2,640,256]{2,1,0:T(8,128)(2,1)}, u32[]{:S(2)}) copy-start(bf16[2,640,256]{2,1,0:T(8,128)(2,1)} %copy-done.20) | copy-start | bytes 1966084
  98.8 4.4 %copy-start.28 = (bf16[128,1920]{1,0:T(8,128)(2,1)}, bf16[128,1920]{1,0:T(8,128)(2,1)S(1)}, u32[]{:S(2)}) copy-start(bf16[128,1920]{1,0:T(8,128)(2,1)S(1)} %get-tuple-element.98.pgrad_ref) | copy-start | bytes 1474564
  98.8 4.4 %copy-start.30 = (f32[128,640]{1,0:T(8,128)}, f32[128,640]{1,0:T(8,128)S(1)}, u32[]{:S(2)}) copy-start(f32[128,640]{1,0:T(8,128)S(1)} %get-tuple-element.99.stream_grad_ref) | copy-start | bytes 983044
  98.8 2.5 %collective-permute-start.7 = (bf16[128,1280]{1,0:T(8,128)(2,1)S(1)}, bf16[128,1280]{1,0:T(8,128)(2,1)S(1)}, u32[]{:S(2)}, u32[]{:S(2)}) collective-permute-start(bf16[128,1280]{1,0:T(8,128)(2,1)S(1)} %get-tuple-element.87), channel_id=1, source_target_pairs={{0,4},{4,0},{1,5},{5,1},{2,6},{6,2},{3,7},{7,3},{8,12},{12,8},{9,1... | collective-permute-start | bytes 983048 | tf_op jit(solution)/shard_map/ppermute | solution.py:485
  103.3 5.1 %copy-start.6 = (bf16[160,1280]{1,0:T(8,128)(2,1)S(1)}, bf16[160,1280]{1,0:T(8,128)(2,1)}, u32[]{:S(2)}) copy-start(bf16[160,1280]{1,0:T(8,128)(2,1)} %copy-done.5) | copy-start | bytes 1228804
  103.3 5.1 %copy-start.8 = (bf16[160,1280]{1,0:T(8,128)(2,1)S(1)}, bf16[160,1280]{1,0:T(8,128)(2,1)}, u32[]{:S(2)}) copy-start(bf16[160,1280]{1,0:T(8,128)(2,1)} %copy-done.7) | copy-start | bytes 1228804
  103.3 30.2 %all-to-all-start.5 = ((bf16[16,40,1280]{2,1,0:T(8,128)(2,1)}), bf16[16,40,1280]{2,1,0:T(8,128)(2,1)S(1)}, u32[]{:S(2)}, u32[]{:S(2)}) async-start(bf16[16,40,1280]{2,1,0:T(8,128)(2,1)} %bitcast.3), calls=%async_computation.5 | async-start | bytes 3276800 | tf_op jit(solution)/shard_map/all_to_all | solution.py:526
  108.4 1.0 copy-start.27
  109.4 5.3 %copy-start.2 = (bf16[640,1920]{1,0:T(8,128)(2,1)S(1)}, bf16[640,1920]{1,0:T(8,128)(2,1)}, u32[]{:S(2)}) copy-start(bf16[640,1920]{1,0:T(8,128)(2,1)} %wqkv_ref.5) | copy-start | bytes 7372804
  109.4 5.3 %copy-start.13 = (bf16[4,1,32,640]{3,2,1,0:T(8,128)(2,1)S(1)}, bf16[4,1,32,640]{3,2,1,0:T(8,128)(2,1)}, u32[]{:S(2)}) copy-start(bf16[4,1,32,640]{3,2,1,0:T(8,128)(2,1)} %x_ref.7) | copy-start | bytes 491524
  109.4 5.3 %copy-start.15 = (bf16[4,1,32,640]{3,2,1,0:T(8,128)(2,1)S(1)}, bf16[4,1,32,640]{3,2,1,0:T(8,128)(2,1)}, u32[]{:S(2)}) copy-start(bf16[4,1,32,640]{3,2,1,0:T(8,128)(2,1)} %copy-done.14) | copy-start | bytes 491524
  109.4 5.3 %copy-start.25 = (f32[128,640]{1,0:T(8,128)S(1)}, f32[128,640]{1,0:T(8,128)}, u32[]{:S(2)}) copy-start(f32[128,640]{1,0:T(8,128)} %copy-done.22) | copy-start | bytes 983044
  109.4 5.3 %copy-start.29 = (bf16[128,1920]{1,0:T(8,128)(2,1)S(1)}, bf16[128,1920]{1,0:T(8,128)(2,1)}, u32[]{:S(2)}) copy-start(bf16[128,1920]{1,0:T(8,128)(2,1)} %copy-done.28) | copy-start | bytes 1474564
  109.4 5.3 %copy-start.31 = (f32[128,640]{1,0:T(8,128)S(1)}, f32[128,640]{1,0:T(8,128)}, u32[]{:S(2)}) copy-start(f32[128,640]{1,0:T(8,128)} %copy-done.30) | copy-start | bytes 983044
  109.7 20.7 %collective-permute-start.8 = (bf16[40,1280]{1,0:T(8,128)(2,1)S(1)}, bf16[40,1280]{1,0:T(8,128)(2,1)S(1)}, u32[]{:S(2)}, u32[]{:S(2)}) collective-permute-start(bf16[40,1280]{1,0:T(8,128)(2,1)S(1)} %get-tuple-element.95), channel_id=1, source_target_pairs={{0,8},{8,128},{128,136},{136,0},{1,9},{9,129},{129,137},{137,1},{2... | collective-permute-start | bytes 307208 | tf_op jit(solution)/shard_map/ppermute | solution.py:489
  111.1 22.4 %collective-permute-start.9 = (bf16[40,1280]{1,0:T(8,128)(2,1)S(1)}, bf16[40,1280]{1,0:T(8,128)(2,1)S(1)}, u32[]{:S(2)}, u32[]{:S(2)}) collective-permute-start(bf16[40,1280]{1,0:T(8,128)(2,1)S(1)} %get-tuple-element.96), channel_id=1, source_target_pairs={{0,128},{8,136},{128,0},{136,8},{1,129},{9,137},{129,1},{137,9},{2... | collective-permute-start | bytes 307208 | tf_op jit(solution)/shard_map/ppermute | solution.py:489
  113.5 20.0 %collective-permute-start.10 = (bf16[40,1280]{1,0:T(8,128)(2,1)S(1)}, bf16[40,1280]{1,0:T(8,128)(2,1)S(1)}, u32[]{:S(2)}, u32[]{:S(2)}) collective-permute-start(bf16[40,1280]{1,0:T(8,128)(2,1)S(1)} %get-tuple-element.97), channel_id=1, source_target_pairs={{0,136},{8,0},{128,8},{136,128},{1,137},{9,1},{129,9},{137,129},{2... | collective-permute-start | bytes 307208 | tf_op jit(solution)/shard_map/ppermute | solution.py:489
  116.4 4.9 %collective-permute-start.11 = (f32[16,128]{1,0:T(8,128)S(1)}, f32[16,128]{1,0:T(8,128)S(1)}, u32[]{:S(2)}, u32[]{:S(2)}) collective-permute-start(f32[16,128]{1,0:T(8,128)S(1)} %get-tuple-element.101), channel_id=1, source_target_pairs={{0,2},{1,3},{2,0},{3,1},{4,6},{5,7},{6,4},{7,5},{8,10},{9,11},{10,... | collective-permute-start | bytes 24584 | tf_op jit(solution)/shard_map/ppermute | solution.py:493
  121.4 4.0 %collective-permute-start.12 = (f32[16,128]{1,0:T(8,128)S(1)}, f32[16,128]{1,0:T(8,128)S(1)}, u32[]{:S(2)}, u32[]{:S(2)}) collective-permute-start(f32[16,128]{1,0:T(8,128)S(1)} %add.17), channel_id=1, source_target_pairs={{0,1},{1,0},{2,3},{3,2},{4,5},{5,4},{6,7},{7,6},{8,9},{9,8},{10,11... | collective-permute-start | bytes 24584 | tf_op jit(solution)/shard_map/ppermute | solution.py:493
  134.8 15.3 %all-to-all-start.6 = ((bf16[8,4,3200]{2,1,0:T(4,128)(2,1)}), bf16[8,4,3200]{2,1,0:T(4,128)(2,1)S(1)}, u32[]{:S(2)}, u32[]{:S(2)}) async-start(bf16[8,4,3200]{2,1,0:T(4,128)(2,1)} %shard_map.146), calls=%async_computation.6 | async-start | bytes 409600 | tf_op jit(solution)/shard_map/all_to_all | solution.py:532
  141.3 5.8 %collective-permute-start.14 = (bf16[64,1280]{1,0:T(8,128)(2,1)S(1)}, bf16[64,1280]{1,0:T(8,128)(2,1)S(1)}, u32[]{:S(2)}, u32[]{:S(2)}) collective-permute-start(bf16[64,1280]{1,0:T(8,128)(2,1)S(1)} %get-tuple-element.111), channel_id=1, source_target_pairs={{0,128},{128,0},{1,129},{129,1},{2,130},{130,2},{3,131},{131,3},{4... | collective-permute-start | bytes 491528 | tf_op jit(solution)/shard_map/ppermute | solution.py:485
  142.8 4.3 %collective-permute-start.13 = (f32[16,128]{1,0:T(8,128)S(1)}, f32[16,128]{1,0:T(8,128)S(1)}, u32[]{:S(2)}, u32[]{:S(2)}) collective-permute-start(f32[16,128]{1,0:T(8,128)S(1)} %add.18), channel_id=1, source_target_pairs={{0,128},{128,0},{1,129},{129,1},{2,130},{130,2},{3,131},{131,3},{4... | collective-permute-start | bytes 24584 | tf_op jit(solution)/shard_map/ppermute | solution.py:485
  150.1 7.8 %collective-permute-start.17 = (bf16[4,3200]{1,0:T(4,128)(2,1)S(1)}, bf16[4,3200]{1,0:T(4,128)(2,1)S(1)}, u32[]{:S(2)}, u32[]{:S(2)}) collective-permute-start(bf16[4,3200]{1,0:T(4,128)(2,1)S(1)} %shard_map.148.own_ref), channel_id=1, source_target_pairs={{0,132},{4,128},{128,4},{132,0},{1,133},{5,129},{129,5},{133,1},{2... | collective-permute-start | bytes 76808 | tf_op jit(solution)/shard_map/ppermute | solution.py:543
  154.4 4.2 %collective-permute-start.16 = (bf16[4,3200]{1,0:T(4,128)(2,1)S(1)}, bf16[4,3200]{1,0:T(4,128)(2,1)S(1)}, u32[]{:S(2)}, u32[]{:S(2)}) collective-permute-start(bf16[4,3200]{1,0:T(4,128)(2,1)S(1)} %shard_map.148.own_ref), channel_id=1, source_target_pairs={{0,128},{128,0},{1,129},{129,1},{2,130},{130,2},{3,131},{131,3},{4... | collective-permute-start | bytes 76808 | tf_op jit(solution)/shard_map/ppermute | solution.py:485
  156.2 2.4 %collective-permute-start.15 = (bf16[4,3200]{1,0:T(4,128)(2,1)S(1)}, bf16[4,3200]{1,0:T(4,128)(2,1)S(1)}, u32[]{:S(2)}, u32[]{:S(2)}) collective-permute-start(bf16[4,3200]{1,0:T(4,128)(2,1)S(1)} %shard_map.148.own_ref), channel_id=1, source_target_pairs={{0,4},{4,0},{1,5},{5,1},{2,6},{6,2},{3,7},{7,3},{8,12},{12,8},{9,1... | collective-permute-start | bytes 76808 | tf_op jit(solution)/shard_map/ppermute | solution.py:485

commit v6 on v5

--- a/solution.py
+++ b/solution.py
@@ -172,7 +172,7 @@
     return jnp.concatenate([jnp.where(first, mine, theirs), jnp.where(first, theirs, mine)], axis=0)
 
 
-def k_first_stats(x_ref, stats_ref):
+def k_first_stats(place, x_ref, stats_ref):
     low, high = x_ref[:, 0, 0:PX, :].reshape(HALF, D), x_ref[:, 0, PX : 2 * PX, :].reshape(HALF, D)
     tokens = jnp.concatenate([low, high], axis=0).astype(F32)
     spread_out(stats_ref, partial_stats(tokens, group_matrix()))
@@ -494,14 +494,16 @@
 
     views = VIEWS // 2
     rows16 = ((2 * VIEWS, 128), F32)
-    x_other, og_other = swap(level_in, "view"), swap(out_grad, "view")
-    (st1,) = call(k_first_stats, [stats], level_in)
+    x_other = swap(level_in, "view")
+    (st1,) = call(k_first_stats, [stats], level_in, place=place)
     stream, packed_one, sides, own, st2 = call(
         functools.partial(k_view, entries), [tok32, ((T, 3 * D), BF16), ((T, 2 * D), BF16), rows16, stats],
         level_in, x_other, share(st1), view_qkv, view_out, place=place, us=4,
     )
     column = jnp.asarray(view_rows(z, xl, core, dp))
     (left,) = call(k_left_sides, [((2, D, 2 * T), BF16)], column, sides, swap(sides, "core"), place=place)
+    late_grad, st2 = lax.optimization_barrier((out_grad, st2))
+    og_other = swap(late_grad, "view")
     out_field, rows_two = call(
         functools.partial(k_norm_two, entries), [moved, rows16], stream, out_grad, og_other, share(st2), place=place
     )

time: 161 us -> 161 us (level)
  blocking collectives: 38.7 us -> 61 us
  waiting for transfers between devices: 34.3 us -> 23.8 us
  starting transfers between devices: 52.7 us -> 42.6 us
    all_to_all x1 -> x3, blocking collectives: 12.7 us -> 34.7 us  [share(): return lax.all_to_all(field, mates, 0, 0, tiled=True)]
    all_to_all x2 -> x0, waiting for transfers between devices: 10.3 us -> none  [share(): return lax.all_to_all(field, mates, 0, 0, tiled=True)]
    all_to_all x2 -> x0, starting transfers between devices: 7.54 us -> none  [share(): return lax.all_to_all(field, mates, 0, 0, tiled=True)]
    ppermute x9, starting transfers between devices: 14.2 us -> 11.9 us  [swap(): return lax.ppermute(field, axis, [(0, 1), (1, 0)])]
    unnamed x72 -> x60, local copies, waits for them, and re-layouts: 8.31 us -> 7.22 us
  transfers between devices with their start and end apart: 23 -> 21, of which waited for: 11 -> 9; matrix products, arithmetic and copies ran while one was open for 0% -> 0% of each run, Pallas kernels for 8% -> 6%
where the time goes in v6:
time: 161 us; the launch traced here: 160 us
  blocking collectives  61 us (38%)
  starting transfers between devices  42.6 us (26%)
  Pallas kernels  24.3 us (15%)
  waiting for transfers between devices  23.8 us (15%)
  local copies, waits for them, and re-layouts  7.22 us (4%)
    all_to_all x3, blocking collectives, share(): return lax.all_to_all(field, mates, 0, 0, tiled=True)  34.7 us
    all_to_all x1, blocking collectives, transpose(): return lax.all_to_all(field, frame_axes, 0, 0, tiled=True)  26.3 us
    pallas_call x15, Pallas kernels, call(): pl.pallas_call(kernel, out_shape=[jax.ShapeDtypeStruct(shape, dtype) for...  24.3 us
    ppermute x9, starting transfers between devices, swap(): return lax.ppermute(field, axis, [(0, 1), (1, 0)])  11.9 us
    ppermute x6, waiting for transfers between devices, shifted(): lax.ppermute(piece, axis, [(i, (i + step + 1) % 4) for i in range(4)])  8.1 us
    ppermute x6, starting transfers between devices, shifted(): lax.ppermute(piece, axis, [(i, (i + step + 1) % 4) for i in range(4)])  7.89 us
    unnamed x60, local copies, waits for them, and re-layouts  7.22 us
    all_to_all x1, starting transfers between devices, body(): by_z = lax.all_to_all(by_z, 'z', 0, 0, tiled=True)  6.47 us
  transfers between devices with their start and end apart: 21, of which 9 were waited for; matrix products, arithmetic and copies ran while one was open for 0% of the time, Pallas kernels for 6%

profile of v6, /device:TPU:1, one launch (start us, length us, event | category | flops | bytes accessed | tf_op | source)
XLA Modules:
  0.0 160.0 jit_solution(12237092860176799302)
XLA Ops:
  0.6 3.7 %collective-permute-start = (bf16[4,1,32,640]{3,2,1,0:T(8,128)(2,1)}, bf16[4,1,32,640]{3,2,1,0:T(8,128)(2,1)S(1)}, u32[]{:S(2)}, u32[]{:S(2)}) collective-permute-start(bf16[4,1,32,640]{3,2,1,0:T(8,128)(2,1)} %x_ref.7), channel_id=1, source_target_pairs={{0,128},{128,0},{1,129},{129,1},{2,130},{130,2},{3,131},{131,3},{4... | collective-permute-start | bytes 491528 | tf_op jit(solution)/shard_map/ppermute | solution.py:485
  4.3 0.1 pad_add_fusion.place
  4.4 0.9 copy-done.6
  5.3 1.3 shard_map.135
  6.5 10.7 %all_to_all.42.g_ref = f32[8,16,128]{2,1,0:T(8,128)S(1)} all-to-all(f32[8,16,128]{2,1,0:T(8,128)S(1)} %shard_map.135), channel_id=1, replica_groups=mesh['view'=2,'z'=8,'xl'=2,'core'=2,'dp'=4] {'view','dp'}, dimensions={0} | all-to-all | bytes 131072 | tf_op jit(solution)/shard_map/all_to_all | solution.py:479
  17.3 0.0 copy-start.9
  17.3 2.7 %shard_map.136 = (f32[128,640]{1,0:T(8,128)S(1)}, bf16[128,1920]{1,0:T(8,128)(2,1)S(1)}, bf16[128,1280]{1,0:T(8,128)(2,1)S(1)}, f32[16,128]{1,0:T(8,128)S(1)}, f32[8,16,128]{2,1,0:T(8,128)S(1)}) custom-call(s32[3]{0:T(128)S(1)} %pad_add_fusion.place, bf16[4,1,32,640]{3,2,1,0:T(8,128)(2,1)S(1)} %copy-done.7, ...), custom_call_target="tpu_custom_call" | custom-call | flops 4000000000 | bytes 12000000 | tf_op jit(solution)/shard_map/pallas_call | solution.py:429
  20.1 0.5 collective-permute-start.1
  20.5 11.0 %all_to_all.43.g_ref = f32[8,16,128]{2,1,0:T(8,128)S(1)} all-to-all(f32[8,16,128]{2,1,0:T(8,128)S(1)} %get-tuple-element.71), channel_id=1, replica_groups=mesh['view'=2,'z'=8,'xl'=2,'core'=2,'dp'=4] {'view','dp'}, dimensions={0} | all-to-all | bytes 131072 | tf_op jit(solution)/shard_map/all_to_all | solution.py:479
  31.5 0.0 collective-permute-done.1.other_ref.ogother_ref
  31.5 0.9 shard_map.137
  32.4 26.3 %all_to_all.44.recv_ref = bf16[32,4,1280]{2,1,0:T(4,128)(2,1)S(1)} all-to-all(bf16[32,4,1280]{2,1,0:T(4,128)(2,1)S(1)} %get-tuple-element.72), channel_id=1, replica_groups=mesh['view'=2,'z'=8,'xl'=2,'core'=2,'dp'=4] {'z','xl','core'}, dimensions={0} | all-to-all | bytes 655360 | tf_op jit(solution)/shard_map/all_to_all | solution.py:482
  58.7 4.2 %shard_map.138 = (bf16[32,4,1280]{2,1,0:T(4,128)(2,1)}, bf16[128,2560]{1,0:T(8,128)(2,1)S(1)}, bf16[128,2560]{1,0:T(8,128)(2,1)S(1)}) custom-call(s32[3]{0:T(128)S(1)} %pad_add_fusion.place, bf16[32,4,1280]{2,1,0:T(4,128)(2,1)S(1)} %all_to_all.44.recv_ref, bf16[640,1920]{1,0:T(8,128)(2,1)S(1)} %copy-done, bf16[640,640]{1,0:T(8,128)(2,1)S(1)} %copy-done.3), custom_call_target="tpu_custom_call" | custom-call | flops 6000000000 | bytes 18000000 | tf_op jit(solution)/shard_map/pallas_call | solution.py:429
  62.9 0.8 copy-done.26
  63.8 1.3 collective-permute-start.2
  65.1 3.7 %all-to-all-start.3 = ((bf16[32,4,1280]{2,1,0:T(4,128)(2,1)}), bf16[32,4,1280]{2,1,0:T(4,128)(2,1)S(1)}, u32[]{:S(2)}, u32[]{:S(2)}) async-start(bf16[32,4,1280]{2,1,0:T(4,128)(2,1)} %get-tuple-element.73), calls=%async_computation.3 | async-start | bytes 655360 | tf_op jit(solution)/shard_map/all_to_all | solution.py:482
  68.7 0.3 collective-permute-start.3
  69.0 1.1 copy-done.27
  70.1 3.1 %shard_map.139 = (bf16[160,1280]{1,0:T(8,128)(2,1)S(1)}, bf16[160,1280]{1,0:T(8,128)(2,1)}, bf16[160,1280]{1,0:T(8,128)(2,1)}, bf16[160,1280]{1,0:T(8,128)(2,1)}) custom-call(s32[3]{0:T(128)S(1)} %pad_add_fusion.place, s32[16,1,640]{2,1,0:T(1,128)S(1)} %copy-done.14, bf16[128,2560]{1,0:T(8,128)(2,1)S(1)} %copy-done.27, ...), custom_call_target="tpu_custom_call" | custom-call | flops 3000000000 | bytes 9000000 | tf_op jit(solution)/shard_map/pallas_call | solution.py:429
  73.3 0.7 copy-done.20
  74.0 0.3 collective-permute-start.4
  74.3 1.8 %collective-permute-start.5 = (bf16[160,1280]{1,0:T(8,128)(2,1)}, bf16[160,1280]{1,0:T(8,128)(2,1)S(1)}, u32[]{:S(2)}, u32[]{:S(2)}) collective-permute-start(bf16[160,1280]{1,0:T(8,128)(2,1)} %get-tuple-element.77), channel_id=1, source_target_pairs={{0,2},{1,3},{2,0},{3,1},{4,6},{5,7},{6,4},{7,5},{8,10},{9,11},{10,... | collective-permute-start | bytes 1228808 | tf_op jit(solution)/shard_map/ppermute | solution.py:489
  76.1 0.8 collective-permute-start.6
  76.9 1.3 shard_map.140.left_ref
  78.2 0.8 copy-done.15
  79.1 2.3 %all-to-all-done.3.back_ref = bf16[32,4,1280]{2,1,0:T(4,128)(2,1)S(1)} async-done(((bf16[32,4,1280]{2,1,0:T(4,128)(2,1)}), bf16[32,4,1280]{2,1,0:T(4,128)(2,1)S(1)}, u32[]{:S(2)}, u32[]{:S(2)}) %all-to-all-start.3) | async-done | bytes 327712 | tf_op jit(solution)/shard_map/all_to_all | solution.py:482
  81.4 1.0 copy-done.18
  82.3 0.6 shard_map.141
  82.9 13.0 %all_to_all.45.g_ref = f32[8,16,128]{2,1,0:T(8,128)S(1)} all-to-all(f32[8,16,128]{2,1,0:T(8,128)S(1)} %shard_map.141), channel_id=1, replica_groups=mesh['view'=2,'z'=8,'xl'=2,'core'=2,'dp'=4] {'view','dp'}, dimensions={0} | all-to-all | bytes 131072 | tf_op jit(solution)/shard_map/all_to_all | solution.py:479
  96.0 0.0 collective-permute-done.4.refs_1_
  96.0 0.0 collective-permute-done.5.refs_2_
  96.0 2.3 %shard_map.142 = (bf16[128,1280]{1,0:T(8,128)(2,1)S(1)}, bf16[128,1280]{1,0:T(8,128)(2,1)S(1)}, bf16[128,1920]{1,0:T(8,128)(2,1)S(1)}, f32[128,640]{1,0:T(8,128)S(1)}, f32[16,128]{1,0:T(8,128)S(1)}) custom-call(s32[3]{0:T(128)S(1)} %pad_add_fusion.place, bf16[32,4,1280]{2,1,0:T(4,128)(2,1)S(1)} %all-to-all-done.3.back_ref, f32[128,640]{1,0:T(8,128)S(1)} %copy-done.18, ...), custom_call_target="tpu_custom_call" | custom-call | flops 5000000000 | bytes 15000000 | tf_op jit(solution)/shard_map/pallas_call | solution.py:429
  98.3 0.7 copy-done.24
  99.0 1.4 collective-permute-start.7
  100.4 1.3 collective-permute-done.7.theirs_ref
  101.7 1.9 %shard_map.143 = bf16[640,1280]{1,0:T(8,128)(2,1)} custom-call(bf16[2,640,256]{2,1,0:T(8,128)(2,1)S(1)} %copy-done.16, bf16[128,1280]{1,0:T(8,128)(2,1)S(1)} %get-tuple-element.90.mine_ref, bf16[128,1280]{1,0:T(8,128)(2,1)S(1)} %collective-permute-done.7.theirs_ref), custom_call_target="tpu_custom_call" | custom-call | flops 1000000000 | bytes 3000000 | tf_op jit(solution)/shard_map/pallas_call | solution.py:429
  103.5 5.0 %all-to-all-start.5 = ((bf16[16,40,1280]{2,1,0:T(8,128)(2,1)}), bf16[16,40,1280]{2,1,0:T(8,128)(2,1)S(1)}, u32[]{:S(2)}, u32[]{:S(2)}) async-start(bf16[16,40,1280]{2,1,0:T(8,128)(2,1)} %bitcast.3), calls=%async_computation.5 | async-start | bytes 3276800 | tf_op jit(solution)/shard_map/all_to_all | solution.py:528
  108.5 1.0 copy-done.21
  109.6 0.2 shard_map.144
  109.8 1.4 collective-permute-start.8
  111.2 2.4 %collective-permute-start.9 = (bf16[40,1280]{1,0:T(8,128)(2,1)S(1)}, bf16[40,1280]{1,0:T(8,128)(2,1)S(1)}, u32[]{:S(2)}, u32[]{:S(2)}) collective-permute-start(bf16[40,1280]{1,0:T(8,128)(2,1)S(1)} %get-tuple-element.100), channel_id=1, source_target_pairs={{0,128},{8,136},{128,0},{136,8},{1,129},{9,137},{129,1},{137,9},{2... | collective-permute-start | bytes 307208 | tf_op jit(solution)/shard_map/ppermute | solution.py:489
  113.6 1.2 collective-permute-start.10
  114.8 1.7 %shard_map.145 = (f32[64,640]{1,0:T(8,128)S(1)}, bf16[64,640]{1,0:T(8,128)(2,1)S(1)}, bf16[64,1280]{1,0:T(8,128)(2,1)S(1)}, f32[16,128]{1,0:T(8,128)S(1)}) custom-call(s32[3]{0:T(128)S(1)} %pad_add_fusion.place, bf16[128,1920]{1,0:T(8,128)(2,1)S(1)} %copy-done.23, f32[128,640]{1,0:T(8,128)S(1)} %copy-done.25, ...), custom_call_target="tpu_custom_call" | custom-call | flops 3000000000 | bytes 9000000 | tf_op jit(solution)/shard_map/pallas_call | solution.py:429
  116.6 2.8 %collective-permute-start.11 = (f32[16,128]{1,0:T(8,128)S(1)}, f32[16,128]{1,0:T(8,128)S(1)}, u32[]{:S(2)}, u32[]{:S(2)}) collective-permute-start(f32[16,128]{1,0:T(8,128)S(1)} %get-tuple-element.105), channel_id=1, source_target_pairs={{0,2},{1,3},{2,0},{3,1},{4,6},{5,7},{6,4},{7,5},{8,10},{9,11},{10,... | collective-permute-start | bytes 24584 | tf_op jit(solution)/shard_map/ppermute | solution.py:493
  119.3 2.2 %collective-permute-done.11 = f32[16,128]{1,0:T(8,128)S(1)} collective-permute-done((f32[16,128]{1,0:T(8,128)S(1)}, f32[16,128]{1,0:T(8,128)S(1)}, u32[]{:S(2)}, u32[]{:S(2)}) %collective-permute-start.11) | collective-permute-done | bytes 8224 | tf_op jit(solution)/shard_map/ppermute | solution.py:493
  121.5 0.6 collective-permute-start.12
  122.1 3.4 %collective-permute-done.12 = f32[16,128]{1,0:T(8,128)S(1)} collective-permute-done((f32[16,128]{1,0:T(8,128)S(1)}, f32[16,128]{1,0:T(8,128)S(1)}, u32[]{:S(2)}, u32[]{:S(2)}) %collective-permute-start.12) | collective-permute-done | bytes 8224 | tf_op jit(solution)/shard_map/ppermute | solution.py:493
  125.6 5.0 %collective-permute-done.8.refs_1_ = bf16[40,1280]{1,0:T(8,128)(2,1)S(1)} collective-permute-done((bf16[40,1280]{1,0:T(8,128)(2,1)S(1)}, bf16[40,1280]{1,0:T(8,128)(2,1)S(1)}, u32[]{:S(2)}, u32[]{:S(2)}) %collective-permute-start.8) | collective-permute-done | bytes 102432 | tf_op jit(solution)/shard_map/ppermute | solution.py:489
  130.5 3.1 %collective-permute-done.9.refs_2_ = bf16[40,1280]{1,0:T(8,128)(2,1)S(1)} collective-permute-done((bf16[40,1280]{1,0:T(8,128)(2,1)S(1)}, bf16[40,1280]{1,0:T(8,128)(2,1)S(1)}, u32[]{:S(2)}, u32[]{:S(2)}) %collective-permute-start.9) | collective-permute-done | bytes 102432 | tf_op jit(solution)/shard_map/ppermute | solution.py:489
  133.6 0.0 collective-permute-done.10.refs_3_
  133.6 0.0 all-to-all-done.5
  133.7 1.3 shard_map.146
  135.0 6.5 %all-to-all-start.6 = ((bf16[8,4,3200]{2,1,0:T(4,128)(2,1)}), bf16[8,4,3200]{2,1,0:T(4,128)(2,1)S(1)}, u32[]{:S(2)}, u32[]{:S(2)}) async-start(bf16[8,4,3200]{2,1,0:T(4,128)(2,1)} %shard_map.146), calls=%async_computation.6 | async-start | bytes 409600 | tf_op jit(solution)/shard_map/all_to_all | solution.py:534
  141.4 1.5 collective-permute-start.14
  142.9 1.5 collective-permute-start.13
  144.4 2.8 %collective-permute-done.13 = f32[16,128]{1,0:T(8,128)S(1)} collective-permute-done((f32[16,128]{1,0:T(8,128)S(1)}, f32[16,128]{1,0:T(8,128)S(1)}, u32[]{:S(2)}, u32[]{:S(2)}) %collective-permute-start.13) | collective-permute-done | bytes 8224 | tf_op jit(solution)/shard_map/ppermute | solution.py:485
  147.2 0.0 collective-permute-done.14.recv_ref
  147.2 3.0 %all-to-all-done.6.parts_ref = bf16[8,4,3200]{2,1,0:T(4,128)(2,1)S(1)} async-done(((bf16[8,4,3200]{2,1,0:T(4,128)(2,1)}), bf16[8,4,3200]{2,1,0:T(4,128)(2,1)S(1)}, u32[]{:S(2)}, u32[]{:S(2)}) %all-to-all-start.6) | async-done | bytes 204832 | tf_op jit(solution)/shard_map/all_to_all | solution.py:534
  150.2 4.3 %collective-permute-start.17 = (bf16[4,3200]{1,0:T(4,128)(2,1)S(1)}, bf16[4,3200]{1,0:T(4,128)(2,1)S(1)}, u32[]{:S(2)}, u32[]{:S(2)}) collective-permute-start(bf16[4,3200]{1,0:T(4,128)(2,1)S(1)} %shard_map.148.own_ref), channel_id=1, source_target_pairs={{0,132},{4,128},{128,4},{132,0},{1,133},{5,129},{129,5},{133,1},{2... | collective-permute-start | bytes 76808 | tf_op jit(solution)/shard_map/ppermute | solution.py:545
  154.6 1.8 %collective-permute-start.16 = (bf16[4,3200]{1,0:T(4,128)(2,1)S(1)}, bf16[4,3200]{1,0:T(4,128)(2,1)S(1)}, u32[]{:S(2)}, u32[]{:S(2)}) collective-permute-start(bf16[4,3200]{1,0:T(4,128)(2,1)S(1)} %shard_map.148.own_ref), channel_id=1, source_target_pairs={{0,128},{128,0},{1,129},{129,1},{2,130},{130,2},{3,131},{131,3},{4... | collective-permute-start | bytes 76808 | tf_op jit(solution)/shard_map/ppermute | solution.py:485
  156.4 1.6 %shard_map.147 = (bf16[4,32,640]{2,1,0:T(8,128)(2,1)}, bf16[4,32,640]{2,1,0:T(8,128)(2,1)}, f32[4,4,128]{2,1,0:T(4,128)}) custom-call(s32[3]{0:T(128)S(1)} %pad_add_fusion.place, f32[16,128]{1,0:T(8,128)S(1)} %add.19.g_ref, f32[16,128]{1,0:T(8,128)S(1)} %get-tuple-element.117.sumstwo_ref, f32[16,128]{1,0:T(8,128)S(1)} %get-tuple-element.104.own_ref, ...), custom_call_target="tpu_custom_call" | custom-call | flops 3000000000 | bytes 9000000 | tf_op jit(solution)/shard_map/pallas_call | solution.py:429
  158.0 0.8 collective-permute-done.16.view_ref
  158.8 0.0 collective-permute-done.15.core_ref
  158.8 1.2 shard_map.149
  (61 shorter events, 0.2 us)
Async XLA Ops:
  0.6 16.6 %collective-permute-start = (bf16[4,1,32,640]{3,2,1,0:T(8,128)(2,1)}, bf16[4,1,32,640]{3,2,1,0:T(8,128)(2,1)S(1)}, u32[]{:S(2)}, u32[]{:S(2)}) collective-permute-start(bf16[4,1,32,640]{3,2,1,0:T(8,128)(2,1)} %x_ref.7), channel_id=1, source_target_pairs={{0,128},{128,0},{1,129},{129,1},{2,130},{130,2},{3,131},{131,3},{4... | collective-permute-start | bytes 491528 | tf_op jit(solution)/shard_map/ppermute | solution.py:485
  4.4 0.9 copy-start.6
  5.3 12.0 %copy-start.1 = (bf16[640,1920]{1,0:T(8,128)(2,1)S(1)}, bf16[640,1920]{1,0:T(8,128)(2,1)}, u32[]{:S(2)}) copy-start(bf16[640,1920]{1,0:T(8,128)(2,1)} %wqkv_ref.5) | copy-start | bytes 7372804
  5.3 12.0 %copy-start.4 = (bf16[640,640]{1,0:T(8,128)(2,1)S(1)}, bf16[640,640]{1,0:T(8,128)(2,1)}, u32[]{:S(2)}) copy-start(bf16[640,640]{1,0:T(8,128)(2,1)} %wout_ref.5) | copy-start | bytes 2457604
  5.3 12.0 %copy-start.7 = (bf16[4,1,32,640]{3,2,1,0:T(8,128)(2,1)S(1)}, bf16[4,1,32,640]{3,2,1,0:T(8,128)(2,1)}, u32[]{:S(2)}) copy-start(bf16[4,1,32,640]{3,2,1,0:T(8,128)(2,1)} %x_ref.7) | copy-start | bytes 491524
  17.2 2.8 %copy-start.5 = (bf16[4,1,32,640]{3,2,1,0:T(8,128)(2,1)S(1)}, bf16[4,1,32,640]{3,2,1,0:T(8,128)(2,1)}, u32[]{:S(2)}) copy-start(bf16[4,1,32,640]{3,2,1,0:T(8,128)(2,1)} %og_ref.1) | copy-start | bytes 491524
  17.3 2.8 %copy-start.9 = (bf16[4,1,32,640]{3,2,1,0:T(8,128)(2,1)}, bf16[4,1,32,640]{3,2,1,0:T(8,128)(2,1)S(1)}, u32[]{:S(2)}) copy-start(bf16[4,1,32,640]{3,2,1,0:T(8,128)(2,1)S(1)} %collective-permute-done.other_ref) | copy-start | bytes 491524
  20.0 12.4 %copy-start.17 = (f32[128,640]{1,0:T(8,128)}, f32[128,640]{1,0:T(8,128)S(1)}, u32[]{:S(2)}) copy-start(f32[128,640]{1,0:T(8,128)S(1)} %get-tuple-element.68.stream_ref) | copy-start | bytes 983044
  20.0 12.4 %copy-start.28 = (bf16[128,1920]{1,0:T(8,128)(2,1)}, bf16[128,1920]{1,0:T(8,128)(2,1)S(1)}, u32[]{:S(2)}) copy-start(bf16[128,1920]{1,0:T(8,128)(2,1)S(1)} %get-tuple-element.89.packed_ref) | copy-start | bytes 1474564
  20.1 11.4 %collective-permute-start.1 = (bf16[4,1,32,640]{3,2,1,0:T(8,128)(2,1)S(1)}, bf16[4,1,32,640]{3,2,1,0:T(8,128)(2,1)S(1)}, u32[]{:S(2)}, u32[]{:S(2)}) collective-permute-start(bf16[4,1,32,640]{3,2,1,0:T(8,128)(2,1)S(1)} %copy-done.5), channel_id=1, source_target_pairs={{0,128},{128,0},{1,129},{129,1},{2,130},{130,2},{3,131},{131,3},{4... | collective-permute-start | bytes 491528 | tf_op jit(solution)/shard_map/ppermute | solution.py:485
  31.5 0.9 copy-start.11
  31.5 27.2 %copy-start = (bf16[640,1920]{1,0:T(8,128)(2,1)S(1)}, bf16[640,1920]{1,0:T(8,128)(2,1)}, u32[]{:S(2)}) copy-start(bf16[640,1920]{1,0:T(8,128)(2,1)} %wqkv_ref.4) | copy-start | bytes 7372804
  31.5 27.2 %copy-start.3 = (bf16[640,640]{1,0:T(8,128)(2,1)S(1)}, bf16[640,640]{1,0:T(8,128)(2,1)}, u32[]{:S(2)}) copy-start(bf16[640,640]{1,0:T(8,128)(2,1)} %wout_ref.4) | copy-start | bytes 2457604
  58.7 10.3 %copy-start.14 = (s32[16,1,640]{2,1,0:T(1,128)S(1)}, s32[16,1,640]{2,1,0:T(1,128)}, u32[]{:S(2)}) copy-start(s32[16,1,640]{2,1,0:T(1,128)} %constant.24.clone.table_ref) | copy-start | bytes 122884
  62.9 0.8 copy-start.26
  63.8 5.3 %collective-permute-start.2 = (bf16[128,2560]{1,0:T(8,128)(2,1)S(1)}, bf16[128,2560]{1,0:T(8,128)(2,1)S(1)}, u32[]{:S(2)}, u32[]{:S(2)}) collective-permute-start(bf16[128,2560]{1,0:T(8,128)(2,1)S(1)} %get-tuple-element.75), channel_id=1, source_target_pairs={{0,4},{4,0},{1,5},{5,1},{2,6},{6,2},{3,7},{7,3},{8,12},{12,8},{9,1... | collective-permute-start | bytes 1966088 | tf_op jit(solution)/shard_map/ppermute | solution.py:485
  65.1 16.3 %all-to-all-start.3 = ((bf16[32,4,1280]{2,1,0:T(4,128)(2,1)}), bf16[32,4,1280]{2,1,0:T(4,128)(2,1)S(1)}, u32[]{:S(2)}, u32[]{:S(2)}) async-start(bf16[32,4,1280]{2,1,0:T(4,128)(2,1)} %get-tuple-element.73), calls=%async_computation.3 | async-start | bytes 655360 | tf_op jit(solution)/shard_map/all_to_all | solution.py:482
  68.7 8.2 %collective-permute-start.3 = (bf16[128,1280]{1,0:T(8,128)(2,1)S(1)}, bf16[128,1280]{1,0:T(8,128)(2,1)S(1)}, u32[]{:S(2)}, u32[]{:S(2)}) collective-permute-start(bf16[128,1280]{1,0:T(8,128)(2,1)S(1)} %get-tuple-element.79.mine_ref), channel_id=1, source_target_pairs={{0,4},{4,0},{1,5},{5,1},{2,6},{6,2},{3,7},{7,3},{8,12},{12,8},{9,1... | collective-permute-start | bytes 983048 | tf_op jit(solution)/shard_map/ppermute | solution.py:485
  69.0 1.1 copy-start.27
  70.1 6.8 %copy-start.13 = (s32[640,1]{1,0:T(8,128)S(1)}, s32[640,1]{1,0:T(8,128)}, u32[]{:S(2)}) copy-start(s32[640,1]{1,0:T(8,128)} %constant.25.clone.column_ref) | copy-start | bytes 7684
  73.3 0.8 copy-start.20
  74.0 21.9 %collective-permute-start.4 = (bf16[160,1280]{1,0:T(8,128)(2,1)}, bf16[160,1280]{1,0:T(8,128)(2,1)S(1)}, u32[]{:S(2)}, u32[]{:S(2)}) collective-permute-start(bf16[160,1280]{1,0:T(8,128)(2,1)} %get-tuple-element.76), channel_id=1, source_target_pairs={{0,1},{1,2},{2,3},{3,0},{4,5},{5,6},{6,7},{7,4},{8,9},{9,10},{10,1... | collective-permute-start | bytes 1228808 | tf_op jit(solution)/shard_map/ppermute | solution.py:489
  74.3 21.7 %collective-permute-start.5 = (bf16[160,1280]{1,0:T(8,128)(2,1)}, bf16[160,1280]{1,0:T(8,128)(2,1)S(1)}, u32[]{:S(2)}, u32[]{:S(2)}) collective-permute-start(bf16[160,1280]{1,0:T(8,128)(2,1)} %get-tuple-element.77), channel_id=1, source_target_pairs={{0,2},{1,3},{2,0},{3,1},{4,6},{5,7},{6,4},{7,5},{8,10},{9,11},{10,... | collective-permute-start | bytes 1228808 | tf_op jit(solution)/shard_map/ppermute | solution.py:489
  76.1 19.9 %collective-permute-start.6 = (bf16[160,1280]{1,0:T(8,128)(2,1)}, bf16[160,1280]{1,0:T(8,128)(2,1)S(1)}, u32[]{:S(2)}, u32[]{:S(2)}) collective-permute-start(bf16[160,1280]{1,0:T(8,128)(2,1)} %get-tuple-element.78), channel_id=1, source_target_pairs={{0,3},{1,0},{2,1},{3,2},{4,7},{5,4},{6,5},{7,6},{8,11},{9,8},{10,9... | collective-permute-start | bytes 1228808 | tf_op jit(solution)/shard_map/ppermute | solution.py:489
  78.2 0.9 copy-start.15
  79.1 16.9 %copy-start.12 = (bf16[4,1,32,640]{3,2,1,0:T(8,128)(2,1)S(1)}, bf16[4,1,32,640]{3,2,1,0:T(8,128)(2,1)}, u32[]{:S(2)}) copy-start(bf16[4,1,32,640]{3,2,1,0:T(8,128)(2,1)} %copy-done.11) | copy-start | bytes 491524
  81.4 1.0 copy-start.18
  82.3 13.6 %copy-start.29 = (bf16[128,1920]{1,0:T(8,128)(2,1)S(1)}, bf16[128,1920]{1,0:T(8,128)(2,1)}, u32[]{:S(2)}) copy-start(bf16[128,1920]{1,0:T(8,128)(2,1)} %copy-done.28) | copy-start | bytes 1474564
  96.0 5.7 %copy-start.16 = (bf16[2,640,256]{2,1,0:T(8,128)(2,1)S(1)}, bf16[2,640,256]{2,1,0:T(8,128)(2,1)}, u32[]{:S(2)}) copy-start(bf16[2,640,256]{2,1,0:T(8,128)(2,1)} %copy-done.15) | copy-start | bytes 1966084
  98.3 0.7 copy-start.24
  99.0 4.5 %copy-start.22 = (bf16[128,1920]{1,0:T(8,128)(2,1)}, bf16[128,1920]{1,0:T(8,128)(2,1)S(1)}, u32[]{:S(2)}) copy-start(bf16[128,1920]{1,0:T(8,128)(2,1)S(1)} %get-tuple-element.102.pgrad_ref) | copy-start | bytes 1474564
  99.0 2.6 %collective-permute-start.7 = (bf16[128,1280]{1,0:T(8,128)(2,1)S(1)}, bf16[128,1280]{1,0:T(8,128)(2,1)S(1)}, u32[]{:S(2)}, u32[]{:S(2)}) collective-permute-start(bf16[128,1280]{1,0:T(8,128)(2,1)S(1)} %get-tuple-element.91), channel_id=1, source_target_pairs={{0,4},{4,0},{1,5},{5,1},{2,6},{6,2},{3,7},{7,3},{8,12},{12,8},{9,1... | collective-permute-start | bytes 983048 | tf_op jit(solution)/shard_map/ppermute | solution.py:485
  103.5 30.1 %all-to-all-start.5 = ((bf16[16,40,1280]{2,1,0:T(8,128)(2,1)}), bf16[16,40,1280]{2,1,0:T(8,128)(2,1)S(1)}, u32[]{:S(2)}, u32[]{:S(2)}) async-start(bf16[16,40,1280]{2,1,0:T(8,128)(2,1)} %bitcast.3), calls=%async_computation.5 | async-start | bytes 3276800 | tf_op jit(solution)/shard_map/all_to_all | solution.py:528
  108.5 1.0 copy-start.21
  109.5 5.3 %copy-start.2 = (bf16[640,1920]{1,0:T(8,128)(2,1)S(1)}, bf16[640,1920]{1,0:T(8,128)(2,1)}, u32[]{:S(2)}) copy-start(bf16[640,1920]{1,0:T(8,128)(2,1)} %wqkv_ref.5) | copy-start | bytes 7372804
  109.5 5.3 %copy-start.8 = (bf16[4,1,32,640]{3,2,1,0:T(8,128)(2,1)S(1)}, bf16[4,1,32,640]{3,2,1,0:T(8,128)(2,1)}, u32[]{:S(2)}) copy-start(bf16[4,1,32,640]{3,2,1,0:T(8,128)(2,1)} %x_ref.7) | copy-start | bytes 491524
  109.5 5.3 %copy-start.10 = (bf16[4,1,32,640]{3,2,1,0:T(8,128)(2,1)S(1)}, bf16[4,1,32,640]{3,2,1,0:T(8,128)(2,1)}, u32[]{:S(2)}) copy-start(bf16[4,1,32,640]{3,2,1,0:T(8,128)(2,1)} %copy-done.9) | copy-start | bytes 491524
  109.5 5.3 %copy-start.19 = (f32[128,640]{1,0:T(8,128)S(1)}, f32[128,640]{1,0:T(8,128)}, u32[]{:S(2)}) copy-start(f32[128,640]{1,0:T(8,128)} %copy-done.17) | copy-start | bytes 983044
  109.5 5.3 %copy-start.23 = (bf16[128,1920]{1,0:T(8,128)(2,1)S(1)}, bf16[128,1920]{1,0:T(8,128)(2,1)}, u32[]{:S(2)}) copy-start(bf16[128,1920]{1,0:T(8,128)(2,1)} %copy-done.22) | copy-start | bytes 1474564
  109.6 5.3 %copy-start.25 = (f32[128,640]{1,0:T(8,128)S(1)}, f32[128,640]{1,0:T(8,128)}, u32[]{:S(2)}) copy-start(f32[128,640]{1,0:T(8,128)} %copy-done.24) | copy-start | bytes 983044
  109.8 20.7 %collective-permute-start.8 = (bf16[40,1280]{1,0:T(8,128)(2,1)S(1)}, bf16[40,1280]{1,0:T(8,128)(2,1)S(1)}, u32[]{:S(2)}, u32[]{:S(2)}) collective-permute-start(bf16[40,1280]{1,0:T(8,128)(2,1)S(1)} %get-tuple-element.99), channel_id=1, source_target_pairs={{0,8},{8,128},{128,136},{136,0},{1,9},{9,129},{129,137},{137,1},{2... | collective-permute-start | bytes 307208 | tf_op jit(solution)/shard_map/ppermute | solution.py:489
  111.2 22.4 %collective-permute-start.9 = (bf16[40,1280]{1,0:T(8,128)(2,1)S(1)}, bf16[40,1280]{1,0:T(8,128)(2,1)S(1)}, u32[]{:S(2)}, u32[]{:S(2)}) collective-permute-start(bf16[40,1280]{1,0:T(8,128)(2,1)S(1)} %get-tuple-element.100), channel_id=1, source_target_pairs={{0,128},{8,136},{128,0},{136,8},{1,129},{9,137},{129,1},{137,9},{2... | collective-permute-start | bytes 307208 | tf_op jit(solution)/shard_map/ppermute | solution.py:489
  113.6 20.0 %collective-permute-start.10 = (bf16[40,1280]{1,0:T(8,128)(2,1)S(1)}, bf16[40,1280]{1,0:T(8,128)(2,1)S(1)}, u32[]{:S(2)}, u32[]{:S(2)}) collective-permute-start(bf16[40,1280]{1,0:T(8,128)(2,1)S(1)} %get-tuple-element.101), channel_id=1, source_target_pairs={{0,136},{8,0},{128,8},{136,128},{1,137},{9,1},{129,9},{137,129},{2... | collective-permute-start | bytes 307208 | tf_op jit(solution)/shard_map/ppermute | solution.py:489
  116.6 4.9 %collective-permute-start.11 = (f32[16,128]{1,0:T(8,128)S(1)}, f32[16,128]{1,0:T(8,128)S(1)}, u32[]{:S(2)}, u32[]{:S(2)}) collective-permute-start(f32[16,128]{1,0:T(8,128)S(1)} %get-tuple-element.105), channel_id=1, source_target_pairs={{0,2},{1,3},{2,0},{3,1},{4,6},{5,7},{6,4},{7,5},{8,10},{9,11},{10,... | collective-permute-start | bytes 24584 | tf_op jit(solution)/shard_map/ppermute | solution.py:493
  121.5 4.0 %collective-permute-start.12 = (f32[16,128]{1,0:T(8,128)S(1)}, f32[16,128]{1,0:T(8,128)S(1)}, u32[]{:S(2)}, u32[]{:S(2)}) collective-permute-start(f32[16,128]{1,0:T(8,128)S(1)} %add.17), channel_id=1, source_target_pairs={{0,1},{1,0},{2,3},{3,2},{4,5},{5,4},{6,7},{7,6},{8,9},{9,8},{10,11... | collective-permute-start | bytes 24584 | tf_op jit(solution)/shard_map/ppermute | solution.py:493
  135.0 15.2 %all-to-all-start.6 = ((bf16[8,4,3200]{2,1,0:T(4,128)(2,1)}), bf16[8,4,3200]{2,1,0:T(4,128)(2,1)S(1)}, u32[]{:S(2)}, u32[]{:S(2)}) async-start(bf16[8,4,3200]{2,1,0:T(4,128)(2,1)} %shard_map.146), calls=%async_computation.6 | async-start | bytes 409600 | tf_op jit(solution)/shard_map/all_to_all | solution.py:534
  141.4 5.8 %collective-permute-start.14 = (bf16[64,1280]{1,0:T(8,128)(2,1)S(1)}, bf16[64,1280]{1,0:T(8,128)(2,1)S(1)}, u32[]{:S(2)}, u32[]{:S(2)}) collective-permute-start(bf16[64,1280]{1,0:T(8,128)(2,1)S(1)} %get-tuple-element.115), channel_id=1, source_target_pairs={{0,128},{128,0},{1,129},{129,1},{2,130},{130,2},{3,131},{131,3},{4... | collective-permute-start | bytes 491528 | tf_op jit(solution)/shard_map/ppermute | solution.py:485
  142.9 4.3 %collective-permute-start.13 = (f32[16,128]{1,0:T(8,128)S(1)}, f32[16,128]{1,0:T(8,128)S(1)}, u32[]{:S(2)}, u32[]{:S(2)}) collective-permute-start(f32[16,128]{1,0:T(8,128)S(1)} %add.18), channel_id=1, source_target_pairs={{0,128},{128,0},{1,129},{129,1},{2,130},{130,2},{3,131},{131,3},{4... | collective-permute-start | bytes 24584 | tf_op jit(solution)/shard_map/ppermute | solution.py:485
  150.2 7.8 %collective-permute-start.17 = (bf16[4,3200]{1,0:T(4,128)(2,1)S(1)}, bf16[4,3200]{1,0:T(4,128)(2,1)S(1)}, u32[]{:S(2)}, u32[]{:S(2)}) collective-permute-start(bf16[4,3200]{1,0:T(4,128)(2,1)S(1)} %shard_map.148.own_ref), channel_id=1, source_target_pairs={{0,132},{4,128},{128,4},{132,0},{1,133},{5,129},{129,5},{133,1},{2... | collective-permute-start | bytes 76808 | tf_op jit(solution)/shard_map/ppermute | solution.py:545
  154.6 4.2 %collective-permute-start.16 = (bf16[4,3200]{1,0:T(4,128)(2,1)S(1)}, bf16[4,3200]{1,0:T(4,128)(2,1)S(1)}, u32[]{:S(2)}, u32[]{:S(2)}) collective-permute-start(bf16[4,3200]{1,0:T(4,128)(2,1)S(1)} %shard_map.148.own_ref), channel_id=1, source_target_pairs={{0,128},{128,0},{1,129},{129,1},{2,130},{130,2},{3,131},{131,3},{4... | collective-permute-start | bytes 76808 | tf_op jit(solution)/shard_map/ppermute | solution.py:485
  156.4 2.4 %collective-permute-start.15 = (bf16[4,3200]{1,0:T(4,128)(2,1)S(1)}, bf16[4,3200]{1,0:T(4,128)(2,1)S(1)}, u32[]{:S(2)}, u32[]{:S(2)}) collective-permute-start(bf16[4,3200]{1,0:T(4,128)(2,1)S(1)} %shard_map.148.own_ref), channel_id=1, source_target_pairs={{0,4},{4,0},{1,5},{5,1},{2,6},{6,2},{3,7},{7,3},{8,12},{12,8},{9,1... | collective-permute-start | bytes 76808 | tf_op jit(solution)/shard_map/ppermute | solution.py:485
